TPU v7x, 32 devices: a whole 2x2x4 slice. The times are simulated.
32 devices in a mesh: dp: 2 (over core), fsdp: 16 (over z, y, x).
Axes of the slice: x: 2, y: 2, z: 4, core: 2. Of those that a mesh axis runs over, the one named last changes fastest.
Arguments:
- tokens: bfloat16 [32768, 1024], P(('dp', 'fsdp')), may hold values from -18 to 18
- condition: bfloat16 [128, 768], P(('dp', 'fsdp')), may hold values from -6 to 6
- shapes: int32 [128, 2], P(('dp', 'fsdp')), may hold values from 8 to 32, as said below
- cotangent: bfloat16 [32768, 1024], P(('dp', 'fsdp')), may hold values from -6 to 6
- ada_weight: float32 [2, 768, 1024], P(None, 'fsdp'), may hold values from -0.109375 to 0.109375
- ada_first: float32 [2, 768, 1024], P(None, 'fsdp'), may hold values from -0.00018310547 to 0.00018310547
- ada_second: float32 [2, 768, 1024], P(None, 'fsdp'), may hold values from 3.2885286e-09 to 1.3154114e-08
- qkv_weight: float32 [1024, 3072], P('fsdp'), may hold values from -0.1875 to 0.1875
- qkv_first: float32 [1024, 3072], P('fsdp'), may hold values from -0.00018310547 to 0.00018310547
- qkv_second: float32 [1024, 3072], P('fsdp'), may hold values from 3.2885286e-09 to 1.3154114e-08
- out_weight: float32 [1024, 1024], P('fsdp'), may hold values from -1.5 to 1.5
- out_first: float32 [1024, 1024], P('fsdp'), may hold values from -4.5776367e-05 to 4.5776367e-05
- out_second: float32 [1024, 1024], P('fsdp'), may hold values from 1.9731172e-10 to 7.892469e-10
- up_weight: float32 [1024, 6144], P('fsdp'), may hold values from -0.1875 to 0.1875
- up_first: float32 [1024, 6144], P('fsdp'), may hold values from -6.1035156e-05 to 6.1035156e-05
- up_second: float32 [1024, 6144], P('fsdp'), may hold values from 3.2885286e-10 to 1.3154114e-09
- down_weight: float32 [3072, 1024], P('fsdp'), may hold values from -0.109375 to 0.109375
- down_first: float32 [3072, 1024], P('fsdp'), may hold values from -0.00018310547 to 0.00018310547
- down_second: float32 [3072, 1024], P('fsdp'), may hold values from 3.2885286e-09 to 1.3154114e-08
- head_scale: float32 [16], replicated, may hold values from 5 to 20
- scale_first: float32 [16], replicated, may hold values from -0.00018310547 to 0.00018310547
- scale_second: float32 [16], replicated, may hold values from 3.2885286e-09 to 1.3154114e-08
Outputs:
- block_output: bfloat16 [32768, 1024], P(('dp', 'fsdp'))
- input_grad: bfloat16 [32768, 1024], P(('dp', 'fsdp'))
- grad_norm: float32 [], replicated
- new_ada: float32 [2, 768, 1024], P(None, 'fsdp')
- new_ada_first: float32 [2, 768, 1024], P(None, 'fsdp')
- new_ada_second: float32 [2, 768, 1024], P(None, 'fsdp')
- new_qkv: float32 [1024, 3072], P('fsdp')
- new_qkv_first: float32 [1024, 3072], P('fsdp')
- new_qkv_second: float32 [1024, 3072], P('fsdp')
- new_out: float32 [1024, 1024], P('fsdp')
- new_out_first: float32 [1024, 1024], P('fsdp')
- new_out_second: float32 [1024, 1024], P('fsdp')
- new_up: float32 [1024, 6144], P('fsdp')
- new_up_first: float32 [1024, 6144], P('fsdp')
- new_up_second: float32 [1024, 6144], P('fsdp')
- new_down: float32 [3072, 1024], P('fsdp')
- new_down_first: float32 [3072, 1024], P('fsdp')
- new_down_second: float32 [3072, 1024], P('fsdp')
- new_scale: float32 [16], replicated
- new_scale_first: float32 [16], replicated
- new_scale_second: float32 [16], replicated
Inputs may be any that keep to these rules, and one draw needn't show every extreme that they name: `shapes`: each row is an image's bucket (height, width) with height = 256 // width, so that its valid tokens height * width never exceed 256; the first image is a full 16 x 16 bucket.
All inputs are finite; a program needn't handle non-finite values.
Results may differ from a plain program's by a relative error of at most 0.02.
Values may be sent and summed in bfloat16 or wider, within the bound.
No kernel may reach another device: no remote copies, remote signals or barrier semaphores. Data moves between devices by JAX's collectives and lax.ppermute only.
A program may use at most 256 MiB of HBM per device.

v0:
```python
import math

import jax
import jax.numpy as jnp
from jax import lax
from jax.sharding import PartitionSpec as P

FF = 3072
STEP = 10


NORM_EPS = 1e-06
COSINE_EPS = 1e-06
MASK_FILL = -1e30
ROPE_BASE = 100.0
CLIP = 1.0
RATE = 0.02
OUTPUT_RATE = 0.2
SCALE_RATE = 8.0
BETA_ONE = 0.9
BETA_TWO = 0.95
ADAM_EPS = 1e-08
DECAY = 0.01
PRECISE = lax.Precision.HIGHEST


def rope_tables(shapes, seq_len, head_dim):
    heights = shapes[:, 0:1]
    widths = shapes[:, 1:2]
    slot_index = jnp.arange(seq_len, dtype=jnp.int32)[None, :]
    row_index = slot_index // widths
    col_index = slot_index % widths
    valid_keys = slot_index < heights * widths
    freq_count = head_dim // 8
    frequency = ROPE_BASE ** (-jnp.arange(freq_count, dtype=jnp.float32) / freq_count)
    angles = jnp.concatenate(
        [
            row_index.astype(jnp.float32)[..., None] * frequency,
            col_index.astype(jnp.float32)[..., None] * frequency,
        ],
        axis=-1,
    )
    return (jnp.cos(angles), jnp.sin(angles), valid_keys)


def ada_norm(values, scales):
    inverse = lax.rsqrt(jnp.mean(values * values, axis=-1, keepdims=True) + NORM_EPS)
    return values * inverse * scales[:, None, :]


def turn(values, cosine, sine_table):
    quarter = values.shape[-1] // 4
    first_half = values[..., :quarter]
    second = values[..., quarter : 2 * quarter]
    cos_wide = cosine[:, :, None, :]
    sin_wide = sine_table[:, :, None, :]
    return jnp.concatenate(
        [
            first_half * cos_wide - second * sin_wide,
            first_half * sin_wide + second * cos_wide,
            values[..., 2 * quarter :],
        ],
        axis=-1,
    )


def prepare(queries, keys_in, head_scale, cosine, sine_table):
    root_scale = jnp.sqrt(head_scale)[None, None, :, None]
    queries = (
        queries
        * root_scale
        * lax.rsqrt(jnp.sum(queries * queries, axis=-1, keepdims=True) + COSINE_EPS)
    )
    keys_in = (
        keys_in
        * root_scale
        * lax.rsqrt(jnp.sum(keys_in * keys_in, axis=-1, keepdims=True) + COSINE_EPS)
    )
    return (turn(queries, cosine, sine_table), turn(keys_in, cosine, sine_table))


def rounded(values):
    return lax.optimization_barrier(values.astype(jnp.bfloat16)).astype(jnp.float32)


def masked_scores(queries, keys_in, valid_keys):
    scores = jnp.einsum("bqhd,bkhd->bhqk", queries, keys_in, preferred_element_type=jnp.float32)
    return jnp.where(valid_keys[:, None, None, :], scores, MASK_FILL)


def attend_block(block_parts):
    queries, keys_in, values, valid_keys = block_parts
    scores = masked_scores(queries, keys_in, valid_keys)
    top_score = jnp.max(scores, axis=-1, keepdims=True)
    exponent = jnp.exp(scores - top_score)
    totals = jnp.sum(exponent, axis=-1, keepdims=True)
    probabilities = (exponent / totals).astype(jnp.bfloat16)
    mixed_out = jnp.einsum(
        "bhqk,bkhd->bqhd", probabilities, values, preferred_element_type=jnp.float32
    )
    return (mixed_out.astype(jnp.bfloat16), top_score + jnp.log(totals))


def attend_back(block_parts):
    queries, keys_in, values, valid_keys, log_totals, grad_mixed = block_parts
    scores = masked_scores(queries, keys_in, valid_keys)
    probabilities = jnp.exp(scores - log_totals)
    grad_probs = jnp.einsum(
        "bqhd,bkhd->bhqk", grad_mixed, values, preferred_element_type=jnp.float32
    )
    inner_sum = jnp.sum(probabilities * grad_probs, axis=-1, keepdims=True)
    grad_scores = (probabilities * (grad_probs - inner_sum)).astype(jnp.bfloat16)
    probs_low = probabilities.astype(jnp.bfloat16)
    grad_values = jnp.einsum(
        "bhqk,bqhd->bkhd", probs_low, grad_mixed, preferred_element_type=jnp.float32
    )
    grad_queries = jnp.einsum(
        "bhqk,bkhd->bqhd", grad_scores, keys_in, preferred_element_type=jnp.float32
    )
    grad_keys = jnp.einsum(
        "bhqk,bqhd->bkhd", grad_scores, queries, preferred_element_type=jnp.float32
    )
    return (grad_queries, grad_keys, grad_values)


def adamw(weight, first_moment, second_moment, gradient, factor, rate, decay):
    clipped = gradient * factor
    new_first = BETA_ONE * first_moment + (1.0 - BETA_ONE) * clipped
    new_second = BETA_TWO * second_moment + (1.0 - BETA_TWO) * clipped * clipped
    denominator = jnp.sqrt(new_second / (1.0 - BETA_TWO**STEP)) + ADAM_EPS
    new_weight = (
        weight * (1.0 - rate * decay) - rate * (new_first / (1.0 - BETA_ONE**STEP)) / denominator
    )
    return (new_weight, new_first, new_second)


def local(
    tokens,
    condition,
    shapes,
    cotangent,
    ada_weight,
    ada_first,
    ada_second,
    qkv_weight,
    qkv_first,
    qkv_second,
    out_weight,
    out_first,
    out_second,
    up_weight,
    up_first,
    up_second,
    down_weight,
    down_first,
    down_second,
    head_scale,
    scale_first,
    scale_second,
):
    images = shapes.shape[0]
    model_width = tokens.shape[1]
    seq_len = tokens.shape[0] // images
    head_count = head_scale.shape[0]
    head_dim = model_width // head_count
    block_size = math.gcd(images, max(1, 512 // seq_len))
    block_count = images // block_size

    def to_blocks(array):
        return array.reshape((block_count, block_size) + array.shape[1:])

    def from_blocks(array):
        return array.reshape((images,) + array.shape[2:])

    cosine, sine_table, valid_keys = rope_tables(shapes, seq_len, head_dim)
    low_shards = (
        ada_weight.astype(jnp.bfloat16),
        qkv_weight.astype(jnp.bfloat16),
        out_weight.astype(jnp.bfloat16),
        up_weight.astype(jnp.bfloat16),
        down_weight.astype(jnp.bfloat16),
    )
    ada_full, qkv_full, out_full, up_full, down_full = (
        lax.all_gather(low_shards[0], "fsdp", axis=1, tiled=True),
        lax.all_gather(low_shards[1], "fsdp", axis=0, tiled=True),
        lax.all_gather(low_shards[2], "fsdp", axis=0, tiled=True),
        lax.all_gather(low_shards[3], "fsdp", axis=0, tiled=True),
        lax.all_gather(low_shards[4], "fsdp", axis=0, tiled=True),
    )
    inputs = tokens.astype(jnp.float32).reshape(images, seq_len, model_width)
    scale_one = 1.0 + jnp.dot(condition, ada_full[0], preferred_element_type=jnp.float32)
    normed_one, norm_one_back = jax.vjp(ada_norm, inputs, scale_one)
    act_one = normed_one.astype(jnp.bfloat16)
    projected = jnp.einsum("bsd,de->bse", act_one, qkv_full, preferred_element_type=jnp.float32)
    projected = projected.reshape(images, seq_len, 3, head_count, head_dim)
    turned, prepare_back = jax.vjp(
        lambda q_in, k_in, scale_in: prepare(q_in, k_in, scale_in, cosine, sine_table),
        projected[:, :, 0],
        projected[:, :, 1],
        head_scale,
    )
    q_low = turned[0].astype(jnp.bfloat16)
    k_low = turned[1].astype(jnp.bfloat16)
    v_low = projected[:, :, 2].astype(jnp.bfloat16)
    mixed_blocks, log_totals = lax.map(
        attend_block, (to_blocks(q_low), to_blocks(k_low), to_blocks(v_low), to_blocks(valid_keys))
    )
    mixed_flat = from_blocks(mixed_blocks).reshape(images, seq_len, model_width)
    middle = inputs + jnp.einsum(
        "bse,ed->bsd", mixed_flat, out_full, preferred_element_type=jnp.float32
    )
    scale_two = 1.0 + jnp.dot(condition, ada_full[1], preferred_element_type=jnp.float32)
    normed_two, norm_two_back = jax.vjp(ada_norm, middle, scale_two)
    act_two = normed_two.astype(jnp.bfloat16)
    gate_up = jnp.einsum("bsd,de->bse", act_two, up_full, preferred_element_type=jnp.float32)
    hidden_act, gating_back = jax.vjp(
        lambda gate_part, up_part: jax.nn.gelu(gate_part, approximate=False) * up_part,
        gate_up[..., :FF],
        gate_up[..., FF:],
    )
    hidden_low = hidden_act.astype(jnp.bfloat16)
    result = middle + jnp.einsum(
        "bsf,fd->bsd", hidden_low, down_full, preferred_element_type=jnp.float32
    )
    block_output = result.reshape(images * seq_len, model_width).astype(jnp.bfloat16)
    ada_full, qkv_full, out_full, up_full, down_full = (
        lax.all_gather(low_shards[0], "fsdp", axis=1, tiled=True),
        lax.all_gather(low_shards[1], "fsdp", axis=0, tiled=True),
        lax.all_gather(low_shards[2], "fsdp", axis=0, tiled=True),
        lax.all_gather(low_shards[3], "fsdp", axis=0, tiled=True),
        lax.all_gather(low_shards[4], "fsdp", axis=0, tiled=True),
    )
    grad_out = cotangent.reshape(images, seq_len, model_width)
    grad_down = jnp.einsum("bsf,bsd->fd", hidden_low, grad_out, preferred_element_type=jnp.float32)
    grad_hidden = rounded(
        jnp.einsum("bsd,fd->bsf", grad_out, down_full, preferred_element_type=jnp.float32)
    )
    grad_gate, grad_upper = gating_back(grad_hidden)
    grad_gate_up = jnp.concatenate([grad_gate, grad_upper], axis=-1).astype(jnp.bfloat16)
    grad_up = jnp.einsum("bsd,bse->de", act_two, grad_gate_up, preferred_element_type=jnp.float32)
    grad_act_two = jnp.einsum(
        "bse,de->bsd", grad_gate_up, up_full, preferred_element_type=jnp.float32
    )
    grad_middle_part, grad_scale_two = norm_two_back(grad_act_two)
    grad_middle = grad_out.astype(jnp.float32) + grad_middle_part
    grad_branch = grad_middle.astype(jnp.bfloat16)
    grad_outw = jnp.einsum(
        "bse,bsd->ed", mixed_flat, grad_branch, preferred_element_type=jnp.float32
    )
    grad_mixed = jnp.einsum(
        "bsd,ed->bse", grad_branch, out_full, preferred_element_type=jnp.float32
    )
    grad_mixed = grad_mixed.astype(jnp.bfloat16).reshape(images, seq_len, head_count, head_dim)
    grad_q, grad_k, grad_v = lax.map(
        attend_back,
        (
            to_blocks(q_low),
            to_blocks(k_low),
            to_blocks(v_low),
            to_blocks(valid_keys),
            log_totals,
            to_blocks(grad_mixed),
        ),
    )
    grad_pre_q, grad_pre_k, grad_heads = prepare_back((from_blocks(grad_q), from_blocks(grad_k)))
    grad_projected = jnp.stack([grad_pre_q, grad_pre_k, from_blocks(grad_v)], axis=2)
    grad_projected = grad_projected.reshape(images, seq_len, 3 * model_width).astype(jnp.bfloat16)
    grad_qkv = jnp.einsum(
        "bsd,bse->de", act_one, grad_projected, preferred_element_type=jnp.float32
    )
    grad_act_one = jnp.einsum(
        "bse,de->bsd", grad_projected, qkv_full, preferred_element_type=jnp.float32
    )
    grad_input_part, grad_scale_one = norm_one_back(grad_act_one)
    input_grad = (
        (grad_middle + grad_input_part).reshape(images * seq_len, model_width).astype(jnp.bfloat16)
    )
    cond_wide = condition.astype(jnp.float32)
    grad_ada = jnp.stack(
        [
            jnp.dot(cond_wide.T, grad_scale_one, precision=PRECISE),
            jnp.dot(cond_wide.T, grad_scale_two, precision=PRECISE),
        ],
        axis=0,
    )
    owned = (
        lax.psum_scatter(grad_ada, "fsdp", scatter_dimension=1, tiled=True),
        lax.psum_scatter(grad_qkv, "fsdp", scatter_dimension=0, tiled=True),
        lax.psum_scatter(grad_outw, "fsdp", scatter_dimension=0, tiled=True),
        lax.psum_scatter(grad_up, "fsdp", scatter_dimension=0, tiled=True),
        lax.psum_scatter(grad_down, "fsdp", scatter_dimension=0, tiled=True),
    )
    owned = (
        lax.psum(owned[0].astype(jnp.bfloat16), "dp").astype(jnp.float32),
        lax.psum(owned[1].astype(jnp.bfloat16), "dp").astype(jnp.float32),
        lax.psum(owned[2].astype(jnp.bfloat16), "dp").astype(jnp.float32),
        lax.psum(owned[3].astype(jnp.bfloat16), "dp").astype(jnp.float32),
        lax.psum(owned[4].astype(jnp.bfloat16), "dp").astype(jnp.float32),
    )
    head_grad = lax.psum(grad_heads, ("dp", "fsdp"))
    local_squares = (
        jnp.sum(owned[0] * owned[0]) + jnp.sum(owned[1] * owned[1]) + jnp.sum(owned[2] * owned[2])
    )
    local_squares = local_squares + jnp.sum(owned[3] * owned[3]) + jnp.sum(owned[4] * owned[4])
    total = lax.psum(local_squares, "fsdp") + jnp.sum(head_grad * head_grad)
    grad_norm = jnp.sqrt(total)
    factor = jnp.minimum(1.0, CLIP / (grad_norm + 1e-06))
    ada_new = adamw(ada_weight, ada_first, ada_second, owned[0], factor, RATE, DECAY)
    qkv_new = adamw(qkv_weight, qkv_first, qkv_second, owned[1], factor, RATE, DECAY)
    out_new = adamw(out_weight, out_first, out_second, owned[2], factor, OUTPUT_RATE, DECAY)
    up_new = adamw(up_weight, up_first, up_second, owned[3], factor, RATE, DECAY)
    down_new = adamw(down_weight, down_first, down_second, owned[4], factor, RATE, DECAY)
    scale_new = adamw(head_scale, scale_first, scale_second, head_grad, factor, SCALE_RATE, 0.0)
    return (
        block_output,
        input_grad,
        grad_norm,
        ada_new[0],
        ada_new[1],
        ada_new[2],
        qkv_new[0],
        qkv_new[1],
        qkv_new[2],
        out_new[0],
        out_new[1],
        out_new[2],
        up_new[0],
        up_new[1],
        up_new[2],
        down_new[0],
        down_new[1],
        down_new[2],
        scale_new[0],
        scale_new[1],
        scale_new[2],
    )


def solution(mesh):
    placed = (
        P(("dp", "fsdp"), None),
        P(("dp", "fsdp"), None),
        P(("dp", "fsdp"), None),
        P(("dp", "fsdp"), None),
        P(None, "fsdp", None),
        P(None, "fsdp", None),
        P(None, "fsdp", None),
        P("fsdp", None),
        P("fsdp", None),
        P("fsdp", None),
        P("fsdp", None),
        P("fsdp", None),
        P("fsdp", None),
        P("fsdp", None),
        P("fsdp", None),
        P("fsdp", None),
        P("fsdp", None),
        P("fsdp", None),
        P("fsdp", None),
        P(),
        P(),
        P(),
    )
    return jax.shard_map(
        local,
        mesh=mesh,
        in_specs=placed,
        out_specs=(
            P(("dp", "fsdp"), None),
            P(("dp", "fsdp"), None),
            P(),
            P(None, "fsdp", None),
            P(None, "fsdp", None),
            P(None, "fsdp", None),
            P("fsdp", None),
            P("fsdp", None),
            P("fsdp", None),
            P("fsdp", None),
            P("fsdp", None),
            P("fsdp", None),
            P("fsdp", None),
            P("fsdp", None),
            P("fsdp", None),
            P("fsdp", None),
            P("fsdp", None),
            P("fsdp", None),
            P(),
            P(),
            P(),
        ),
        check_vma=False,
    )
```

profile of v0, /device:TPU:0, one launch (start us, length us, event | category | flops | bytes accessed | tf_op | source)
XLA Modules:
  0.0 1709.8 jit_solution(7849002056737552425)
XLA Ops:
  9.2 1.9 convert_element_type.145
  11.2 1.9 convert_element_type.153
  14.9 2.4 convert_element_type.151
  20.0 62.2 %all-gather.6.cloned.1.call-done = bf16[2,768,1024]{2,1,0:T(8,128)(2,1)} async-done(((bf16[2,48,1024]{2,1,0:T(8,128)(2,1)}), bf16[2,768,1024]{2,1,0:T(8,128)(2,1)}) %all-gather.6.cloned.1.call-update) | async-done | bytes 3145744 | tf_op jit(solution)/shard_map/all_gather | solution.py:184
  86.3 91.9 %all-gather.8.cloned.1.call-done = bf16[1024,3072]{1,0:T(8,128)(2,1)} async-done(((bf16[64,3072]{1,0:T(8,128)(2,1)}), bf16[1024,3072]{1,0:T(8,128)(2,1)}) %all-gather.8.cloned.1.call-update) | async-done | bytes 6291472 | tf_op jit(solution)/shard_map/all_gather | solution.py:185
  178.2 9.3 copy.105
  187.5 10.6 fusion.136
  203.5 3.0 multiply_multiply_fusion.5
  206.4 2.0 copy-done.8
  211.2 62.9 %all-gather.14.cloned.1.call-done = bf16[3072,1024]{1,0:T(8,128)(2,1)} async-done(((bf16[192,1024]{1,0:T(8,128)(2,1)}), bf16[3072,1024]{1,0:T(8,128)(2,1)}) %all-gather.14.cloned.1.call-update) | async-done | bytes 6291472 | tf_op jit(solution)/shard_map/all_gather | solution.py:188
  274.1 11.4 fusion.63
  288.6 15.4 while.26
  288.7 2.9 select_reduce_fusion.2
  293.3 3.0 fusion.172
  296.4 2.9 select_reduce_fusion.2
  300.9 3.0 fusion.172
  304.0 32.4 %all-gather.10.cloned.1.call-done = bf16[1024,1024]{1,0:T(8,128)(2,1)} async-done(((bf16[64,1024]{1,0:T(8,128)(2,1)}), bf16[1024,1024]{1,0:T(8,128)(2,1)}) %all-gather.10.cloned.1.call-update) | async-done | bytes 2097168 | tf_op jit(solution)/shard_map/all_gather | solution.py:186
  336.3 7.5 multiply_reduce_fusion.9
  343.9 146.3 %all-gather.12.cloned.1.call-done = bf16[1024,6144]{1,0:T(8,128)(2,1)} async-done(((bf16[64,6144]{1,0:T(8,128)(2,1)}), bf16[1024,6144]{1,0:T(8,128)(2,1)}) %all-gather.12.cloned.1.call-update) | async-done | bytes 12582928 | tf_op jit(solution)/shard_map/all_gather | solution.py:187
  490.2 21.9 %fusion.49 = f32[4,256,6144]{2,1,0:T(8,128)} fusion(bf16[1024,6144]{1,0:T(8,128)(2,1)} %all-gather.12.cloned.1.call-done, f32[4,256,1024]{2,1,0:T(8,128)} %get-tuple-element.295, f32[4,1024]{1,0:T(4,128)S(1)} %fusion.92, f32[4,256]{1,0:T(4,128)S(1)} %fusion.118), kind=kOutput, calls=%fused_computation.65 | convolution fusion | flops 12888047616 | bytes 41963520 | tf_op jit(solution)/shard_map/bsd,de->bse/dot_general | solution.py:215
  512.2 33.0 %add_convert_fusion = (bf16[4,256,3072]{2,1,0:T(8,128)(2,1)}, f32[4,256,3072]{2,1,0:T(8,128)}) fusion(bf16[4,256,3072]{2,1,0:T(8,128)(2,1)} %fusion.63, f32[4,256,6144]{2,1,0:T(8,128)} %fusion.49), kind=kLoop, calls=%fused_computation.67 | loop fusion | flops 232783872 | bytes 50331648 | tf_op jit(solution)/shard_map/convert
  545.1 21.2 %fusion.45 = (bf16[4,256,3072]{2,1,0:T(8,128)(2,1)}, bf16[4,256,3072]{2,1,0:T(8,128)(2,1)}) fusion(bf16[4,256,3072]{2,1,0:T(8,128)(2,1)} %fusion.63, f32[4,256,3072]{2,1,0:T(8,128)} %get-tuple-element.261, f32[4,256,6144]{2,1,0:T(8,128)} %fusion.49), kind=kLoop, calls=%fused_computation.59 | loop fusion | flops 22020096 | bytes 56623104 | tf_op jit(solution)/shard_map/convert.1
  566.3 22.0 %multiply_reduce_fusion.3 = (f32[4,1024]{1,0:T(4,128)}, f32[4,256]{1,0:T(4,128)S(1)}, f32[4,256,1024]{2,1,0:T(8,128)}) fusion(f32[4,256,1024]{2,1,0:T(8,128)} %get-tuple-element.295, f32[4,256]{1,0:T(4,128)S(1)} %fusion.118, f32[4,1024]{1,0:T(4,128)S(1)} %fusion.92, bf16[1024,6144]{1,0:T(8,128)(2,1)} %all-gather.12.cloned.1.call-done, ...), kind=kOutput, calls=%fused_computation.110 | convolution fusion | flops 12916354048 | bytes 33595392 | tf_op jit(solution)/shard_map/bse,de->bsd/dot_general | solution.py:241
  588.4 4.6 fusion.90
  594.4 5.9 convolution_bitcast_fusion.3
  600.3 5.9 fusion.81
  606.2 3.9 copy.108
  610.2 32.8 %while.27 = (s32[]{:T(128)}, f32[2,2,256,16,64]{2,4,3,1,0:T(8,128)}, f32[2,2,256,16,64]{2,4,3,1,0:T(8,128)}, bf16[2,2,256,16,64]{2,4,3,1,0:T(8,128)(2,1)}, bf16[...) while((s32[]{:T(128)}, ...), condition=%wide.region_11.12_spmd, body=%wide.region_9.11_spmd.sunk | while | flops 1367334912 | bytes 135504656 | solution.py:254
  610.6 2.7 fusion.181
  613.4 2.7 multiply_reduce_fusion.16
  616.1 2.4 multiply_convert_fusion.6
  618.5 2.7 bitcast_dynamic-update-slice_fusion.10
  622.1 2.0 copy-done.16
  624.1 2.7 bitcast_dynamic-update-slice_fusion.11
  626.8 2.7 fusion.181
  629.5 2.7 multiply_reduce_fusion.16
  632.3 2.4 multiply_convert_fusion.6
  634.7 2.7 bitcast_dynamic-update-slice_fusion.10
  638.3 2.0 copy-done.16
  640.3 2.7 bitcast_dynamic-update-slice_fusion.11
  648.1 6.5 multiply_reduce_fusion.2
  654.8 3.8 fusion.71
  658.5 2.3 maximum_convert_fusion
  662.0 2.6 copy-done.13
  664.6 9.1 convolution_bitcast_fusion.2
  675.3 12.5 convolution_bitcast_fusion.1
  688.6 23.9 %convolution_bitcast_fusion = f32[1024,6144]{1,0:T(8,128)} fusion(bf16[4,256,3072]{2,1,0:T(8,128)(2,1)} %get-tuple-element.266, bf16[4,256,3072]{2,1,0:T(8,128)(2,1)} %get-tuple-element.260, f32[4,256,1024]{2,1,0:T(8,128)} %get-tuple-element.295, f32[4,1024]{1,0:T(4,128)S(1)} %copy-done.55, f32[4,256]{1,0:T(4,128)S(1)} %copy-done.59), kind=kOutput, calls=%fused_computation.58 | convolution fusion | flops 12913213440 | bytes 41963520 | tf_op jit(solution)/shard_map/bsd,bse->de/dot_general | solution.py:240
  714.4 41.3 %psum.55 = f32[16]{0:T(128)S(1)} all-reduce(f32[16]{0:T(128)S(1)} %divide_multiply_fusion), channel_id=1, replica_groups=mesh['dp'=2,'fsdp'=16] {'dp','fsdp'}, use_global_device_ids=true, to_apply=%region_35.36 | all-reduce | flops 16 | bytes 128 | tf_op jit(solution)/shard_map/psum | solution.py:300
  755.8 12.9 multiply_reduce_fusion.4
  771.6 3.0 pad_maximum_fusion.3
  774.7 10.4 copy.111
  785.1 320.0 %all-reduce.12 = bf16[2,768,1024]{2,0,1:T(2,128)(2,1)} all-reduce(f32[2,768,1024]{2,0,1:T(2,128)} %copy.111), channel_id=2, replica_groups=mesh['dp'=2,'fsdp'=16] {'fsdp'}, use_global_device_ids=true, to_apply=%region_17.18.clone | all-reduce | flops 1572864 | bytes 9437184
  1106.9 8.1 fusion.68
  1116.6 1.9 convert_element_type.167
  1118.5 123.4 %reduce-scatter.11.cloned.1.call-done = f32[192,1024]{1,0:T(8,128)} async-done(((f32[3072,1024]{1,0:T(8,128)}), f32[192,1024]{1,0:T(8,128)}) %reduce-scatter.11.cloned.1.call-update) | async-done | bytes 786448 | tf_op jit(solution)/shard_map/reduce_scatter | solution.py:291
  1241.9 1.9 convert_element_type.173
  1243.9 365.2 %reduce-scatter.9.cloned.1.call-done = f32[64,6144]{1,0:T(8,128)} async-done(((f32[1024,6144]{1,0:T(8,128)}), f32[64,6144]{1,0:T(8,128)}) %reduce-scatter.9.cloned.1.call-update) | async-done | bytes 1572880 | tf_op jit(solution)/shard_map/reduce_scatter | solution.py:290
  1609.1 2.4 convert_element_type.171
  1611.5 12.2 add_convert_fusion.1
  1623.8 9.8 all-reduce.11.cloned.1.call-done
  1638.6 2.1 fusion.86
  1646.4 42.5 %psum.54 = f32[]{:T(128)} all-reduce(f32[]{:T(128)S(6)} %add.248), channel_id=1, replica_groups=mesh['dp'=2,'fsdp'=16] {'fsdp'}, use_global_device_ids=true, to_apply=%region_32.33 | all-reduce | flops 1 | bytes 8 | tf_op jit(solution)/shard_map/psum | solution.py:305
  1690.9 3.6 divide_subtract_fusion.1
  1694.6 3.0 divide_subtract_fusion
  (246 shorter events, 56.2 us)
Async XLA Ops:
  7.2 75.0 %copy-start = (bf16[4,768]{1,0:T(4,128)(2,1)S(1)}, bf16[4,768]{1,0:T(4,128)(2,1)}, u32[]{:S(2)}) copy-start(bf16[4,768]{1,0:T(4,128)(2,1)} %param.27) | copy-start | bytes 18436
  7.2 10.2 copy-start.64
  7.2 10.2 copy-start.66
  7.2 11.7 copy-start.6
  7.2 75.0 %all-gather.6.cloned.1.call-start = ((), (), s32[]{:S(2)}) async-start(), calls=%async_computation.4 | async-start | bytes 3342336 | tf_op jit(solution)/shard_map/all_gather | solution.py:184
  9.2 169.1 %all-gather.8.cloned.1.call-start = ((), (), s32[]{:S(2)}) async-start(), calls=%async_computation.5 | async-start | bytes 6684672 | tf_op jit(solution)/shard_map/all_gather | solution.py:185
  11.1 262.9 %all-gather.14.cloned.1.call-start = ((), (), s32[]{:S(2)}) async-start(), calls=%async_computation.8 | async-start | bytes 6684672 | tf_op jit(solution)/shard_map/all_gather | solution.py:188
  13.2 323.2 %all-gather.10.cloned.1.call-start = ((), (), s32[]{:S(2)}) async-start(), calls=%async_computation.6 | async-start | bytes 2228224 | tf_op jit(solution)/shard_map/all_gather | solution.py:186
  14.9 475.4 %all-gather.12.cloned.1.call-start = ((), (), s32[]{:S(2)}) async-start(), calls=%async_computation.7 | async-start | bytes 13369344 | tf_op jit(solution)/shard_map/all_gather | solution.py:187
  17.3 1097.7 %reduce-scatter.7.cloned.1.call-start = ((), (), s32[]{:S(2)}) async-start(), calls=%async_computation.10 | async-start | bytes 4456448 | tf_op jit(solution)/shard_map/reduce_scatter | solution.py:289
  17.4 185.6 %copy-start.62 = (f32[16]{0:T(128)}, f32[16]{0:T(128)S(1)}, u32[]{:S(2)}) copy-start(f32[16]{0:T(128)S(1)} %sqrt.24) | copy-start | bytes 196
  82.2 3.7 copy-start.21
  86.3 502.1 %copy-start.54 = (f32[4,1024]{1,0:T(4,128)}, f32[4,1024]{1,0:T(4,128)S(1)}, u32[]{:S(2)}) copy-start(f32[4,1024]{1,0:T(4,128)S(1)} %fusion.92) | copy-start | bytes 49156
  178.2 9.3 copy-start.25
  198.2 5.3 copy-start.2
  206.4 3.6 copy-start.10
  274.1 11.4 copy-start.9
  274.1 11.4 copy-start.11
  274.1 11.4 copy-start.38
  274.1 11.4 copy-start.40
  343.9 244.5 %copy-start.58 = (f32[4,256]{1,0:T(4,128)}, f32[4,256]{1,0:T(4,128)S(1)}, u32[]{:S(2)}) copy-start(f32[4,256]{1,0:T(4,128)S(1)} %fusion.118) | copy-start | bytes 12292
  588.4 4.6 copy-start.56
  610.1 506.5 %reduce-scatter.5.cloned.1.call-start = ((), (), s32[]{:S(2)}) async-start(), calls=%async_computation.9 | async-start | bytes 13369344 | tf_op jit(solution)/shard_map/reduce_scatter | solution.py:288
  610.2 36.0 %copy-start.39 = (f32[4,256,16]{1,2,0:T(8,128)S(1)}, f32[4,256,16]{1,2,0:T(8,128)}, u32[]{:S(2)}) copy-start(f32[4,256,16]{1,2,0:T(8,128)} %get-tuple-element.284) | copy-start | bytes 196612
  610.2 36.0 %copy-start.41 = (f32[4,256,16]{1,2,0:T(8,128)S(1)}, f32[4,256,16]{1,2,0:T(8,128)}, u32[]{:S(2)}) copy-start(f32[4,256,16]{1,2,0:T(8,128)} %get-tuple-element.285) | copy-start | bytes 196612
  610.6 2.7 copy-start.3
  610.6 2.7 copy-start.5
  618.5 2.7 copy-start.15
  626.8 2.7 copy-start.5
  634.7 2.8 copy-start.15
  643.0 2.9 copy-start.18
  643.0 4.1 copy-start.17
  647.2 7.5 slice-start
  648.1 6.5 copy-start.45
  648.1 6.6 copy-start.43
  648.1 6.6 slice-start.1
  648.1 6.7 slice-start.2
  660.8 3.8 copy-start.26
  673.8 568.2 %reduce-scatter.11.cloned.1.call-start = ((), (), s32[]{:S(2)}) async-start(), calls=%async_computation.12 | async-start | bytes 13369344 | tf_op jit(solution)/shard_map/reduce_scatter | solution.py:291
  687.9 921.2 %reduce-scatter.9.cloned.1.call-start = ((), (), s32[]{:S(2)}) async-start(), calls=%async_computation.11 | async-start | bytes 26738688 | tf_op jit(solution)/shard_map/reduce_scatter | solution.py:290
  712.5 43.3 %copy-start.7 = (bf16[1024,1024]{1,0:T(8,128)(2,1)S(1)}, bf16[1024,1024]{1,0:T(8,128)(2,1)}, u32[]{:S(2)}) copy-start(bf16[1024,1024]{1,0:T(8,128)(2,1)} %param.26) | copy-start | bytes 6291460
  712.5 43.3 %copy-start.53 = (f32[4,1024]{1,0:T(4,128)S(1)}, f32[4,1024]{1,0:T(4,128)}, u32[]{:S(2)}) copy-start(f32[4,1024]{1,0:T(4,128)} %copy-done.52) | copy-start | bytes 49156
  712.5 921.0 %all-reduce.11.cloned.1.call-start = ((), (), s32[]{:S(2)}) async-start(), calls=%async_computation.13 | async-start | bytes 3801088 | tf_op jit(solution)/shard_map/psum | solution.py:294
  755.8 14.4 copy-start.60
  785.1 321.8 %copy-start.57 = (f32[4,256]{1,0:T(4,128)S(1)}, f32[4,256]{1,0:T(4,128)}, u32[]{:S(2)}) copy-start(f32[4,256]{1,0:T(4,128)} %copy-done.56) | copy-start | bytes 12292
  1611.5 78.8 %copy-start.67 = (f32[16]{0:T(128)S(1)}, f32[16]{0:T(128)}, u32[]{:S(2)}) copy-start(f32[16]{0:T(128)} %param.46) | copy-start | bytes 196
  1611.5 78.8 %copy-start.68 = (f32[16]{0:T(128)S(1)}, f32[16]{0:T(128)}, u32[]{:S(2)}) copy-start(f32[16]{0:T(128)} %param.47) | copy-start | bytes 196
  1611.5 79.4 %copy-start.23 = (f32[192,1024]{1,0:T(8,128)S(1)}, f32[192,1024]{1,0:T(8,128)}, u32[]{:S(2)}) copy-start(f32[192,1024]{1,0:T(8,128)} %param.42) | copy-start | bytes 2359300
  1623.8 70.7 %copy-start.14 = (f32[64,6144]{1,0:T(8,128)S(1)}, f32[64,6144]{1,0:T(8,128)}, u32[]{:S(2)}) copy-start(f32[64,6144]{1,0:T(8,128)} %param.39) | copy-start | bytes 4718596
  1633.5 60.9 %copy-start.22 = (bf16[64,6144]{1,0:T(8,128)(2,1)S(1)}, bf16[64,6144]{1,0:T(8,128)(2,1)}, u32[]{:S(2)}) copy-start(bf16[64,6144]{1,0:T(8,128)(2,1)} %get-tuple-element.240) | copy-start | bytes 2359300
  1690.3 4.1 copy-start.28
  1690.3 4.1 copy-start.29
  1694.5 3.1 copy-start.34
  1694.5 3.1 copy-start.46
  1694.5 3.1 copy-start.50
  1694.5 3.0 copy-start.51
  1694.5 4.1 copy-start.24
  1694.5 4.1 copy-start.31
  1694.5 4.1 copy-start.35
  1694.5 4.1 copy-start.36
  1697.5 2.8 copy-start.30
  1697.6 2.8 copy-start.37
  1697.6 2.8 copy-start.48
  1697.6 2.8 copy-start.49
  (25 other events, 38.7 us)
Sparse Core Ops, SparseCore 0:
  11.3 70.8 all-gather.5
  85.6 92.6 all-gather.7
  181.6 92.4 all-gather.13
  277.3 58.9 all-gather.9
  339.5 150.6 all-gather.11
  610.2 93.4 reduce-scatter.6
  709.4 286.3 reduce-scatter.4
  1002.4 239.4 reduce-scatter.10
  1247.7 361.3 reduce-scatter.8
  1613.4 20.1 all-reduce.10
where the time goes:
time: 1710 us
  waiting for transfers between devices  894 us (52%)
  blocking collectives  404 us (24%)
  matrix products  196 us (11%)
  other arithmetic  142 us (8%)
  local copies, waits for them, and re-layouts  50.1 us (3%)
  between operations  21.7 us (1%)
    reduce_scatter x1, waiting for transfers between devices, local(): lax.psum_scatter(grad_up, 'fsdp', scatter_dimension=0, tiled=True)  365 us
    unnamed x1, blocking collectives  320 us
    all_gather x1, waiting for transfers between devices, local(): lax.all_gather(low_shards[3], 'fsdp', axis=0, tiled=True)  146 us
    reduce_scatter x1, waiting for transfers between devices, local(): lax.psum_scatter(grad_down, 'fsdp', scatter_dimension=0, tiled=True)  123 us
    all_gather x1, waiting for transfers between devices, local(): lax.all_gather(low_shards[1], 'fsdp', axis=0, tiled=True)  91.9 us
    all_gather x1, waiting for transfers between devices, local(): lax.all_gather(low_shards[4], 'fsdp', axis=0, tiled=True)  62.9 us
    all_gather x1, waiting for transfers between devices, local(): lax.all_gather(low_shards[0], 'fsdp', axis=1, tiled=True)  62.2 us
    another operation x6, other arithmetic  54.9 us
  transfers between devices with their start and end apart: 10, of which 8 were waited for; matrix products, arithmetic and copies ran while one was open for 13% of the time, Pallas kernels for 0%

commit v1 on v0

v1 whole, which is shorter than its diff:
```python
import functools
import math

import jax
import jax.numpy as jnp
import numpy as np
from jax import lax
from jax.experimental import pallas as pl
from jax.experimental.pallas import tpu as pltpu
from jax.sharding import PartitionSpec as P

FF = 3072
STEP = 10


NORM_EPS = 1e-06
COSINE_EPS = 1e-06
ROPE_BASE = 100.0
CLIP = 1.0
RATE = 0.02
OUTPUT_RATE = 0.2
SCALE_RATE = 8.0
BETA_ONE = 0.9
BETA_TWO = 0.95
ADAM_EPS = 1e-08
DECAY = 0.01
PRECISE = lax.Precision.HIGHEST
AXES = ("dp", "fsdp")
LOW = jnp.bfloat16
WIDE = jnp.float32


class Net:
    def __init__(self, size, dp_size):
        self.size = size
        self.dp_size = dp_size
        self.sub = size // 16
        self.core = lax.axis_index("dp")
        self.me = lax.axis_index("fsdp") // self.sub
        self.gather_order = ((8, 4, 1, 2), (8, 4, 2, 1))
        self.scatter_order = ((1, 2, 4, 8), (2, 1, 4, 8))

    def exchange(self, array, bits):
        pairs = []
        for core in range(self.dp_size):
            for place in range(self.size):
                target = place ^ (bits[core % 2] * self.sub)
                pairs.append((core * self.size + place, core * self.size + target))
        return lax.ppermute(array, AXES, pairs)

    def swap(self, array):
        pairs = []
        for core in range(self.dp_size):
            for place in range(self.size):
                pairs.append((core * self.size + place, (core ^ 1) * self.size + place))
        return lax.ppermute(array, AXES, pairs)

    def origins(self, order, sibling=False):
        tables = []
        for core in range(2):
            bits = order[core ^ 1] if sibling else order[core]
            table = []
            for index in range(16):
                value = 0
                for stage in range(4):
                    if index >> stage & 1:
                        value ^= bits[stage]
                table.append(value)
            tables.append(table)
        table = jnp.asarray(tables, jnp.int32)[self.core]
        return table ^ self.me

    def join_sub(self, shard):
        if self.sub == 1:
            return shard
        groups = [list(range(g * self.sub, (g + 1) * self.sub)) for g in range(16)]
        return lax.all_gather(shard, "fsdp", axis=0, tiled=True, axis_index_groups=groups)

    def gather(self, half):
        low, high = self.gather_order
        held = half[None]
        for stage in range(3):
            other = self.exchange(held, (low[stage], high[stage]))
            held = jnp.concatenate([held, other], axis=0)
        far = self.exchange(held, (low[3], high[3]))
        return held, far, self.swap(held), self.swap(far)

    def scatter(self, held):
        low, high = self.scatter_order
        for stage in range(4):
            count = held.shape[0] // 2
            other = self.exchange(held[count:], (low[stage], high[stage]))
            held = (held[:count].astype(WIDE) + other.astype(WIDE)).astype(LOW)
        return held[0]

    def table(self, order):
        return jnp.concatenate(
            [self.origins(order), self.origins(order, True), self.core[None]]
        ).astype(jnp.int32)

    def split_sub(self, gradient):
        if self.sub == 1:
            return gradient
        groups = [list(range(g * self.sub, (g + 1) * self.sub)) for g in range(16)]
        gathered = lax.all_gather(gradient, "fsdp", axis=0, axis_index_groups=groups)
        rows = gradient.shape[0] // self.sub
        place = lax.axis_index("fsdp") % self.sub
        return lax.dynamic_slice_in_dim(jnp.sum(gathered, axis=0), place * rows, rows, axis=0)

    def gather_small(self, rows):
        if self.sub > 1:
            return lax.all_gather(rows, AXES, axis=0, tiled=True)
        for bit in (8, 4, 2, 1):
            rows = jnp.concatenate([rows, self.exchange(rows, (bit, bit))], axis=0)
        return jnp.concatenate([rows, self.swap(rows)], axis=0)

    def total(self, value):
        if self.sub > 1:
            return lax.psum(value, "fsdp")
        value = jnp.broadcast_to(value, (1, 128))
        for bit in (1, 2, 4, 8):
            value = value + self.exchange(value, (bit, bit))
        return value[0, 0]


def half_rows(shard, core):
    rows = shard.shape[0] // 2
    return lax.dynamic_slice_in_dim(shard, core * rows, rows, axis=0).astype(LOW)


def owner_start(table_ref, index, rows, side):
    return pl.multiple_of(table_ref[index] * (2 * rows) + side * rows, 16)


def load_weight(table_ref, pieces, full_ref, sems):
    core = table_ref[32]
    rows = pieces[0].shape[1]
    copies = []
    for number, piece in enumerate(pieces):
        side = core if number < 2 else 1 - core
        for index in range(8):
            start = owner_start(table_ref, number * 8 + index, rows, side)
            copies.append(
                pltpu.make_async_copy(
                    piece.at[index], full_ref.at[pl.ds(start, rows)], sems.at[number, index]
                )
            )
    return copies


def fetch(copies):
    for copy in copies:
        copy.start()
    for copy in copies:
        copy.wait()


ANY = pl.BlockSpec(memory_space=pl.ANY)
SMEM = pl.BlockSpec(memory_space=pltpu.SMEM)
NT = (((1,), (1,)), ((), ()))
VMEM_LIMIT = 56 * 1024 * 1024


def params(dims):
    return pltpu.CompilerParams(
        dimension_semantics=("arbitrary",) * dims, vmem_limit_bytes=VMEM_LIMIT
    )


def mul(a, b):
    return jnp.dot(a, b, preferred_element_type=WIDE)


def mul_nt(a, b):
    return lax.dot_general(a, b, NT, preferred_element_type=WIDE)


def whole(shape):
    return pl.BlockSpec(shape, lambda *_: (0,) * len(shape))


def rotate(values, cos_rep, up_rep, down_rep, sign):
    ahead = pltpu.roll(values, values.shape[-1] - 16, 1)
    behind = pltpu.roll(values, 16, 1)
    turned = ahead * up_rep + behind * down_rep
    return values * cos_rep + (turned if sign > 0 else -turned)


def front_kernel(
    table_ref, x_ref, scale_ref, p0, p1, p2, p3, sums_ref, spread_ref, root_ref,
    cos_ref, up_ref, down_ref, act_ref, q_ref, k_ref, v_ref, pack_ref, w_ref, sems,
):
    @pl.when(pl.program_id(0) == 0)
    def _():
        fetch(load_weight(table_ref, (p0, p1, p2, p3), w_ref, sems))

    width = x_ref.shape[1]
    x = x_ref[...].astype(WIDE)
    inverse = lax.rsqrt(jnp.mean(x * x, axis=-1, keepdims=True) + NORM_EPS)
    act = (x * inverse * scale_ref[0]).astype(LOW)
    act_ref[...] = act
    v_ref[...] = mul(act, w_ref[:, 2 * width :]).astype(LOW)
    q = mul(act, w_ref[:, :width])
    k = mul(act, w_ref[:, width : 2 * width])
    sums = mul((q * q).astype(LOW), sums_ref[0]) + mul((k * k).astype(LOW), sums_ref[1])
    factor = lax.rsqrt(sums + COSINE_EPS)
    high = factor.astype(LOW)
    low = (factor - high.astype(WIDE)).astype(LOW)
    lane = lax.broadcasted_iota(jnp.int32, factor.shape, 1)
    pack = jnp.where(lane < 32, high.astype(WIDE), jnp.where(lane < 64, low.astype(WIDE), 0.0))
    pack = pack.astype(LOW)
    pack_ref[...] = pack
    q = q * mul(pack, spread_ref[0]) * root_ref[...]
    k = k * mul(pack, spread_ref[1]) * root_ref[...]
    cos_rep, up_rep, down_rep = cos_ref[...], up_ref[...], down_ref[...]
    for pair in range(width // 128):
        lanes = slice(pair * 128, pair * 128 + 128)
        q_ref[:, lanes] = rotate(q[:, lanes], cos_rep, up_rep, down_rep, 1).astype(LOW)
        k_ref[:, lanes] = rotate(k[:, lanes], cos_rep, up_rep, down_rep, 1).astype(LOW)


def front(table, x, scale, pieces, sums, spread, root, turns, images):
    tokens, width = x.shape
    seq = tokens // images
    row = pl.BlockSpec((seq, width), lambda i: (i, 0))
    narrow = pl.BlockSpec((seq, 128), lambda i: (i, 0))
    full = jax.ShapeDtypeStruct((tokens, width), LOW)
    return pl.pallas_call(
        front_kernel,
        grid=(images,),
        in_specs=[SMEM, row, pl.BlockSpec((1, 1, width), lambda i: (i, 0, 0)), ANY, ANY, ANY, ANY,
                  whole(sums.shape), whole(spread.shape), whole(root.shape), narrow, narrow, narrow],
        out_specs=[row, row, row, row, narrow],
        out_shape=[full, full, full, full, jax.ShapeDtypeStruct((tokens, 128), LOW)],
        scratch_shapes=[pltpu.VMEM((width, 3 * width), LOW), pltpu.SemaphoreType.DMA((4, 8))],
        compiler_params=params(1),
        cost_estimate=pl.CostEstimate(flops=6 * tokens * width * width, bytes_accessed=20 << 20, transcendentals=0),
        name="front",
    )(table, x, scale, *pieces, sums, spread, root, *turns)


def attend_kernel(q_ref, k_ref, v_ref, valid_ref, o_ref, lse_ref):
    seq, width = q_ref.shape
    valid = valid_ref[...]
    lane = lax.broadcasted_iota(jnp.int32, (seq, 128), 1)
    first = lane < 64
    totals = jnp.zeros((seq, 128), WIDE)
    zero = jnp.zeros((seq, 128), LOW)
    for pair in range(width // 128):
        lanes = slice(pair * 128, pair * 128 + 128)
        q, k = q_ref[:, lanes], k_ref[:, lanes]
        v = v_ref[:, lanes] * valid
        mixed = None
        for half in range(2):
            pick = first if half == 0 else jnp.logical_not(first)
            scores = mul_nt(jnp.where(pick, q, zero), k)
            weights = jnp.exp(scores).astype(LOW)
            right = jnp.concatenate([jnp.where(pick, v, zero), valid], axis=1)
            both = mul(weights, right)
            total = both[:, 128:]
            part = both[:, :128] / total
            mixed = part if mixed is None else mixed + part
            totals = jnp.where(lane == 2 * pair + half, total, totals)
        o_ref[:, lanes] = mixed.astype(LOW)
    lane_ok = lane < width // 64
    lse = jnp.log(jnp.where(lane_ok, totals, 1.0))
    lse_ref[0] = lse.T[: width // 64]


def attend(q, k, v, valid, images):
    tokens, width = q.shape
    seq = tokens // images
    row = pl.BlockSpec((seq, width), lambda i: (i, 0))
    heads = width // 64
    return pl.pallas_call(
        attend_kernel,
        grid=(images,),
        in_specs=[row, row, row, pl.BlockSpec((seq, 128), lambda i: (i, 0))],
        out_specs=[row, pl.BlockSpec((1, heads, seq), lambda i: (i, 0, 0))],
        out_shape=[jax.ShapeDtypeStruct((tokens, width), LOW),
                   jax.ShapeDtypeStruct((images, heads, seq), WIDE)],
        compiler_params=params(1),
        cost_estimate=pl.CostEstimate(flops=16 * tokens * seq * width, bytes_accessed=8 << 20, transcendentals=0),
        name="attend",
    )(q, k, v, valid)


def middle_kernel(table_ref, o_ref, x_ref, scale_ref, p0, p1, p2, p3, mid_ref, act_ref, w_ref, sems):
    @pl.when(pl.program_id(0) == 0)
    def _():
        fetch(load_weight(table_ref, (p0, p1, p2, p3), w_ref, sems))

    mid = x_ref[...].astype(WIDE) + mul(o_ref[...], w_ref[...])
    mid_ref[...] = mid
    inverse = lax.rsqrt(jnp.mean(mid * mid, axis=-1, keepdims=True) + NORM_EPS)
    act_ref[...] = (mid * inverse * scale_ref[0]).astype(LOW)


def middle_block(table, o, x, scale, pieces, images):
    tokens, width = x.shape
    seq = tokens // images
    row = pl.BlockSpec((seq, width), lambda i: (i, 0))
    return pl.pallas_call(
        middle_kernel,
        grid=(images,),
        in_specs=[SMEM, row, row, pl.BlockSpec((1, 1, width), lambda i: (i, 0, 0)), ANY, ANY, ANY, ANY],
        out_specs=[row, row],
        out_shape=[jax.ShapeDtypeStruct((tokens, width), WIDE), jax.ShapeDtypeStruct((tokens, width), LOW)],
        scratch_shapes=[pltpu.VMEM((width, width), LOW), pltpu.SemaphoreType.DMA((4, 8))],
        compiler_params=params(1),
        cost_estimate=pl.CostEstimate(flops=2 * tokens * width * width, bytes_accessed=12 << 20, transcendentals=0),
        name="middle",
    )(table, o, x, scale, *pieces)


def gate_kernel(table_ref, act_ref, dy_ref, u0, u1, u2, u3, d0, d1, d2, d3,
                hid_ref, dgu_ref, up_ref, down_ref, sems, sems_down):
    step = pl.program_id(1)

    @pl.when((pl.program_id(0) == 0) & (step == 0))
    def _():
        fetch(
            load_weight(table_ref, (u0, u1, u2, u3), up_ref, sems)
            + load_weight(table_ref, (d0, d1, d2, d3), down_ref, sems_down)
        )

    hidden = hid_ref.shape[1]
    size = 512
    at = pl.multiple_of(step * size, size)
    above = pl.multiple_of(hidden + step * size, size)
    act = act_ref[...]
    gate = mul(act, up_ref[:, pl.ds(at, size)])
    upper = mul(act, up_ref[:, pl.ds(above, size)])
    grad = mul_nt(dy_ref[...], down_ref[pl.ds(at, size), :]).astype(LOW).astype(WIDE)
    cdf = 0.5 * (1.0 + lax.erf(gate * math.sqrt(0.5)))
    bell = jnp.exp(-0.5 * gate * gate) * (1.0 / math.sqrt(2.0 * math.pi))
    gelu = gate * cdf
    hid_ref[:, pl.ds(at, size)] = (gelu * upper).astype(LOW)
    dgu_ref[:, pl.ds(at, size)] = (grad * upper * (cdf + gate * bell)).astype(LOW)
    dgu_ref[:, pl.ds(above, size)] = (grad * gelu).astype(LOW)


def gate_block(table, act, dy, up_pieces, down_pieces, images):
    tokens, width = act.shape
    seq = tokens // images
    hidden = 32 * down_pieces[0].shape[1]
    row = pl.BlockSpec((seq, width), lambda i, j: (i, 0))
    return pl.pallas_call(
        gate_kernel,
        grid=(images, hidden // 512),
        in_specs=[SMEM, row, row] + [ANY] * 8,
        out_specs=[pl.BlockSpec((seq, hidden), lambda i, j: (i, 0)),
                   pl.BlockSpec((seq, 2 * hidden), lambda i, j: (i, 0))],
        out_shape=[jax.ShapeDtypeStruct((tokens, hidden), LOW),
                   jax.ShapeDtypeStruct((tokens, 2 * hidden), LOW)],
        scratch_shapes=[pltpu.VMEM((width, 2 * hidden), LOW), pltpu.VMEM((hidden, width), LOW),
                        pltpu.SemaphoreType.DMA((4, 8)), pltpu.SemaphoreType.DMA((4, 8))],
        compiler_params=params(2),
        cost_estimate=pl.CostEstimate(flops=6 * tokens * width * hidden, bytes_accessed=40 << 20, transcendentals=0),
        name="geglu",
    )(table, act, dy, *up_pieces, *down_pieces)


def branch_kernel(table_ref, dgu_ref, dy_ref, mid_ref, scale_ref, u0, u1, u2, u3, o0, o1, o2, o3,
                  dmid_ref, db_ref, do_ref, dscale_ref, up_ref, out_ref, acc_ref, sems, sems_out):
    step = pl.program_id(1)

    @pl.when((pl.program_id(0) == 0) & (step == 0))
    def _():
        fetch(
            load_weight(table_ref, (u0, u1, u2, u3), up_ref, sems)
            + load_weight(table_ref, (o0, o1, o2, o3), out_ref, sems_out)
        )

    size = dgu_ref.shape[1]
    at = pl.multiple_of(step * size, size)
    part = mul_nt(dgu_ref[...], up_ref[:, pl.ds(at, size)])

    @pl.when(step == 0)
    def _():
        acc_ref[...] = part

    @pl.when(step > 0)
    def _():
        acc_ref[...] += part

    @pl.when(step == pl.num_programs(1) - 1)
    def _():
        grad = acc_ref[...]
        mid = mid_ref[...]
        inverse = lax.rsqrt(jnp.mean(mid * mid, axis=-1, keepdims=True) + NORM_EPS)
        normed = mid * inverse
        dscale_ref[0] = jnp.sum(grad * normed, axis=0, keepdims=True)
        grad = grad * scale_ref[0]
        inner = jnp.mean(grad * normed, axis=-1, keepdims=True)
        dmid = dy_ref[...].astype(WIDE) + inverse * (grad - normed * inner)
        dmid_ref[...] = dmid
        low = dmid.astype(LOW)
        db_ref[...] = low
        do_ref[...] = mul_nt(low, out_ref[...]).astype(LOW)


def branch_block(table, dgu, dy, mid, scale, up_pieces, out_pieces, images):
    tokens, width = dy.shape
    seq = tokens // images
    wide = dgu.shape[1]
    size = 1024
    row = pl.BlockSpec((seq, width), lambda i, j: (i, 0))
    one = pl.BlockSpec((1, 1, width), lambda i, j: (i, 0, 0))
    return pl.pallas_call(
        branch_kernel,
        grid=(images, wide // size),
        in_specs=[SMEM, pl.BlockSpec((seq, size), lambda i, j: (i, j)), row, row, one] + [ANY] * 8,
        out_specs=[row, row, row, one],
        out_shape=[jax.ShapeDtypeStruct((tokens, width), WIDE), jax.ShapeDtypeStruct((tokens, width), LOW),
                   jax.ShapeDtypeStruct((tokens, width), LOW), jax.ShapeDtypeStruct((images, 1, width), WIDE)],
        scratch_shapes=[pltpu.VMEM((width, wide), LOW), pltpu.VMEM((width, width), LOW),
                        pltpu.VMEM((seq, width), WIDE),
                        pltpu.SemaphoreType.DMA((4, 8)), pltpu.SemaphoreType.DMA((4, 8))],
        compiler_params=params(2),
        cost_estimate=pl.CostEstimate(flops=2 * tokens * width * (wide + width), bytes_accessed=40 << 20, transcendentals=0),
        name="branch",
    )(table, dgu, dy, mid, scale, *up_pieces, *out_pieces)


def attend_back_kernel(q_ref, k_ref, v_ref, o_ref, do_ref, lse_ref, valid_ref, pack_ref, spread_ref,
                       root_ref, pick_ref, block_ref, cos_ref, up_ref, down_ref, dproj_ref, dhead_ref):
    seq, width = q_ref.shape
    valid = valid_ref[...]
    valid_wide = valid.astype(WIDE)
    first = lax.broadcasted_iota(jnp.int32, (seq, 128), 1) < 64
    zero = jnp.zeros((seq, 128), LOW)
    cos_rep, up_rep, down_rep = cos_ref[...], up_ref[...], down_ref[...]
    product = (do_ref[...].astype(WIDE) * o_ref[...].astype(WIDE)).astype(LOW)
    delta = mul_nt(pick_ref[...], product)
    pack = pack_ref[...]
    block = block_ref[...]
    for pair in range(width // 128):
        lanes = slice(pair * 128, pair * 128 + 128)
        q, k, v, do = q_ref[:, lanes], k_ref[:, lanes], v_ref[:, lanes], do_ref[:, lanes]
        k_turned = (k * valid).T
        dv = dk = None
        dq_parts = []
        for half in range(2):
            head = 2 * pair + half
            pick = first if half == 0 else jnp.logical_not(first)
            q_one = jnp.where(pick, q, zero)
            do_one = jnp.where(pick, do, zero)
            weights = jnp.exp(mul_nt(k, q_one) - lse_ref[0, head : head + 1, :])
            grads = mul_nt(v, do_one)
            dscore = (weights * (grads - delta[head : head + 1, :])).astype(LOW)
            part_v = mul(weights.astype(LOW), do_one)
            part_k = mul(dscore, q_one)
            dv = part_v if dv is None else dv + part_v
            dk = part_k if dk is None else dk + part_k
            dq_parts.append(mul(k_turned[half * 64 : half * 64 + 64], dscore))
        dq = jnp.concatenate(dq_parts, axis=0).T
        dk = dk * valid_wide
        root = root_ref[:, lanes]
        for side, (grad, value) in enumerate(((dq, q), (dk, k))):
            value = value.astype(WIDE)
            inner = mul((grad * value).astype(LOW), block)
            total = jnp.sum(inner, axis=0, keepdims=True)
            if side == 0:
                head_total = total
            else:
                dhead_ref[0, :, lanes] = head_total + total
            factor = mul(pack, spread_ref[side, :, lanes])
            back = factor * (root * grad - value * (inner / root))
            back = rotate(back, cos_rep, up_rep, down_rep, -1)
            dproj_ref[:, side * width + pair * 128 : side * width + pair * 128 + 128] = back.astype(LOW)
        dproj_ref[:, 2 * width + pair * 128 : 2 * width + pair * 128 + 128] = (dv * valid_wide).astype(LOW)


def attend_back(q, k, v, o, do, lse, valid, pack, spread, root, pick, block, turns, images):
    tokens, width = q.shape
    seq = tokens // images
    heads = width // 64
    row = pl.BlockSpec((seq, width), lambda i: (i, 0))
    narrow = pl.BlockSpec((seq, 128), lambda i: (i, 0))
    return pl.pallas_call(
        attend_back_kernel,
        grid=(images,),
        in_specs=[row, row, row, row, row, pl.BlockSpec((1, heads, seq), lambda i: (i, 0, 0)), narrow, narrow,
                  whole(spread.shape), whole(root.shape), whole(pick.shape), whole(block.shape),
                  narrow, narrow, narrow],
        out_specs=[pl.BlockSpec((seq, 3 * width), lambda i: (i, 0)),
                   pl.BlockSpec((1, 1, width), lambda i: (i, 0, 0))],
        out_shape=[jax.ShapeDtypeStruct((tokens, 3 * width), LOW),
                   jax.ShapeDtypeStruct((images, 1, width), WIDE)],
        compiler_params=params(1),
        cost_estimate=pl.CostEstimate(flops=40 * tokens * seq * width, bytes_accessed=20 << 20, transcendentals=0),
        name="attend_back",
    )(q, k, v, o, do, lse, valid, pack, spread, root, pick, block, *turns)


def input_kernel(table_ref, dproj_ref, x_ref, dmid_ref, scale_ref, p0, p1, p2, p3,
                 out_ref, dscale_ref, w_ref, sems):
    @pl.when(pl.program_id(0) == 0)
    def _():
        fetch(load_weight(table_ref, (p0, p1, p2, p3), w_ref, sems))

    width = x_ref.shape[1]
    grad = mul_nt(dproj_ref[:, :width], w_ref[:, :width])
    grad += mul_nt(dproj_ref[:, width : 2 * width], w_ref[:, width : 2 * width])
    grad += mul_nt(dproj_ref[:, 2 * width :], w_ref[:, 2 * width :])
    x = x_ref[...].astype(WIDE)
    inverse = lax.rsqrt(jnp.mean(x * x, axis=-1, keepdims=True) + NORM_EPS)
    normed = x * inverse
    dscale_ref[0] = jnp.sum(grad * normed, axis=0, keepdims=True)
    grad = grad * scale_ref[0]
    inner = jnp.mean(grad * normed, axis=-1, keepdims=True)
    out_ref[...] = (dmid_ref[...] + inverse * (grad - normed * inner)).astype(LOW)


def input_block(table, dproj, x, dmid, scale, pieces, images):
    tokens, width = x.shape
    seq = tokens // images
    row = pl.BlockSpec((seq, width), lambda i: (i, 0))
    one = pl.BlockSpec((1, 1, width), lambda i: (i, 0, 0))
    return pl.pallas_call(
        input_kernel,
        grid=(images,),
        in_specs=[SMEM, pl.BlockSpec((seq, 3 * width), lambda i: (i, 0)), row, row, one] + [ANY] * 4,
        out_specs=[row, one],
        out_shape=[jax.ShapeDtypeStruct((tokens, width), LOW), jax.ShapeDtypeStruct((images, 1, width), WIDE)],
        scratch_shapes=[pltpu.VMEM((width, 3 * width), LOW), pltpu.SemaphoreType.DMA((4, 8))],
        compiler_params=params(1),
        cost_estimate=pl.CostEstimate(flops=6 * tokens * width * width, bytes_accessed=24 << 20, transcendentals=0),
        name="input_grad",
    )(table, dproj, x, dmid, scale, *pieces)


def result_kernel(table_ref, hid_ref, mid_ref, p0, p1, p2, p3, out_ref, w_ref, sems):
    @pl.when(pl.program_id(0) == 0)
    def _():
        fetch(load_weight(table_ref, (p0, p1, p2, p3), w_ref, sems))

    out_ref[...] = (mid_ref[...] + mul(hid_ref[...], w_ref[...])).astype(LOW)


def result_block(table, hid, mid, pieces, images):
    tokens, width = mid.shape
    seq = tokens // images
    hidden = hid.shape[1]
    row = pl.BlockSpec((seq, width), lambda i: (i, 0))
    return pl.pallas_call(
        result_kernel,
        grid=(images,),
        in_specs=[SMEM, pl.BlockSpec((seq, hidden), lambda i: (i, 0)), row] + [ANY] * 4,
        out_specs=row,
        out_shape=jax.ShapeDtypeStruct((tokens, width), LOW),
        scratch_shapes=[pltpu.VMEM((hidden, width), LOW), pltpu.SemaphoreType.DMA((4, 8))],
        compiler_params=params(1),
        cost_estimate=pl.CostEstimate(flops=2 * tokens * width * hidden, bytes_accessed=20 << 20, transcendentals=0),
        name="result",
    )(table, hid, mid, *pieces)


def weight_kernel(side, add, table_ref, act_ref, grad_ref, *rest):
    if add:
        other_ref, out_ref, turned_ref, left_ref = rest
    else:
        out_ref, turned_ref, left_ref = rest
    rows = left_ref.shape[0] // 16

    @pl.when(pl.program_id(0) == 0)
    def _():
        for start in range(0, act_ref.shape[1], 256):
            turned_ref[start : start + 256, :] = act_ref[:, start : start + 256].T
        core = table_ref[32]
        for index in range(16):
            start = owner_start(table_ref, side * 16 + index, rows, core if side == 0 else 1 - core)
            left_ref[index * rows : index * rows + rows, :] = turned_ref[pl.ds(start, rows), :]

    total = mul(left_ref[...], grad_ref[...])
    if add:
        total = total + other_ref[...].astype(WIDE)
    out_ref[...] = total.astype(LOW)


def weight_half(table, act, grad, side, other=None):
    tokens, depth = act.shape
    columns = grad.shape[1]
    size = 256
    half = depth // 2
    tile = pl.BlockSpec((half, size), lambda j: (0, j))
    extra = () if other is None else (other,)
    return pl.pallas_call(
        functools.partial(weight_kernel, side, other is not None),
        grid=(columns // size,),
        in_specs=[SMEM, whole(act.shape), pl.BlockSpec((tokens, size), lambda j: (0, j))] + [tile] * len(extra),
        out_specs=tile,
        out_shape=jax.ShapeDtypeStruct((half, columns), LOW),
        scratch_shapes=[pltpu.VMEM((depth, tokens), LOW), pltpu.VMEM((half, tokens), LOW)],
        compiler_params=params(1),
        cost_estimate=pl.CostEstimate(flops=tokens * depth * columns, bytes_accessed=(tokens * (depth + columns) + half * columns) * 2, transcendentals=0),
        name="weight_grad",
    )(table, act, grad, *extra)


def rope_tables(shapes, seq_len, head_dim):
    heights = shapes[:, 0:1]
    widths = shapes[:, 1:2]
    slot_index = jnp.arange(seq_len, dtype=jnp.int32)[None, :]
    row_index = slot_index // widths
    col_index = slot_index % widths
    valid_keys = slot_index < heights * widths
    freq_count = head_dim // 8
    frequency = ROPE_BASE ** (-jnp.arange(freq_count, dtype=jnp.float32) / freq_count)
    angles = jnp.concatenate(
        [
            row_index.astype(jnp.float32)[..., None] * frequency,
            col_index.astype(jnp.float32)[..., None] * frequency,
        ],
        axis=-1,
    )
    return (jnp.cos(angles), jnp.sin(angles), valid_keys)


def turn_tables(shapes, seq_len, head_dim):
    cosine, sine, valid = rope_tables(shapes, seq_len, head_dim)
    tokens = cosine.shape[0] * seq_len
    cosine = cosine.reshape(tokens, -1)
    sine = sine.reshape(tokens, -1)
    ones = jnp.ones((tokens, head_dim // 2), WIDE)
    none = jnp.zeros_like(sine)
    blank = jnp.zeros((tokens, head_dim // 2), WIDE)
    cos_rep = jnp.concatenate([cosine, cosine, ones] * 2, axis=1)
    up_rep = jnp.concatenate([-sine, none, blank] * 2, axis=1)
    down_rep = jnp.concatenate([none, sine, blank] * 2, axis=1)
    valid = jnp.broadcast_to(valid.reshape(tokens, 1), (tokens, 128)).astype(LOW)
    return (cos_rep, up_rep, down_rep), valid


def head_matrices(width, head_dim):
    heads = width // head_dim
    owner = np.arange(width) // head_dim
    sums = np.zeros((2, width, 128), np.float32)
    spread = np.zeros((2, 128, width), np.float32)
    for side in range(2):
        for copy in range(2):
            sums[side, np.arange(width), side * heads + copy * 2 * heads + owner] = 1.0
            spread[side, side * heads + copy * 2 * heads + owner, np.arange(width)] = 1.0
    pick = np.zeros((heads, width), np.float32)
    pick[owner, np.arange(width)] = 1.0
    block = np.kron(np.eye(128 // head_dim), np.ones((head_dim, head_dim)))
    return tuple(jnp.asarray(m, LOW) for m in (sums, spread, pick, block))


def adamw(weight, first_moment, second_moment, gradient, factor, rate, decay):
    clipped = gradient * factor
    new_first = BETA_ONE * first_moment + (1.0 - BETA_ONE) * clipped
    new_second = BETA_TWO * second_moment + (1.0 - BETA_TWO) * clipped * clipped
    denominator = jnp.sqrt(new_second / (1.0 - BETA_TWO**STEP)) + ADAM_EPS
    new_weight = (
        weight * (1.0 - rate * decay) - rate * (new_first / (1.0 - BETA_ONE**STEP)) / denominator
    )
    return (new_weight, new_first, new_second)


def local(
    tokens,
    condition,
    shapes,
    cotangent,
    ada_weight,
    ada_first,
    ada_second,
    qkv_weight,
    qkv_first,
    qkv_second,
    out_weight,
    out_first,
    out_second,
    up_weight,
    up_first,
    up_second,
    down_weight,
    down_first,
    down_second,
    head_scale,
    scale_first,
    scale_second,
    *,
    dp_size,
    fsdp_size,
):
    net = Net(fsdp_size, dp_size)
    core = net.core
    images = shapes.shape[0]
    width = tokens.shape[1]
    seq_len = tokens.shape[0] // images
    head_count = head_scale.shape[0]
    head_dim = width // head_count

    table = net.table(net.gather_order)
    scatter_table = net.table(tuple(order[::-1] for order in net.scatter_order))

    ada_rows = ada_weight.shape[1] * net.sub
    ada_flat = net.join_sub(ada_weight.transpose(1, 0, 2).reshape(ada_weight.shape[1], 2 * width))
    ada_pieces = net.gather(
        lax.dynamic_slice_in_dim(ada_flat, core * width, width, axis=1).astype(LOW)
    )
    qkv_pieces = net.gather(half_rows(net.join_sub(qkv_weight), core))
    out_pieces = net.gather(half_rows(net.join_sub(out_weight), core))
    up_pieces = net.gather(half_rows(net.join_sub(up_weight), core))
    down_pieces = net.gather(half_rows(net.join_sub(down_weight), core))

    condition_blocks = condition.reshape(images, 16, ada_rows)

    def project(low, high, order):
        weight = jnp.concatenate([low, high], axis=0)
        cond = jnp.take(condition_blocks, order, axis=1)
        return 1.0 + jnp.einsum("igr,grn->in", cond, weight, preferred_element_type=WIDE)

    scale_own = project(ada_pieces[0], ada_pieces[1], table[:16])
    scale_sib = project(ada_pieces[2], ada_pieces[3], table[16:32])
    scale_one = jnp.where(core == 0, scale_own, scale_sib)[:, None]
    scale_two = jnp.where(core == 0, scale_sib, scale_own)[:, None]

    turns, valid = turn_tables(shapes, seq_len, head_dim)
    sums, spread, pick, block = head_matrices(width, head_dim)
    root = jnp.repeat(jnp.sqrt(head_scale), head_dim)[None]

    act_one, q, k, v, pack = front(
        table, tokens, scale_one, qkv_pieces, sums, spread, root, turns, images
    )
    o, lse = attend(q, k, v, valid, images)
    mid, act_two = middle_block(table, o, tokens, scale_two, out_pieces, images)
    hid, dgu = gate_block(table, act_two, cotangent, up_pieces, down_pieces, images)

    def reduce_blocks(act, grad):
        send = weight_half(scatter_table, act, grad, 1)
        held = weight_half(scatter_table, act, grad, 0, net.swap(send))
        mine = net.scatter(held.reshape(16, held.shape[0] // 16, held.shape[1]))
        other = net.swap(mine)
        gradient = jnp.where(
            core == 0,
            jnp.concatenate([mine, other], axis=0),
            jnp.concatenate([other, mine], axis=0),
        ).astype(WIDE)
        return net.split_sub(gradient)

    grad_down = reduce_blocks(hid, cotangent)
    grad_up = reduce_blocks(act_two, dgu)
    dmid, db, do, dscale_two = branch_block(
        table, dgu, cotangent, mid, scale_two, up_pieces, out_pieces, images
    )
    grad_outw = reduce_blocks(o, db)
    dproj, dhead = attend_back(
        q, k, v, o, do, lse, valid, pack, spread, root, pick, block, turns, images
    )
    grad_qkv = reduce_blocks(act_one, dproj)
    input_grad, dscale_one = input_block(
        table, dproj, tokens, dmid, scale_one, qkv_pieces, images
    )
    block_output = result_block(table, hid, mid, down_pieces, images)

    dhead = jnp.sum(dhead.reshape(images, head_count, head_dim)[:, :, 0], axis=0)
    dhead = jnp.broadcast_to(dhead / (2.0 * head_scale), (images, head_count)) / images
    early = net.gather_small(jnp.concatenate([condition.astype(WIDE), dscale_two[:, 0]], axis=1))
    late = net.gather_small(jnp.concatenate([dscale_one[:, 0], dhead], axis=1))
    own_rows = ada_weight.shape[1]
    cond_own = lax.dynamic_slice_in_dim(
        early[:, : condition.shape[1]], lax.axis_index("fsdp") * own_rows, own_rows, axis=1
    )
    grad_ada = jnp.stack(
        [
            jnp.dot(cond_own.T, late[:, :width], precision=PRECISE),
            jnp.dot(cond_own.T, early[:, condition.shape[1] :], precision=PRECISE),
        ]
    )
    head_grad = jnp.sum(late[:, width:], axis=0)

    owned = (grad_ada, grad_qkv, grad_outw, grad_up, grad_down)
    local_squares = (
        jnp.sum(owned[0] * owned[0]) + jnp.sum(owned[1] * owned[1]) + jnp.sum(owned[2] * owned[2])
    )
    local_squares = local_squares + jnp.sum(owned[3] * owned[3]) + jnp.sum(owned[4] * owned[4])
    total = net.total(local_squares) + jnp.sum(head_grad * head_grad)
    grad_norm = jnp.sqrt(total)
    factor = jnp.minimum(1.0, CLIP / (grad_norm + 1e-06))
    ada_new = adamw(ada_weight, ada_first, ada_second, owned[0], factor, RATE, DECAY)
    qkv_new = adamw(qkv_weight, qkv_first, qkv_second, owned[1], factor, RATE, DECAY)
    out_new = adamw(out_weight, out_first, out_second, owned[2], factor, OUTPUT_RATE, DECAY)
    up_new = adamw(up_weight, up_first, up_second, owned[3], factor, RATE, DECAY)
    down_new = adamw(down_weight, down_first, down_second, owned[4], factor, RATE, DECAY)
    scale_new = adamw(head_scale, scale_first, scale_second, head_grad, factor, SCALE_RATE, 0.0)
    return (
        block_output,
        input_grad,
        grad_norm,
        *ada_new,
        *qkv_new,
        *out_new,
        *up_new,
        *down_new,
        *scale_new,
    )


def solution(mesh):
    tokens = P(("dp", "fsdp"), None)
    ada = P(None, "fsdp", None)
    rows = P("fsdp", None)
    return jax.shard_map(
        functools.partial(local, dp_size=mesh.shape["dp"], fsdp_size=mesh.shape["fsdp"]),
        mesh=mesh,
        in_specs=(tokens,) * 4 + (ada,) * 3 + (rows,) * 12 + (P(),) * 3,
        out_specs=(tokens, tokens, P()) + (ada,) * 3 + (rows,) * 12 + (P(),) * 3,
        check_vma=False,
    )
```

time: 1710 us -> 705 us (0.41)
  waiting for transfers between devices: 894 us -> 245 us
  blocking collectives: 404 us -> 0 us
  Pallas kernels: 0 us -> 278 us
  matrix products: 196 us -> 3.31 us
  other arithmetic: 142 us -> 38.6 us
  starting transfers between devices: 0.41 us -> 62.8 us
    reduce_scatter x4 -> x0, waiting for transfers between devices: 489 us -> none  [the longest x1 365 us: local(): lax.psum_scatter(grad_up, 'fsdp', scatter_dimension=0, tiled=True)]
    all_gather x5 -> x0, waiting for transfers between devices: 396 us -> none  [the longest x1 146 us: local(): lax.all_gather(low_shards[3], 'fsdp', axis=0, tiled=True)]
    unnamed x1 -> x0, blocking collectives: 320 us -> none
    pallas_call x0 -> x16, Pallas kernels: none -> 278 us  [the longest x8 105 us: weight_half(): pl.pallas_call(functools.partial(weight_kernel, side, other is not None),...]
    ppermute x0 -> x68, waiting for transfers between devices: none -> 245 us  [the longest x48 245 us: exchange(): return lax.ppermute(array, AXES, pairs)]
    dot_general x30 -> x4, matrix products: 196 us -> 3.31 us  [the longest x2 2.36 us: project(): jnp.einsum('igr,grn->in', cond, weight, preferred_element_type=WIDE)]
    psum x2 -> x0, blocking collectives: 83.8 us -> none  [the longest x1 42.5 us: local(): total = lax.psum(local_squares, 'fsdp') + jnp.sum(head_grad * head_grad)]
    ppermute x0 -> x68, starting transfers between devices: none -> 62.8 us  [the longest x48 58.3 us: exchange(): return lax.ppermute(array, AXES, pairs)]
  transfers between devices with their start and end apart: 10 -> 68, of which waited for: 8 -> 25; matrix products, arithmetic and copies ran while one was open for 13% -> 12% of each run, Pallas kernels for 0% -> 31%
where the time goes in v1:
time: 705 us; the launch traced here: 692 us
  Pallas kernels  278 us (39%)
  waiting for transfers between devices  245 us (35%)
  starting transfers between devices  62.8 us (9%)
  local copies, waits for them, and re-layouts  57.4 us (8%)
  other arithmetic  38.6 us (5%)
  between operations  7.33 us (1%)
    ppermute x48, waiting for transfers between devices, exchange(): return lax.ppermute(array, AXES, pairs)  245 us
    pallas_call x8, Pallas kernels, weight_half(): pl.pallas_call(functools.partial(weight_kernel, side, other is not None),...  105 us
    ppermute x48, starting transfers between devices, exchange(): return lax.ppermute(array, AXES, pairs)  58.3 us
    pallas_call x1, Pallas kernels, gate_block(): pl.pallas_call(gate_kernel, grid=(images, hidden // 512), in_specs=[SMEM,...  41.6 us
    pallas_call x1, Pallas kernels, branch_block(): pl.pallas_call(branch_kernel, grid=(images, wide // size), in_specs=[SMEM...  37.8 us
    pallas_call x1, Pallas kernels, attend_back(): pl.pallas_call(attend_back_kernel, grid=(images,), in_specs=[row, row, ro...  29.9 us
    pallas_call x1, Pallas kernels, front(): pl.pallas_call(front_kernel, grid=(images,), in_specs=[SMEM, row, pl.Bloc...  19.6 us
    pallas_call x1, Pallas kernels, input_block(): pl.pallas_call(input_kernel, grid=(images,), in_specs=[SMEM, pl.BlockSpec...  14.6 us
  transfers between devices with their start and end apart: 68, of which 25 were waited for; matrix products, arithmetic and copies ran while one was open for 12% of the time, Pallas kernels for 31%

profile of v1, /device:TPU:0, one launch (start us, length us, event | category | flops | bytes accessed | tf_op | source)
XLA Modules:
  0.0 692.1 jit_solution(6217857926440297973)
XLA Ops:
  1.9 4.1 collective-permute-start.18
  6.0 17.5 %collective-permute-done.18 = bf16[1,32,6144]{2,1,0:T(8,128)(2,1)S(1)} collective-permute-done((bf16[1,32,6144]{2,1,0:T(8,128)(2,1)S(1)}, bf16[1,32,6144]{2,1,0:T(8,128)(2,1)S(1)}, u32[]{:S(2)}, u32[]{:S(2)}) %collective-permute-start.18) | collective-permute-done | bytes 393248 | tf_op jit(solution)/shard_map/ppermute | solution.py:49
  25.9 3.4 collective-permute-start
  29.3 16.2 %collective-permute-done.19 = bf16[2,32,6144]{2,1,0:T(8,128)(2,1)S(1)} collective-permute-done((bf16[2,32,6144]{2,1,0:T(8,128)(2,1)}, bf16[2,32,6144]{2,1,0:T(8,128)(2,1)S(1)}, u32[]{:S(2)}, u32[]{:S(2)}) %collective-permute-start.19) | collective-permute-done | bytes 786464 | tf_op jit(solution)/shard_map/ppermute | solution.py:49
  49.1 2.8 collective-permute-start.6
  54.1 2.8 collective-permute-start.24
  56.9 12.2 %collective-permute-done.12 = bf16[1,32,1024]{2,1,0:T(8,128)(2,1)S(1)} collective-permute-done((bf16[1,32,1024]{2,1,0:T(8,128)(2,1)S(1)}, bf16[1,32,1024]{2,1,0:T(8,128)(2,1)S(1)}, u32[]{:S(2)}, u32[]{:S(2)}) %collective-permute-start.12) | collective-permute-done | bytes 65568 | tf_op jit(solution)/shard_map/ppermute | solution.py:49
  69.3 2.1 collective-permute-start.7
  71.3 2.9 pad_maximum_fusion.u0
  76.5 7.5 %collective-permute-done.7 = bf16[2,32,3072]{2,1,0:T(8,128)(2,1)S(1)} collective-permute-done((bf16[2,32,3072]{2,1,0:T(8,128)(2,1)S(1)}, bf16[2,32,3072]{2,1,0:T(8,128)(2,1)S(1)}, u32[]{:S(2)}, u32[]{:S(2)}) %collective-permute-start.7) | collective-permute-done | bytes 393248 | tf_op jit(solution)/shard_map/ppermute | solution.py:49
  85.1 3.1 collective-permute-done.1
  90.4 4.8 collective-permute-done.25
  97.6 15.5 %collective-permute-done.2 = bf16[4,48,1024]{2,1,0:T(8,128)(2,1)S(1)} collective-permute-done((bf16[4,48,1024]{2,1,0:T(8,128)(2,1)S(1)}, bf16[4,48,1024]{2,1,0:T(8,128)(2,1)S(1)}, u32[]{:S(2)}, u32[]{:S(2)}) %collective-permute-start.2) | collective-permute-done | bytes 393248 | tf_op jit(solution)/shard_map/ppermute | solution.py:49
  117.6 21.9 %collective-permute-done.15.p1.o1 = bf16[8,32,1024]{2,1,0:T(8,128)(2,1)} collective-permute-done((bf16[8,32,1024]{2,1,0:T(8,128)(2,1)}, bf16[8,32,1024]{2,1,0:T(8,128)(2,1)}, u32[]{:S(2)}, u32[]{:S(2)}) %collective-permute-start.15) | collective-permute-done | bytes 524320 | tf_op jit(solution)/shard_map/ppermute | solution.py:49
  140.1 7.7 %collective-permute-done.3 = bf16[8,48,1024]{2,1,0:T(8,128)(2,1)S(1)} collective-permute-done((bf16[8,48,1024]{2,1,0:T(8,128)(2,1)}, bf16[8,48,1024]{2,1,0:T(8,128)(2,1)S(1)}, u32[]{:S(2)}, u32[]{:S(2)}) %collective-permute-start.3) | collective-permute-done | bytes 786464 | tf_op jit(solution)/shard_map/ppermute | solution.py:49
  149.7 2.4 pad_maximum_fusion.3.d0.p0
  154.4 10.3 %collective-permute-done.9.p1 = bf16[8,32,3072]{2,1,0:T(8,128)(2,1)} collective-permute-done((bf16[8,32,3072]{2,1,0:T(8,128)(2,1)}, bf16[8,32,3072]{2,1,0:T(8,128)(2,1)}, u32[]{:S(2)}, u32[]{:S(2)}) %collective-permute-start.9) | collective-permute-done | bytes 1572896 | tf_op jit(solution)/shard_map/ppermute | solution.py:49
  165.6 1.7 concatenate.162.down_ref
  172.7 8.9 %collective-permute-done.27.d1.p1 = bf16[8,96,1024]{2,1,0:T(8,128)(2,1)} collective-permute-done((bf16[8,96,1024]{2,1,0:T(8,128)(2,1)}, bf16[8,96,1024]{2,1,0:T(8,128)(2,1)}, u32[]{:S(2)}, u32[]{:S(2)}) %collective-permute-start.27) | collective-permute-done | bytes 1572896 | tf_op jit(solution)/shard_map/ppermute | solution.py:49
  182.1 1.9 select_bitcast_fusion
  185.7 19.6 %front.1 = (bf16[1024,1024]{1,0:T(8,128)(2,1)}, bf16[1024,1024]{1,0:T(8,128)(2,1)}, bf16[1024,1024]{1,0:T(8,128)(2,1)}, bf16[1024,1024]{1,0:T(8,128)(2,1)}, bf16[1024,128]{1,0:T(8,128)(2,1)}) custom-call(s32[33]{0:T(128)} %get-tuple-element.99.table_ref, bf16[1024,1024]{1,0:T(8,128)(2,1)} %x_ref.5, f32[4,1,1024]{2,1,0:T(1,128)} %broadcast_in_dim.64.scale_ref, ...), custom_call_target="tpu_custom_call" | custom-call | flops 6442450944 | bytes 20971520 | tf_op jit(solution)/shard_map/front/pallas_call | solution.py:228
  206.2 8.0 %attend.1 = (bf16[1024,1024]{1,0:T(8,128)(2,1)}, f32[4,16,256]{2,1,0:T(8,128)}) custom-call(bf16[1024,1024]{1,0:T(8,128)(2,1)} %get-tuple-element.41.q_ref, bf16[1024,1024]{1,0:T(8,128)(2,1)} %get-tuple-element.42.k_ref, bf16[1024,1024]{1,0:T(8,128)(2,1)} %get-tuple-element.43.v_ref, bf16[1024,128]{1,0:T(8,128)(2,1)} %broadcast_in_dim.70.valid_ref), custom_call_target="tpu_custom_call" | custom-call | flops 4294967296 | bytes 8388608 | tf_op jit(solution)/shard_map/attend/pallas_call | solution.py:275
  215.0 8.3 %middle.1 = (f32[1024,1024]{1,0:T(8,128)}, bf16[1024,1024]{1,0:T(8,128)(2,1)}) custom-call(s32[33]{0:T(128)} %get-tuple-element.99.table_ref, bf16[1024,1024]{1,0:T(8,128)(2,1)} %get-tuple-element.44.o_ref.act_ref, bf16[1024,1024]{1,0:T(8,128)(2,1)} %x_ref.5, f32[4,1,1024]{2,1,0:T(1,128)} %copy.79.scale_ref, bf16[8,32,1024]{2,1,0:T(8,128)(2,1)} %pad_maximum_fusion.8.p0.o0, ...), custom_call_target="tpu_custom_call" | custom-call | flops 2147483648 | bytes 12582912 | tf_op jit(solution)/shard_map/middle/pallas_call | solution.py:303
  225.0 41.6 %geglu.1 = (bf16[1024,3072]{1,0:T(8,128)(2,1)}, bf16[1024,6144]{1,0:T(8,128)(2,1)}) custom-call(s32[33]{0:T(128)} %get-tuple-element.99.table_ref, bf16[1024,1024]{1,0:T(8,128)(2,1)} %get-tuple-element.45.act_ref, bf16[1024,1024]{1,0:T(8,128)(2,1)} %grad_ref.3, bf16[8,32,6144]{2,1,0:T(8,128)(2,1)} %pad_maximum_fusion.u0, ...), custom_call_target="tpu_custom_call" | custom-call | flops 19327352832 | bytes 41943040 | tf_op jit(solution)/shard_map/geglu/pallas_call | solution.py:348
  266.7 22.4 %weight_grad.12 = bf16[512,6144]{1,0:T(8,128)(2,1)} custom-call(s32[33]{0:T(128)} %get-tuple-element.98.table_ref, bf16[1024,1024]{1,0:T(8,128)(2,1)} %get-tuple-element.45.act_ref, bf16[1024,6144]{1,0:T(8,128)(2,1)} %get-tuple-element.48.dgu_ref.grad_ref), custom_call_target="tpu_custom_call" | custom-call | flops 6442450944 | bytes 20971520 | tf_op jit(solution)/shard_map/weight_grad/pallas_call | solution.py:589
  289.1 37.8 %branch.1 = (f32[1024,1024]{1,0:T(8,128)}, bf16[1024,1024]{1,0:T(8,128)(2,1)}, bf16[1024,1024]{1,0:T(8,128)(2,1)}, f32[4,1,1024]{2,1,0:T(1,128)}) custom-call(s32[33]{0:T(128)} %get-tuple-element.99.table_ref, bf16[1024,6144]{1,0:T(8,128)(2,1)} %get-tuple-element.48.dgu_ref.grad_ref, bf16[1024,1024]{1,0:T(8,128)(2,1)} %grad_ref.3, ...), custom_call_target="tpu_custom_call" | custom-call | flops 15032385536 | bytes 41943040 | tf_op jit(solution)/shard_map/branch/pallas_call | solution.py:410
  327.6 2.1 collective-permute-start.30
  329.7 29.9 %attend_back.1 = (bf16[1024,3072]{1,0:T(8,128)(2,1)}, f32[4,1,1024]{2,1,0:T(1,128)}) custom-call(bf16[1024,1024]{1,0:T(8,128)(2,1)} %get-tuple-element.41.q_ref, bf16[1024,1024]{1,0:T(8,128)(2,1)} %get-tuple-element.42.k_ref, bf16[1024,1024]{1,0:T(8,128)(2,1)} %get-tuple-element.43.v_ref, bf16[1024,1024]{1,0:T(8,128)(2,1)} %get-tuple-element.44.o_ref.act_ref, ...), custom_call_target="tpu_custom_call" | custom-call | flops 10737418240 | bytes 20971520 | tf_op jit(solution)/shard_map/attend_back/pallas_call | solution.py:481
  360.6 12.5 %weight_grad.8 = bf16[512,3072]{1,0:T(8,128)(2,1)} custom-call(s32[33]{0:T(128)} %get-tuple-element.98.table_ref, bf16[1024,1024]{1,0:T(8,128)(2,1)} %get-tuple-element.58.act_ref, bf16[1024,3072]{1,0:T(8,128)(2,1)} %get-tuple-element.52.dproj_ref.grad_ref), custom_call_target="tpu_custom_call" | custom-call | flops 3221225472 | bytes 11534336 | tf_op jit(solution)/shard_map/weight_grad/pallas_call | solution.py:589
  373.3 14.6 %input_grad.1 = (bf16[1024,1024]{1,0:T(8,128)(2,1)}, f32[4,1,1024]{2,1,0:T(1,128)}) custom-call(s32[33]{0:T(128)} %get-tuple-element.99.table_ref, bf16[1024,3072]{1,0:T(8,128)(2,1)} %get-tuple-element.52.dproj_ref.grad_ref, bf16[1024,1024]{1,0:T(8,128)(2,1)} %x_ref.5, f32[1024,1024]{1,0:T(8,128)} %get-tuple-element.53.dmid_ref, ...), custom_call_target="tpu_custom_call" | custom-call | flops 6442450944 | bytes 25165824 | tf_op jit(solution)/shard_map/input_grad/pallas_call | solution.py:521
  389.7 5.9 weight_grad.10
  397.8 1.8 collective-permute-done.36
  402.2 2.7 collective-permute-done.37
  408.6 10.3 %weight_grad.14 = bf16[1536,1024]{1,0:T(8,128)(2,1)} custom-call(s32[33]{0:T(128)} %get-tuple-element.98.table_ref, bf16[1024,3072]{1,0:T(8,128)(2,1)} %get-tuple-element.46.hid_ref.act_ref, bf16[1024,1024]{1,0:T(8,128)(2,1)} %grad_ref.3), custom_call_target="tpu_custom_call" | custom-call | flops 3221225472 | bytes 11534336 | tf_op jit(solution)/shard_map/weight_grad/pallas_call | solution.py:589
  419.0 5.9 concatenate.182
  425.4 3.4 concatenate.176
  428.8 6.0 weight_grad.11
  437.7 13.1 %weight_grad.9 = bf16[512,3072]{1,0:T(8,128)(2,1)} custom-call(s32[33]{0:T(128)} %get-tuple-element.98.table_ref, bf16[1024,1024]{1,0:T(8,128)(2,1)} %get-tuple-element.58.act_ref, bf16[1024,3072]{1,0:T(8,128)(2,1)} %get-tuple-element.52.dproj_ref.grad_ref, bf16[512,3072]{1,0:T(8,128)(2,1)} %copy-done.3), custom_call_target="tpu_custom_call" | custom-call | flops 3221225472 | bytes 11534336 | tf_op jit(solution)/shard_map/weight_grad/pallas_call | solution.py:589
  450.8 23.5 %weight_grad.13 = bf16[512,6144]{1,0:T(8,128)(2,1)} custom-call(s32[33]{0:T(128)} %get-tuple-element.98.table_ref, bf16[1024,1024]{1,0:T(8,128)(2,1)} %get-tuple-element.45.act_ref, bf16[1024,6144]{1,0:T(8,128)(2,1)} %get-tuple-element.48.dgu_ref.grad_ref, bf16[512,6144]{1,0:T(8,128)(2,1)} %collective-permute-done.52.rest_0_), custom_call_target="tpu_custom_call" | custom-call | flops 6442450944 | bytes 20971520 | tf_op jit(solution)/shard_map/weight_grad/pallas_call | solution.py:589
  474.3 5.2 fusion.83
  480.2 1.9 fusion.85
  485.6 7.5 %concatenate.183 = f32[128,1040]{1,0:T(8,128)} concatenate(f32[4,1040]{1,0:T(4,128)} %copy-done.34, f32[4,1040]{1,0:T(4,128)} %copy-done.27, f32[8,1040]{1,0:T(8,128)} %copy-done.24, f32[16,1040]{1,0:T(8,128)} %copy-done.23, f32[32,1040]{1,0:T(8,128)} %collective-permute-done.38, f32[64,1040]{1,0:T(8,128)} %collective-permute-done.39), dimensions={0} | concatenate | bytes 1064960 | tf_op jit(solution)/shard_map/concatenate | solution.py:115
  493.1 5.1 concatenate.177
  502.6 3.2 collective-permute-done.49
  505.8 2.6 collective-permute-start.50
  508.4 11.1 %weight_grad.15 = bf16[1536,1024]{1,0:T(8,128)(2,1)} custom-call(s32[33]{0:T(128)} %get-tuple-element.98.table_ref, bf16[1024,3072]{1,0:T(8,128)(2,1)} %get-tuple-element.46.hid_ref.act_ref, bf16[1024,1024]{1,0:T(8,128)(2,1)} %grad_ref.3, bf16[1536,1024]{1,0:T(8,128)(2,1)} %collective-permute-done.58.rest_0_), custom_call_target="tpu_custom_call" | custom-call | flops 3221225472 | bytes 11534336 | tf_op jit(solution)/shard_map/weight_grad/pallas_call | solution.py:589
  519.5 2.3 fusion.84
  523.3 13.5 %collective-permute-done.41 = bf16[8,32,3072]{2,1,0:T(8,128)(2,1)} collective-permute-done((bf16[8,32,3072]{2,1,0:T(8,128)(2,1)}, bf16[8,32,3072]{2,1,0:T(8,128)(2,1)}, u32[]{:S(2)}, u32[]{:S(2)}) %collective-permute-start.41) | collective-permute-done | bytes 1572896 | tf_op jit(solution)/shard_map/ppermute | solution.py:49
  536.8 2.0 fusion.2
  539.4 3.0 fusion
  544.2 21.7 %collective-permute-done.59 = bf16[8,96,1024]{2,1,0:T(8,128)(2,1)S(1)} collective-permute-done((bf16[8,96,1024]{2,1,0:T(8,128)(2,1)S(1)}, bf16[8,96,1024]{2,1,0:T(8,128)(2,1)S(1)}, u32[]{:S(2)}, u32[]{:S(2)}) %collective-permute-start.59) | collective-permute-done | bytes 1572896 | tf_op jit(solution)/shard_map/ppermute | solution.py:49
  569.2 17.6 %collective-permute-done.60 = bf16[4,96,1024]{2,1,0:T(8,128)(2,1)S(1)} collective-permute-done((bf16[4,96,1024]{2,1,0:T(8,128)(2,1)S(1)}, bf16[4,96,1024]{2,1,0:T(8,128)(2,1)S(1)}, u32[]{:S(2)}, u32[]{:S(2)}) %collective-permute-start.60) | collective-permute-done | bytes 786464 | tf_op jit(solution)/shard_map/ppermute | solution.py:49
  589.8 2.6 collective-permute-start.44
  592.4 10.9 %collective-permute-done.61 = bf16[2,96,1024]{2,1,0:T(8,128)(2,1)S(1)} collective-permute-done((bf16[2,96,1024]{2,1,0:T(8,128)(2,1)S(1)}, bf16[2,96,1024]{2,1,0:T(8,128)(2,1)S(1)}, u32[]{:S(2)}, u32[]{:S(2)}) %collective-permute-start.61) | collective-permute-done | bytes 393248 | tf_op jit(solution)/shard_map/ppermute | solution.py:49
  605.2 18.6 %collective-permute-done.55 = bf16[2,32,6144]{2,1,0:T(8,128)(2,1)S(1)} collective-permute-done((bf16[2,32,6144]{2,1,0:T(8,128)(2,1)S(1)}, bf16[2,32,6144]{2,1,0:T(8,128)(2,1)S(1)}, u32[]{:S(2)}, u32[]{:S(2)}) %collective-permute-start.55) | collective-permute-done | bytes 786464 | tf_op jit(solution)/shard_map/ppermute | solution.py:49
  625.8 18.1 %collective-permute-done.56 = bf16[1,32,6144]{2,1,0:T(8,128)(2,1)S(1)} collective-permute-done((bf16[1,32,6144]{2,1,0:T(8,128)(2,1)S(1)}, bf16[1,32,6144]{2,1,0:T(8,128)(2,1)S(1)}, u32[]{:S(2)}, u32[]{:S(2)}) %collective-permute-start.56) | collective-permute-done | bytes 393248 | tf_op jit(solution)/shard_map/ppermute | solution.py:49
  653.2 2.9 collective-permute-done.64
  656.6 13.2 %result.1 = bf16[1024,1024]{1,0:T(8,128)(2,1)} custom-call(s32[33]{0:T(128)} %get-tuple-element.99.table_ref, bf16[1024,3072]{1,0:T(8,128)(2,1)} %get-tuple-element.46.hid_ref.act_ref, f32[1024,1024]{1,0:T(8,128)} %get-tuple-element.47.mid_ref, bf16[8,96,1024]{2,1,0:T(8,128)(2,1)} %pad_maximum_fusion.3.d0.p0, ...), custom_call_target="tpu_custom_call" | custom-call | flops 6442450944 | bytes 20971520 | tf_op jit(solution)/shard_map/result/pallas_call | solution.py:547
  670.0 3.5 collective-permute-done.66
  675.3 2.7 collective-permute-done.67
  678.8 2.4 divide_subtract_fusion.3
  681.8 1.8 divide_subtract_fusion.2
  685.7 3.0 divide_subtract_fusion
  688.7 1.8 divide_subtract_fusion.1
  (324 shorter events, 87.4 us)
Async XLA Ops:
  1.9 21.6 %collective-permute-start.18 = (bf16[1,32,6144]{2,1,0:T(8,128)(2,1)S(1)}, bf16[1,32,6144]{2,1,0:T(8,128)(2,1)S(1)}, u32[]{:S(2)}, u32[]{:S(2)}) collective-permute-start(bf16[1,32,6144]{2,1,0:T(8,128)(2,1)S(1)} %fusion.30), channel_id=1, source_target_pairs={{0,8},{1,9},{2,10},{3,11},{4,12},{5,13},{6,14},{7,15},{8,0},{9,1},... | collective-permute-start | bytes 1179656 | tf_op jit(solution)/shard_map/ppermute | solution.py:49
  24.5 21.0 %collective-permute-start.19 = (bf16[2,32,6144]{2,1,0:T(8,128)(2,1)}, bf16[2,32,6144]{2,1,0:T(8,128)(2,1)S(1)}, u32[]{:S(2)}, u32[]{:S(2)}) collective-permute-start(bf16[2,32,6144]{2,1,0:T(8,128)(2,1)} %pad_maximum_fusion.6), channel_id=1, source_target_pairs={{0,4},{1,5},{2,6},{3,7},{4,0},{5,1},{6,2},{7,3},{8,12},{9,13},{10,... | collective-permute-start | bytes 2359304 | tf_op jit(solution)/shard_map/ppermute | solution.py:49
  25.9 48.8 %collective-permute-start = (bf16[1,48,1024]{2,1,0:T(8,128)(2,1)S(1)}, bf16[1,48,1024]{2,1,0:T(8,128)(2,1)S(1)}, u32[]{:S(2)}, u32[]{:S(2)}) collective-permute-start(bf16[1,48,1024]{2,1,0:T(8,128)(2,1)S(1)} %get-tuple-element.83), channel_id=1, source_target_pairs={{0,8},{1,9},{2,10},{3,11},{4,12},{5,13},{6,14},{7,15},{8,0},{9,1},... | collective-permute-start | bytes 294920 | tf_op jit(solution)/shard_map/ppermute | solution.py:49
  46.8 24.5 %collective-permute-start.20 = (bf16[4,32,6144]{2,1,0:T(8,128)(2,1)}, bf16[4,32,6144]{2,1,0:T(8,128)(2,1)}, u32[]{:S(2)}, u32[]{:S(2)}) collective-permute-start(bf16[4,32,6144]{2,1,0:T(8,128)(2,1)} %pad_maximum_fusion.2), channel_id=1, source_target_pairs={{0,1},{1,0},{2,3},{3,2},{4,5},{5,4},{6,7},{7,6},{8,9},{9,8},{10,11... | collective-permute-start | bytes 4718600 | tf_op jit(solution)/shard_map/ppermute | solution.py:49
  49.1 20.1 %collective-permute-start.6 = (bf16[1,32,3072]{2,1,0:T(8,128)(2,1)S(1)}, bf16[1,32,3072]{2,1,0:T(8,128)(2,1)S(1)}, u32[]{:S(2)}, u32[]{:S(2)}) collective-permute-start(bf16[1,32,3072]{2,1,0:T(8,128)(2,1)S(1)} %fusion.36), channel_id=1, source_target_pairs={{0,8},{1,9},{2,10},{3,11},{4,12},{5,13},{6,14},{7,15},{8,0},{9,1},... | collective-permute-start | bytes 589832 | tf_op jit(solution)/shard_map/ppermute | solution.py:49
  52.8 16.3 %collective-permute-start.12 = (bf16[1,32,1024]{2,1,0:T(8,128)(2,1)S(1)}, bf16[1,32,1024]{2,1,0:T(8,128)(2,1)S(1)}, u32[]{:S(2)}, u32[]{:S(2)}) collective-permute-start(bf16[1,32,1024]{2,1,0:T(8,128)(2,1)S(1)} %fusion.41), channel_id=1, source_target_pairs={{0,8},{1,9},{2,10},{3,11},{4,12},{5,13},{6,14},{7,15},{8,0},{9,1},... | collective-permute-start | bytes 196616 | tf_op jit(solution)/shard_map/ppermute | solution.py:49
  54.1 30.9 %collective-permute-start.24 = (bf16[1,96,1024]{2,1,0:T(8,128)(2,1)S(1)}, bf16[1,96,1024]{2,1,0:T(8,128)(2,1)S(1)}, u32[]{:S(2)}, u32[]{:S(2)}) collective-permute-start(bf16[1,96,1024]{2,1,0:T(8,128)(2,1)S(1)} %fusion.37), channel_id=1, source_target_pairs={{0,8},{1,9},{2,10},{3,11},{4,12},{5,13},{6,14},{7,15},{8,0},{9,1},... | collective-permute-start | bytes 589832 | tf_op jit(solution)/shard_map/ppermute | solution.py:49
  69.1 6.5 collective-permute-start.13
  69.3 14.8 %collective-permute-start.7 = (bf16[2,32,3072]{2,1,0:T(8,128)(2,1)S(1)}, bf16[2,32,3072]{2,1,0:T(8,128)(2,1)S(1)}, u32[]{:S(2)}, u32[]{:S(2)}) collective-permute-start(bf16[2,32,3072]{2,1,0:T(8,128)(2,1)S(1)} %pad_maximum_fusion.10), channel_id=1, source_target_pairs={{0,4},{1,5},{2,6},{3,7},{4,0},{5,1},{6,2},{7,3},{8,12},{9,13},{10,... | collective-permute-start | bytes 1179656 | tf_op jit(solution)/shard_map/ppermute | solution.py:49
  74.2 79.9 %collective-permute-start.21 = (bf16[8,32,6144]{2,1,0:T(8,128)(2,1)}, bf16[8,32,6144]{2,1,0:T(8,128)(2,1)}, u32[]{:S(2)}, u32[]{:S(2)}) collective-permute-start(bf16[8,32,6144]{2,1,0:T(8,128)(2,1)} %pad_maximum_fusion.u0), channel_id=1, source_target_pairs={{0,2},{1,3},{2,0},{3,1},{4,6},{5,7},{6,4},{7,5},{8,10},{9,11},{10,... | collective-permute-start | bytes 9437192 | tf_op jit(solution)/shard_map/ppermute | solution.py:49
  74.8 13.5 %collective-permute-start.1 = (bf16[2,48,1024]{2,1,0:T(8,128)(2,1)S(1)}, bf16[2,48,1024]{2,1,0:T(8,128)(2,1)S(1)}, u32[]{:S(2)}, u32[]{:S(2)}) collective-permute-start(bf16[2,48,1024]{2,1,0:T(8,128)(2,1)S(1)} %pad_maximum_fusion.15), channel_id=1, source_target_pairs={{0,4},{1,5},{2,6},{3,7},{4,0},{5,1},{6,2},{7,3},{8,12},{9,13},{10,... | collective-permute-start | bytes 589832 | tf_op jit(solution)/shard_map/ppermute | solution.py:49
  75.7 13.5 %collective-permute-start.14 = (bf16[4,32,1024]{2,1,0:T(8,128)(2,1)S(1)}, bf16[4,32,1024]{2,1,0:T(8,128)(2,1)S(1)}, u32[]{:S(2)}, u32[]{:S(2)}) collective-permute-start(bf16[4,32,1024]{2,1,0:T(8,128)(2,1)S(1)} %pad_maximum_fusion.13), channel_id=1, source_target_pairs={{0,1},{1,0},{2,3},{3,2},{4,5},{5,4},{6,7},{7,6},{8,9},{9,8},{10,11... | collective-permute-start | bytes 786440 | tf_op jit(solution)/shard_map/ppermute | solution.py:49
  84.1 30.5 %collective-permute-start.8 = (bf16[4,32,3072]{2,1,0:T(8,128)(2,1)S(1)}, bf16[4,32,3072]{2,1,0:T(8,128)(2,1)S(1)}, u32[]{:S(2)}, u32[]{:S(2)}) collective-permute-start(bf16[4,32,3072]{2,1,0:T(8,128)(2,1)S(1)} %pad_maximum_fusion.5), channel_id=1, source_target_pairs={{0,1},{1,0},{2,3},{3,2},{4,5},{5,4},{6,7},{7,6},{8,9},{9,8},{10,11... | collective-permute-start | bytes 2359304 | tf_op jit(solution)/shard_map/ppermute | solution.py:49
  85.0 10.2 %collective-permute-start.25 = (bf16[2,96,1024]{2,1,0:T(8,128)(2,1)S(1)}, bf16[2,96,1024]{2,1,0:T(8,128)(2,1)S(1)}, u32[]{:S(2)}, u32[]{:S(2)}) collective-permute-start(bf16[2,96,1024]{2,1,0:T(8,128)(2,1)S(1)} %pad_maximum_fusion.11), channel_id=1, source_target_pairs={{0,4},{1,5},{2,6},{3,7},{4,0},{5,1},{6,2},{7,3},{8,12},{9,13},{10,... | collective-permute-start | bytes 1179656 | tf_op jit(solution)/shard_map/ppermute | solution.py:49
  88.3 24.8 %collective-permute-start.2 = (bf16[4,48,1024]{2,1,0:T(8,128)(2,1)S(1)}, bf16[4,48,1024]{2,1,0:T(8,128)(2,1)S(1)}, u32[]{:S(2)}, u32[]{:S(2)}) collective-permute-start(bf16[4,48,1024]{2,1,0:T(8,128)(2,1)S(1)} %pad_maximum_fusion.9), channel_id=1, source_target_pairs={{0,1},{1,0},{2,3},{3,2},{4,5},{5,4},{6,7},{7,6},{8,9},{9,8},{10,11... | collective-permute-start | bytes 1179656 | tf_op jit(solution)/shard_map/ppermute | solution.py:49
  90.1 49.4 %collective-permute-start.15 = (bf16[8,32,1024]{2,1,0:T(8,128)(2,1)}, bf16[8,32,1024]{2,1,0:T(8,128)(2,1)}, u32[]{:S(2)}, u32[]{:S(2)}) collective-permute-start(bf16[8,32,1024]{2,1,0:T(8,128)(2,1)} %pad_maximum_fusion.8.p0.o0), channel_id=1, source_target_pairs={{0,2},{1,3},{2,0},{3,1},{4,6},{5,7},{6,4},{7,5},{8,10},{9,11},{10,... | collective-permute-start | bytes 1572872 | tf_op jit(solution)/shard_map/ppermute | solution.py:49
  96.1 53.0 %collective-permute-start.26 = (bf16[4,96,1024]{2,1,0:T(8,128)(2,1)}, bf16[4,96,1024]{2,1,0:T(8,128)(2,1)}, u32[]{:S(2)}, u32[]{:S(2)}) collective-permute-start(bf16[4,96,1024]{2,1,0:T(8,128)(2,1)} %pad_maximum_fusion.7), channel_id=1, source_target_pairs={{0,1},{1,0},{2,3},{3,2},{4,5},{5,4},{6,7},{7,6},{8,9},{9,8},{10,11... | collective-permute-start | bytes 2359304 | tf_op jit(solution)/shard_map/ppermute | solution.py:49
  114.1 33.7 %collective-permute-start.3 = (bf16[8,48,1024]{2,1,0:T(8,128)(2,1)}, bf16[8,48,1024]{2,1,0:T(8,128)(2,1)S(1)}, u32[]{:S(2)}, u32[]{:S(2)}) collective-permute-start(bf16[8,48,1024]{2,1,0:T(8,128)(2,1)} %pad_maximum_fusion.4), channel_id=1, source_target_pairs={{0,2},{1,3},{2,0},{3,1},{4,6},{5,7},{6,4},{7,5},{8,10},{9,11},{10,... | collective-permute-start | bytes 2359304 | tf_op jit(solution)/shard_map/ppermute | solution.py:49
  115.9 48.8 %collective-permute-start.9 = (bf16[8,32,3072]{2,1,0:T(8,128)(2,1)}, bf16[8,32,3072]{2,1,0:T(8,128)(2,1)}, u32[]{:S(2)}, u32[]{:S(2)}) collective-permute-start(bf16[8,32,3072]{2,1,0:T(8,128)(2,1)} %pad_maximum_fusion.1.p0), channel_id=1, source_target_pairs={{0,2},{1,3},{2,0},{3,1},{4,6},{5,7},{6,4},{7,5},{8,10},{9,11},{10,... | collective-permute-start | bytes 4718600 | tf_op jit(solution)/shard_map/ppermute | solution.py:49
  139.5 12.8 %collective-permute-start.4 = (bf16[8,48,1024]{2,1,0:T(8,128)(2,1)}, bf16[8,48,1024]{2,1,0:T(8,128)(2,1)}, u32[]{:S(2)}, u32[]{:S(2)}) collective-permute-start(bf16[8,48,1024]{2,1,0:T(8,128)(2,1)} %pad_maximum_fusion.4), channel_id=1, source_target_pairs={{0,16},{1,17},{2,18},{3,19},{4,20},{5,21},{6,22},{7,23},{8,24},{9,... | collective-permute-start | bytes 2359304 | tf_op jit(solution)/shard_map/ppermute | solution.py:56
  147.8 5.3 collective-permute-start.5
  152.2 19.9 %collective-permute-start.10 = (bf16[8,32,3072]{2,1,0:T(8,128)(2,1)}, bf16[8,32,3072]{2,1,0:T(8,128)(2,1)}, u32[]{:S(2)}, u32[]{:S(2)}) collective-permute-start(bf16[8,32,3072]{2,1,0:T(8,128)(2,1)} %pad_maximum_fusion.1.p0), channel_id=1, source_target_pairs={{0,16},{1,17},{2,18},{3,19},{4,20},{5,21},{6,22},{7,23},{8,24},{9,... | collective-permute-start | bytes 4718600 | tf_op jit(solution)/shard_map/ppermute | solution.py:56
  152.3 29.3 %collective-permute-start.27 = (bf16[8,96,1024]{2,1,0:T(8,128)(2,1)}, bf16[8,96,1024]{2,1,0:T(8,128)(2,1)}, u32[]{:S(2)}, u32[]{:S(2)}) collective-permute-start(bf16[8,96,1024]{2,1,0:T(8,128)(2,1)} %pad_maximum_fusion.3.d0.p0), channel_id=1, source_target_pairs={{0,2},{1,3},{2,0},{3,1},{4,6},{5,7},{6,4},{7,5},{8,10},{9,11},{10,... | collective-permute-start | bytes 4718600 | tf_op jit(solution)/shard_map/ppermute | solution.py:49
  153.1 70.3 %collective-permute-start.22 = (bf16[8,32,6144]{2,1,0:T(8,128)(2,1)}, bf16[8,32,6144]{2,1,0:T(8,128)(2,1)}, u32[]{:S(2)}, u32[]{:S(2)}) collective-permute-start(bf16[8,32,6144]{2,1,0:T(8,128)(2,1)} %pad_maximum_fusion.u0), channel_id=1, source_target_pairs={{0,16},{1,17},{2,18},{3,19},{4,20},{5,21},{6,22},{7,23},{8,24},{9,... | collective-permute-start | bytes 9437192 | tf_op jit(solution)/shard_map/ppermute | solution.py:56
  154.2 69.2 %collective-permute-start.23 = (bf16[8,32,6144]{2,1,0:T(8,128)(2,1)}, bf16[8,32,6144]{2,1,0:T(8,128)(2,1)}, u32[]{:S(2)}, u32[]{:S(2)}) collective-permute-start(bf16[8,32,6144]{2,1,0:T(8,128)(2,1)} %collective-permute-done.21.u1), channel_id=1, source_target_pairs={{0,16},{1,17},{2,18},{3,19},{4,20},{5,21},{6,22},{7,23},{8,24},{9,... | collective-permute-start | bytes 9437192 | tf_op jit(solution)/shard_map/ppermute | solution.py:56
  164.7 20.5 %collective-permute-start.11 = (bf16[8,32,3072]{2,1,0:T(8,128)(2,1)}, bf16[8,32,3072]{2,1,0:T(8,128)(2,1)}, u32[]{:S(2)}, u32[]{:S(2)}) collective-permute-start(bf16[8,32,3072]{2,1,0:T(8,128)(2,1)} %collective-permute-done.9.p1), channel_id=1, source_target_pairs={{0,16},{1,17},{2,18},{3,19},{4,20},{5,21},{6,22},{7,23},{8,24},{9,... | collective-permute-start | bytes 4718600 | tf_op jit(solution)/shard_map/ppermute | solution.py:56
  172.1 51.2 %collective-permute-start.28 = (bf16[8,96,1024]{2,1,0:T(8,128)(2,1)}, bf16[8,96,1024]{2,1,0:T(8,128)(2,1)S(1)}, u32[]{:S(2)}, u32[]{:S(2)}) collective-permute-start(bf16[8,96,1024]{2,1,0:T(8,128)(2,1)} %pad_maximum_fusion.3.d0.p0), channel_id=1, source_target_pairs={{0,16},{1,17},{2,18},{3,19},{4,20},{5,21},{6,22},{7,23},{8,24},{9,... | collective-permute-start | bytes 4718600 | tf_op jit(solution)/shard_map/ppermute | solution.py:56
  181.6 41.8 %collective-permute-start.29 = (bf16[8,96,1024]{2,1,0:T(8,128)(2,1)}, bf16[8,96,1024]{2,1,0:T(8,128)(2,1)S(1)}, u32[]{:S(2)}, u32[]{:S(2)}) collective-permute-start(bf16[8,96,1024]{2,1,0:T(8,128)(2,1)} %collective-permute-done.27.d1.p1), channel_id=1, source_target_pairs={{0,16},{1,17},{2,18},{3,19},{4,20},{5,21},{6,22},{7,23},{8,24},{9,... | collective-permute-start | bytes 4718600 | tf_op jit(solution)/shard_map/ppermute | solution.py:56
  185.2 29.0 %collective-permute-start.17 = (bf16[8,32,1024]{2,1,0:T(8,128)(2,1)}, bf16[8,32,1024]{2,1,0:T(8,128)(2,1)S(1)}, u32[]{:S(2)}, u32[]{:S(2)}) collective-permute-start(bf16[8,32,1024]{2,1,0:T(8,128)(2,1)} %collective-permute-done.15.p1.o1), channel_id=1, source_target_pairs={{0,16},{1,17},{2,18},{3,19},{4,20},{5,21},{6,22},{7,23},{8,24},{9,... | collective-permute-start | bytes 1572872 | tf_op jit(solution)/shard_map/ppermute | solution.py:56
  289.0 161.8 %collective-permute-start.52 = (bf16[512,6144]{1,0:T(8,128)(2,1)}, bf16[512,6144]{1,0:T(8,128)(2,1)}, u32[]{:S(2)}, u32[]{:S(2)}) collective-permute-start(bf16[512,6144]{1,0:T(8,128)(2,1)} %weight_grad.12), channel_id=1, source_target_pairs={{0,16},{1,17},{2,18},{3,19},{4,20},{5,21},{6,22},{7,23},{8,24},{9,... | collective-permute-start | bytes 18874376 | tf_op jit(solution)/shard_map/ppermute | solution.py:56
  327.6 69.5 %collective-permute-start.30 = (f32[4,1792]{1,0:T(4,128)S(1)}, f32[4,1792]{1,0:T(4,128)S(1)}, u32[]{:S(2)}, u32[]{:S(2)}) collective-permute-start(f32[4,1792]{1,0:T(4,128)S(1)} %pad_maximum_fusion.23), channel_id=1, source_target_pairs={{0,8},{1,9},{2,10},{3,11},{4,12},{5,13},{6,14},{7,15},{8,0},{9,1},... | collective-permute-start | bytes 86024 | tf_op jit(solution)/shard_map/ppermute | solution.py:49
  373.1 63.0 %collective-permute-start.40 = (bf16[512,3072]{1,0:T(8,128)(2,1)}, bf16[512,3072]{1,0:T(8,128)(2,1)S(1)}, u32[]{:S(2)}, u32[]{:S(2)}) collective-permute-start(bf16[512,3072]{1,0:T(8,128)(2,1)} %weight_grad.8), channel_id=1, source_target_pairs={{0,16},{1,17},{2,18},{3,19},{4,20},{5,21},{6,22},{7,23},{8,24},{9,... | collective-permute-start | bytes 9437192 | tf_op jit(solution)/shard_map/ppermute | solution.py:56
  388.8 6.8 collective-permute-start.35
  395.6 33.2 %collective-permute-start.46 = (bf16[512,1024]{1,0:T(8,128)(2,1)}, bf16[512,1024]{1,0:T(8,128)(2,1)}, u32[]{:S(2)}, u32[]{:S(2)}) collective-permute-start(bf16[512,1024]{1,0:T(8,128)(2,1)} %weight_grad.10), channel_id=1, source_target_pairs={{0,16},{1,17},{2,18},{3,19},{4,20},{5,21},{6,22},{7,23},{8,24},{9,... | collective-permute-start | bytes 3145736 | tf_op jit(solution)/shard_map/ppermute | solution.py:56
  397.2 4.2 collective-permute-start.31
  399.7 5.2 collective-permute-start.37
  401.5 5.0 collective-permute-start.32
  404.9 14.0 %collective-permute-start.38 = (f32[32,1040]{1,0:T(8,128)S(1)}, f32[32,1040]{1,0:T(8,128)}, u32[]{:S(2)}, u32[]{:S(2)}) collective-permute-start(f32[32,1040]{1,0:T(8,128)S(1)} %pad_maximum_fusion.16), channel_id=1, source_target_pairs={{0,1},{1,0},{2,3},{3,2},{4,5},{5,4},{6,7},{7,6},{8,9},{9,8},{10,11... | collective-permute-start | bytes 399368 | tf_op jit(solution)/shard_map/ppermute | solution.py:49
  407.2 17.7 %collective-permute-start.33 = (f32[32,1792]{1,0:T(8,128)}, f32[32,1792]{1,0:T(8,128)S(1)}, u32[]{:S(2)}, u32[]{:S(2)}) collective-permute-start(f32[32,1792]{1,0:T(8,128)} %pad_maximum_fusion.14), channel_id=1, source_target_pairs={{0,1},{1,0},{2,3},{3,2},{4,5},{5,4},{6,7},{7,6},{8,9},{9,8},{10,11... | collective-permute-start | bytes 688136 | tf_op jit(solution)/shard_map/ppermute | solution.py:49
  418.9 89.5 %collective-permute-start.58 = (bf16[1536,1024]{1,0:T(8,128)(2,1)}, bf16[1536,1024]{1,0:T(8,128)(2,1)}, u32[]{:S(2)}, u32[]{:S(2)}) collective-permute-start(bf16[1536,1024]{1,0:T(8,128)(2,1)} %weight_grad.14), channel_id=1, source_target_pairs={{0,16},{1,17},{2,18},{3,19},{4,20},{5,21},{6,22},{7,23},{8,24},{9,... | collective-permute-start | bytes 9437192 | tf_op jit(solution)/shard_map/ppermute | solution.py:56
  424.9 60.3 %collective-permute-start.39 = (f32[64,1040]{1,0:T(8,128)}, f32[64,1040]{1,0:T(8,128)}, u32[]{:S(2)}, u32[]{:S(2)}) collective-permute-start(f32[64,1040]{1,0:T(8,128)} %concatenate.182), channel_id=1, source_target_pairs={{0,16},{1,17},{2,18},{3,19},{4,20},{5,21},{6,22},{7,23},{8,24},{9,... | collective-permute-start | bytes 798728 | tf_op jit(solution)/shard_map/ppermute | solution.py:56
  428.8 64.3 %collective-permute-start.34 = (f32[64,1792]{1,0:T(8,128)}, f32[64,1792]{1,0:T(8,128)}, u32[]{:S(2)}, u32[]{:S(2)}) collective-permute-start(f32[64,1792]{1,0:T(8,128)} %concatenate.176), channel_id=1, source_target_pairs={{0,16},{1,17},{2,18},{3,19},{4,20},{5,21},{6,22},{7,23},{8,24},{9,... | collective-permute-start | bytes 1376264 | tf_op jit(solution)/shard_map/ppermute | solution.py:56
  436.1 45.9 %collective-permute-start.47 = (bf16[8,32,1024]{2,1,0:T(8,128)(2,1)S(1)}, bf16[8,32,1024]{2,1,0:T(8,128)(2,1)S(1)}, u32[]{:S(2)}, u32[]{:S(2)}) collective-permute-start(bf16[8,32,1024]{2,1,0:T(8,128)(2,1)S(1)} %bitcast.102), channel_id=1, source_target_pairs={{0,1},{1,0},{2,3},{3,2},{4,5},{5,4},{6,7},{7,6},{8,9},{9,8},{10,11... | collective-permute-start | bytes 1572872 | tf_op jit(solution)/shard_map/ppermute | solution.py:49
  479.5 59.8 %collective-permute-start.53 = (bf16[8,32,6144]{2,1,0:T(8,128)(2,1)}, bf16[8,32,6144]{2,1,0:T(8,128)(2,1)}, u32[]{:S(2)}, u32[]{:S(2)}) collective-permute-start(bf16[8,32,6144]{2,1,0:T(8,128)(2,1)} %bitcast.28), channel_id=1, source_target_pairs={{0,1},{1,0},{2,3},{3,2},{4,5},{5,4},{6,7},{7,6},{8,9},{9,8},{10,11... | collective-permute-start | bytes 9437192 | tf_op jit(solution)/shard_map/ppermute | solution.py:49
  482.0 54.8 %collective-permute-start.41 = (bf16[8,32,3072]{2,1,0:T(8,128)(2,1)}, bf16[8,32,3072]{2,1,0:T(8,128)(2,1)}, u32[]{:S(2)}, u32[]{:S(2)}) collective-permute-start(bf16[8,32,3072]{2,1,0:T(8,128)(2,1)} %bitcast.22), channel_id=1, source_target_pairs={{0,1},{1,0},{2,3},{3,2},{4,5},{5,4},{6,7},{7,6},{8,9},{9,8},{10,11... | collective-permute-start | bytes 4718600 | tf_op jit(solution)/shard_map/ppermute | solution.py:49
  485.2 14.2 %collective-permute-start.48 = (bf16[4,32,1024]{2,1,0:T(8,128)(2,1)}, bf16[4,32,1024]{2,1,0:T(8,128)(2,1)}, u32[]{:S(2)}, u32[]{:S(2)}) collective-permute-start(bf16[4,32,1024]{2,1,0:T(8,128)(2,1)} %slice.202), channel_id=1, source_target_pairs={{0,2},{1,3},{2,0},{3,1},{4,6},{5,7},{6,4},{7,5},{8,10},{9,11},{10,... | collective-permute-start | bytes 786440 | tf_op jit(solution)/shard_map/ppermute | solution.py:49
  500.5 5.3 collective-permute-start.49
  505.8 61.3 %collective-permute-start.50 = (bf16[1,32,1024]{2,1,0:T(8,128)(2,1)S(1)}, bf16[1,32,1024]{2,1,0:T(8,128)(2,1)S(1)}, u32[]{:S(2)}, u32[]{:S(2)}) collective-permute-start(bf16[1,32,1024]{2,1,0:T(8,128)(2,1)S(1)} %slice.206), channel_id=1, source_target_pairs={{0,8},{1,9},{2,10},{3,11},{4,12},{5,13},{6,14},{7,15},{8,0},{9,1},... | collective-permute-start | bytes 196616 | tf_op jit(solution)/shard_map/ppermute | solution.py:49
  521.8 44.0 %collective-permute-start.59 = (bf16[8,96,1024]{2,1,0:T(8,128)(2,1)S(1)}, bf16[8,96,1024]{2,1,0:T(8,128)(2,1)S(1)}, u32[]{:S(2)}, u32[]{:S(2)}) collective-permute-start(bf16[8,96,1024]{2,1,0:T(8,128)(2,1)S(1)} %bitcast.100), channel_id=1, source_target_pairs={{0,1},{1,0},{2,3},{3,2},{4,5},{5,4},{6,7},{7,6},{8,9},{9,8},{10,11... | collective-permute-start | bytes 4718600 | tf_op jit(solution)/shard_map/ppermute | solution.py:49
  538.9 28.4 %collective-permute-start.42 = (bf16[4,32,3072]{2,1,0:T(8,128)(2,1)S(1)}, bf16[4,32,3072]{2,1,0:T(8,128)(2,1)S(1)}, u32[]{:S(2)}, u32[]{:S(2)}) collective-permute-start(bf16[4,32,3072]{2,1,0:T(8,128)(2,1)S(1)} %slice.194), channel_id=1, source_target_pairs={{0,2},{1,3},{2,0},{3,1},{4,6},{5,7},{6,4},{7,5},{8,10},{9,11},{10,... | collective-permute-start | bytes 2359304 | tf_op jit(solution)/shard_map/ppermute | solution.py:49
  542.5 46.1 %collective-permute-start.54 = (bf16[4,32,6144]{2,1,0:T(8,128)(2,1)S(1)}, bf16[4,32,6144]{2,1,0:T(8,128)(2,1)S(1)}, u32[]{:S(2)}, u32[]{:S(2)}) collective-permute-start(bf16[4,32,6144]{2,1,0:T(8,128)(2,1)S(1)} %slice.210), channel_id=1, source_target_pairs={{0,2},{1,3},{2,0},{3,1},{4,6},{5,7},{6,4},{7,5},{8,10},{9,11},{10,... | collective-permute-start | bytes 4718600 | tf_op jit(solution)/shard_map/ppermute | solution.py:49
  566.6 20.1 %collective-permute-start.60 = (bf16[4,96,1024]{2,1,0:T(8,128)(2,1)S(1)}, bf16[4,96,1024]{2,1,0:T(8,128)(2,1)S(1)}, u32[]{:S(2)}, u32[]{:S(2)}) collective-permute-start(bf16[4,96,1024]{2,1,0:T(8,128)(2,1)S(1)} %slice.218), channel_id=1, source_target_pairs={{0,2},{1,3},{2,0},{3,1},{4,6},{5,7},{6,4},{7,5},{8,10},{9,11},{10,... | collective-permute-start | bytes 2359304 | tf_op jit(solution)/shard_map/ppermute | solution.py:49
  567.2 78.7 %collective-permute-start.51 = (bf16[32,1024]{1,0:T(8,128)(2,1)S(1)}, bf16[32,1024]{1,0:T(8,128)(2,1)S(1)}, u32[]{:S(2)}, u32[]{:S(2)}) collective-permute-start(bf16[32,1024]{1,0:T(8,128)(2,1)S(1)} %fusion.42), channel_id=1, source_target_pairs={{0,16},{1,17},{2,18},{3,19},{4,20},{5,21},{6,22},{7,23},{8,24},{9,... | collective-permute-start | bytes 196616 | tf_op jit(solution)/shard_map/ppermute | solution.py:56
  567.5 22.2 %collective-permute-start.43 = (bf16[2,32,3072]{2,1,0:T(8,128)(2,1)S(1)}, bf16[2,32,3072]{2,1,0:T(8,128)(2,1)S(1)}, u32[]{:S(2)}, u32[]{:S(2)}) collective-permute-start(bf16[2,32,3072]{2,1,0:T(8,128)(2,1)S(1)} %slice.196), channel_id=1, source_target_pairs={{0,4},{1,5},{2,6},{3,7},{4,0},{5,1},{6,2},{7,3},{8,12},{9,13},{10,... | collective-permute-start | bytes 1179656 | tf_op jit(solution)/shard_map/ppermute | solution.py:49
  587.1 16.2 %collective-permute-start.61 = (bf16[2,96,1024]{2,1,0:T(8,128)(2,1)S(1)}, bf16[2,96,1024]{2,1,0:T(8,128)(2,1)S(1)}, u32[]{:S(2)}, u32[]{:S(2)}) collective-permute-start(bf16[2,96,1024]{2,1,0:T(8,128)(2,1)S(1)} %slice.220), channel_id=1, source_target_pairs={{0,4},{1,5},{2,6},{3,7},{4,0},{5,1},{6,2},{7,3},{8,12},{9,13},{10,... | collective-permute-start | bytes 1179656 | tf_op jit(solution)/shard_map/ppermute | solution.py:49
  589.1 34.7 %collective-permute-start.55 = (bf16[2,32,6144]{2,1,0:T(8,128)(2,1)S(1)}, bf16[2,32,6144]{2,1,0:T(8,128)(2,1)S(1)}, u32[]{:S(2)}, u32[]{:S(2)}) collective-permute-start(bf16[2,32,6144]{2,1,0:T(8,128)(2,1)S(1)} %slice.212), channel_id=1, source_target_pairs={{0,4},{1,5},{2,6},{3,7},{4,0},{5,1},{6,2},{7,3},{8,12},{9,13},{10,... | collective-permute-start | bytes 2359304 | tf_op jit(solution)/shard_map/ppermute | solution.py:49
  589.8 35.9 %collective-permute-start.44 = (bf16[1,32,3072]{2,1,0:T(8,128)(2,1)S(1)}, bf16[1,32,3072]{2,1,0:T(8,128)(2,1)S(1)}, u32[]{:S(2)}, u32[]{:S(2)}) collective-permute-start(bf16[1,32,3072]{2,1,0:T(8,128)(2,1)S(1)} %slice.198), channel_id=1, source_target_pairs={{0,8},{1,9},{2,10},{3,11},{4,12},{5,13},{6,14},{7,15},{8,0},{9,1},... | collective-permute-start | bytes 589832 | tf_op jit(solution)/shard_map/ppermute | solution.py:49
  603.5 40.6 %collective-permute-start.62 = (bf16[1,96,1024]{2,1,0:T(8,128)(2,1)S(1)}, bf16[1,96,1024]{2,1,0:T(8,128)(2,1)S(1)}, u32[]{:S(2)}, u32[]{:S(2)}) collective-permute-start(bf16[1,96,1024]{2,1,0:T(8,128)(2,1)S(1)} %slice.222), channel_id=1, source_target_pairs={{0,8},{1,9},{2,10},{3,11},{4,12},{5,13},{6,14},{7,15},{8,0},{9,1},... | collective-permute-start | bytes 589832 | tf_op jit(solution)/shard_map/ppermute | solution.py:49
  624.0 19.9 %collective-permute-start.56 = (bf16[1,32,6144]{2,1,0:T(8,128)(2,1)S(1)}, bf16[1,32,6144]{2,1,0:T(8,128)(2,1)S(1)}, u32[]{:S(2)}, u32[]{:S(2)}) collective-permute-start(bf16[1,32,6144]{2,1,0:T(8,128)(2,1)S(1)} %slice.214), channel_id=1, source_target_pairs={{0,8},{1,9},{2,10},{3,11},{4,12},{5,13},{6,14},{7,15},{8,0},{9,1},... | collective-permute-start | bytes 1179656 | tf_op jit(solution)/shard_map/ppermute | solution.py:49
  625.8 20.8 %collective-permute-start.45 = (bf16[32,3072]{1,0:T(8,128)(2,1)S(1)}, bf16[32,3072]{1,0:T(8,128)(2,1)S(1)}, u32[]{:S(2)}, u32[]{:S(2)}) collective-permute-start(bf16[32,3072]{1,0:T(8,128)(2,1)S(1)} %fusion.38), channel_id=1, source_target_pairs={{0,16},{1,17},{2,18},{3,19},{4,20},{5,21},{6,22},{7,23},{8,24},{9,... | collective-permute-start | bytes 589832 | tf_op jit(solution)/shard_map/ppermute | solution.py:56
  644.0 6.2 collective-permute-start.57
  644.2 5.2 collective-permute-start.63
  656.1 13.8 %collective-permute-start.65 = (f32[1,128]{1,0:T(1,128)S(1)}, f32[1,128]{1,0:T(1,128)S(1)}, u32[]{:S(2)}, u32[]{:S(2)}) collective-permute-start(f32[1,128]{1,0:T(1,128)S(1)} %broadcast_add_fusion), channel_id=1, source_target_pairs={{0,2},{1,3},{2,0},{3,1},{4,6},{5,7},{6,4},{7,5},{8,10},{9,11},{10,... | collective-permute-start | bytes 1544 | tf_op jit(solution)/shard_map/ppermute | solution.py:49
  673.5 4.4 collective-permute-start.67
  (50 other events, 458.4 us)

commit v2 on v1

v2 whole, which is shorter than its diff:
```python
import functools
import math

import jax
import jax.numpy as jnp
import numpy as np
from jax import lax
from jax.experimental import pallas as pl
from jax.experimental.pallas import tpu as pltpu
from jax.sharding import PartitionSpec as P

FF = 3072
STEP = 10


NORM_EPS = 1e-06
COSINE_EPS = 1e-06
ROPE_BASE = 100.0
CLIP = 1.0
RATE = 0.02
OUTPUT_RATE = 0.2
SCALE_RATE = 8.0
BETA_ONE = 0.9
BETA_TWO = 0.95
ADAM_EPS = 1e-08
DECAY = 0.01
PRECISE = lax.Precision.HIGHEST
AXES = ("dp", "fsdp")
LOW = jnp.bfloat16
WIDE = jnp.float32


ORDERS = (((8, 4, 1, 2), (2, 8, 4, 1)), ((8, 4, 2, 1), (1, 8, 4, 2)))


class Net:
    def __init__(self, size, dp_size):
        self.size = size
        self.dp_size = dp_size
        self.sub = size // 16
        self.core = lax.axis_index("dp")
        self.me = lax.axis_index("fsdp") // self.sub
        self.tables = tuple(self.table(order) for order in ORDERS)

    def exchange(self, array, bits):
        pairs = []
        for core in range(self.dp_size):
            for place in range(self.size):
                target = place ^ (bits[core % 2] * self.sub)
                pairs.append((core * self.size + place, core * self.size + target))
        return lax.ppermute(array, AXES, pairs)

    def cross(self, array, parity, stage):
        order = ORDERS[parity]
        return self.exchange(array, (order[0][stage], order[1][stage]))

    def swap(self, array):
        pairs = []
        for core in range(self.dp_size):
            for place in range(self.size):
                pairs.append((core * self.size + place, (core ^ 1) * self.size + place))
        return lax.ppermute(array, AXES, pairs)

    def table(self, order):
        index = lax.iota(jnp.int32, 32)
        side = self.core ^ (index >> 4)
        value = jnp.full((32,), self.me, jnp.int32)
        for stage in range(4):
            bit = jnp.where(side == 0, order[0][stage], order[1][stage])
            value = value ^ ((index >> stage & 1) * bit)
        return jnp.concatenate([value, self.core[None]]).astype(jnp.int32)

    def groups(self):
        return [list(range(g * self.sub, (g + 1) * self.sub)) for g in range(16)]

    def join_sub(self, shard):
        if self.sub == 1:
            return shard
        return lax.all_gather(shard, "fsdp", axis=0, tiled=True, axis_index_groups=self.groups())

    def split_sub(self, gradient):
        gathered = lax.all_gather(gradient, "fsdp", axis=0, axis_index_groups=self.groups())
        rows = gradient.shape[0] // self.sub
        place = lax.axis_index("fsdp") % self.sub
        return lax.dynamic_slice_in_dim(jnp.sum(gathered, axis=0), place * rows, rows, axis=0)

    def total(self, value):
        for bits in ((1, 2, 3), (4, 8, 12)):
            value = value + sum(self.exchange(value, (bit, bit)) for bit in bits)
        return value + self.swap(value)


class Line:
    def __init__(self):
        self.last = None
        self.waits = []

    def call(self, kernel, args, in_specs, prefetch=0, **kwargs):
        deps = []
        if self.last is not None:
            token = self.last
            if self.waits:
                token = lax.optimization_barrier((token, *self.waits))[0]
            deps = [token]
        self.waits = []
        count = len(deps)
        one = not isinstance(kwargs["out_shape"], (list, tuple))
        shapes = [kwargs["out_shape"]] if one else list(kwargs["out_shape"])
        specs = kwargs["out_specs"]
        specs = [specs] if not isinstance(specs, (list, tuple)) else list(specs)
        place = prefetch + len(in_specs) + len(shapes)

        def body(*refs):
            refs = refs[:prefetch] + refs[prefetch + count :]
            refs[place][...] = jnp.zeros((8, 128), WIDE)
            kernel(*refs[:place], *refs[place + 1 :])

        in_specs = [ANY] * count + list(in_specs)
        out_specs = specs + [whole((8, 128)) if "grid" in kwargs else VMEM]
        del kwargs["out_specs"]
        kwargs["out_shape"] = shapes + [jax.ShapeDtypeStruct((8, 128), WIDE)]
        if prefetch:
            kwargs["grid_spec"] = pltpu.PrefetchScalarGridSpec(
                num_scalar_prefetch=prefetch,
                grid=kwargs.pop("grid"),
                in_specs=in_specs,
                out_specs=out_specs,
                scratch_shapes=kwargs.pop("scratch_shapes", []),
            )
        else:
            kwargs["in_specs"] = in_specs
            kwargs["out_specs"] = out_specs
        *outs, self.last = pl.pallas_call(body, **kwargs)(*args[:prefetch], *deps, *args[prefetch:])
        return outs[0] if one else outs

    def pin(self, array):
        if self.last is not None:
            array, _ = lax.optimization_barrier((array, self.last))
        self.waits.append(array)
        return array


class Gather:
    def __init__(self, net, line, parity, half):
        self.net, self.line, self.parity = net, line, parity
        self.held = line.pin(half)
        self.got = net.cross(self.held, parity, 0)

    def second(self):
        self.held = join(self.line, self.held, self.got)
        self.got = self.net.cross(self.held, self.parity, 1)

    def third(self):
        self.held = join(self.line, self.held, self.got)
        self.near = self.net.cross(self.held, self.parity, 2)
        self.far = self.net.cross(self.held, self.parity, 3)

    def fourth(self):
        self.near = self.line.pin(self.near)
        self.last = self.net.cross(self.near, self.parity, 3)
        self.swapped = [self.net.swap(self.held), self.net.swap(self.near)]

    def fifth(self):
        self.far = self.line.pin(self.far)
        self.swapped.append(self.net.swap(self.far))

    def finish(self):
        self.last = self.line.pin(self.last)
        self.swapped = [self.line.pin(array) for array in self.swapped]
        self.swapped.append(self.net.swap(self.last))
        self.pieces = (self.held, self.near, self.far, self.last, *self.swapped)


class Scatter:
    def __init__(self, net, line, parity, keep, send):
        self.net, self.line, self.parity = net, line, parity
        self.keep, self.send = keep, send
        self.part = [None, None, net.swap(send[2]), net.swap(send[3])]

    def first(self):
        two, three = fold_pair(self.line, self.keep[2:], self.part[2:])
        self.part[1] = self.net.swap(self.line.pin(self.send[1]))
        self.part[0] = self.net.swap(self.line.pin(self.send[0]))
        self.got = self.net.cross(three, self.parity, 3)
        self.late = self.net.cross(two, self.parity, 3)

    def second(self):
        self.part[0] = self.line.pin(self.part[0])
        (held,) = fold(self.line, self.keep[1], (self.part[1], self.got), 1)
        self.got = self.net.cross(held, self.parity, 2)

    def third(self):
        self.held, send = fold(self.line, self.keep[0], (self.part[0], self.late, self.got), 2)
        self.got = self.net.cross(send, self.parity, 1)

    def fourth(self):
        self.held, send = fold(self.line, self.held, (self.got,), 2)
        self.got = self.net.cross(send, self.parity, 0)

    def finish(self):
        self.mine, self.square = fold_last(self.line, self.held[0], self.got[0])
        self.other = self.net.swap(self.mine)


class SmallGather:
    def __init__(self, net, line, rows):
        self.net, self.line = net, line
        self.held = line.pin(rows)
        self.send((1, 2, 3))

    def send(self, bits):
        self.got = [self.net.exchange(self.held, (bit, bit)) for bit in bits]

    def step(self):
        got = [self.line.pin(array) for array in self.got]
        self.held = jnp.concatenate([self.held, *got], axis=0)

    def second(self):
        self.step()
        self.send((4, 8, 12))


ANY = pl.BlockSpec(memory_space=pl.ANY)
SMEM = pl.BlockSpec(memory_space=pltpu.SMEM)
VMEM = pl.BlockSpec(memory_space=pltpu.VMEM)
NT = (((1,), (1,)), ((), ()))
TN = (((0,), (0,)), ((), ()))
VMEM_LIMIT = 56 * 1024 * 1024
SMALL_LIMIT = 16 * 1024 * 1024


def load_weight(table_ref, pieces, full_ref, sems):
    core = table_ref[32]
    rows = pieces[0].shape[1]
    copies = []
    for number, piece in enumerate(pieces):
        side = core if number < 4 else 1 - core
        for index in range(4):
            start = pl.multiple_of(table_ref[number * 4 + index] * (2 * rows) + side * rows, 16)
            copies.append(
                pltpu.make_async_copy(
                    piece.at[index], full_ref.at[pl.ds(start, rows)], sems.at[number, index]
                )
            )
    return copies


def part_of(pieces, first, size):
    return tuple(piece.at[:, :, first : first + size] for piece in pieces)


def fetch(copies):
    for copy in copies:
        copy.start()
    for copy in copies:
        copy.wait()


SEMS = pltpu.SemaphoreType.DMA((8, 4))


def params(dims):
    return pltpu.CompilerParams(
        dimension_semantics=("arbitrary",) * dims, vmem_limit_bytes=VMEM_LIMIT
    )


def cost(flops, size):
    return pl.CostEstimate(flops=flops, bytes_accessed=size, transcendentals=0)


def mul(a, b):
    return jnp.dot(a, b, preferred_element_type=WIDE)


def mul_nt(a, b):
    return lax.dot_general(a, b, NT, preferred_element_type=WIDE)


def mul_tn(a, b):
    return lax.dot_general(a, b, TN, preferred_element_type=WIDE)


def whole(shape):
    return pl.BlockSpec(shape, lambda *_: (0,) * len(shape))


def turned_block(width, seq):
    return pl.BlockSpec((width, seq), lambda i: (0, i))


def turned_shape(width, tokens):
    return jax.ShapeDtypeStruct((width, tokens), LOW)


def grouped(images):
    return 2 if images % 2 == 0 else 1


def scaled(values, scale_ref):
    count = scale_ref.shape[0]
    rows = values.shape[0] // count
    parts = [values[i * rows : i * rows + rows] * scale_ref[i] for i in range(count)]
    return parts[0] if count == 1 else jnp.concatenate(parts, axis=0)


def norm_back(grad, values, scale_ref, dscale_ref):
    inverse = lax.rsqrt(jnp.mean(values * values, axis=-1, keepdims=True) + NORM_EPS)
    normed = values * inverse
    product = grad * normed
    count = scale_ref.shape[0]
    rows = values.shape[0] // count
    for i in range(count):
        dscale_ref[i] = jnp.sum(product[i * rows : i * rows + rows], axis=0, keepdims=True)
    grad = scaled(grad, scale_ref)
    inner = jnp.mean(grad * normed, axis=-1, keepdims=True)
    return inverse * (grad - normed * inner)


def rotate(values, cos_rep, up_rep, down_rep, sign):
    ahead = pltpu.roll(values, values.shape[-1] - 16, 1)
    behind = pltpu.roll(values, 16, 1)
    turned = ahead * up_rep + behind * down_rep
    return values * cos_rep + (turned if sign > 0 else -turned)


def join_kernel(a_ref, b_ref, out_ref, sems):
    count = a_ref.shape[0]
    fetch(
        [
            pltpu.make_async_copy(a_ref, out_ref.at[:count], sems.at[0]),
            pltpu.make_async_copy(b_ref, out_ref.at[count:], sems.at[1]),
        ]
    )


def join(line, a, b):
    shape = (2 * a.shape[0],) + a.shape[1:]
    return line.call(
        join_kernel,
        (a, b),
        [ANY, ANY],
        out_specs=VMEM,
        out_shape=jax.ShapeDtypeStruct(shape, a.dtype),
        scratch_shapes=[pltpu.SemaphoreType.DMA((2,))],
        compiler_params=pltpu.CompilerParams(vmem_limit_bytes=SMALL_LIMIT),
        cost_estimate=cost(0, 4 * math.prod(shape)),
        name="join",
    )


def fold_kernel(count, held_ref, *refs):
    outs = refs[count:]
    total = held_ref[...].astype(WIDE)
    for ref in refs[:count]:
        total += ref[...].astype(WIDE)
    size = outs[0].shape[0]
    for number, out in enumerate(outs):
        out[...] = total[number * size : number * size + size].astype(out.dtype)


def fold(line, held, others, parts):
    shape = (held.shape[0] // parts,) + held.shape[1:]
    return line.call(
        functools.partial(fold_kernel, len(others)),
        (held, *others),
        [VMEM] * (1 + len(others)),
        out_specs=[VMEM] * parts,
        out_shape=[jax.ShapeDtypeStruct(shape, held.dtype)] * parts,
        compiler_params=pltpu.CompilerParams(vmem_limit_bytes=SMALL_LIMIT),
        cost_estimate=cost(0, 2 * math.prod(held.shape) * (2 + len(others))),
        name="fold",
    )


def fold_pair_kernel(a_ref, b_ref, c_ref, d_ref, first_ref, second_ref):
    first_ref[...] = (a_ref[...].astype(WIDE) + c_ref[...].astype(WIDE)).astype(LOW)
    second_ref[...] = (b_ref[...].astype(WIDE) + d_ref[...].astype(WIDE)).astype(LOW)


def fold_pair(line, held, others):
    shape = jax.ShapeDtypeStruct(held[0].shape, LOW)
    return line.call(
        fold_pair_kernel,
        (*held, *others),
        [VMEM] * 4,
        out_specs=[VMEM] * 2,
        out_shape=[shape] * 2,
        compiler_params=pltpu.CompilerParams(vmem_limit_bytes=SMALL_LIMIT),
        cost_estimate=cost(0, 12 * math.prod(shape.shape)),
        name="fold_pair",
    )


def fold_last_kernel(held_ref, other_ref, out_ref, square_ref):
    total = (held_ref[...].astype(WIDE) + other_ref[...].astype(WIDE)).astype(LOW)
    out_ref[...] = total
    total = total.astype(WIDE)
    sums = jnp.sum(jnp.sum(total * total, axis=0, keepdims=True), axis=1, keepdims=True)
    square_ref[...] = jnp.broadcast_to(sums, square_ref.shape)


def fold_last(line, held, other):
    return line.call(
        fold_last_kernel,
        (held, other),
        [VMEM, VMEM],
        out_specs=[VMEM, VMEM],
        out_shape=[jax.ShapeDtypeStruct(held.shape, LOW), jax.ShapeDtypeStruct((1, 128), WIDE)],
        compiler_params=pltpu.CompilerParams(vmem_limit_bytes=SMALL_LIMIT),
        cost_estimate=cost(0, 6 * math.prod(held.shape)),
        name="fold_last",
    )


def head_kernel(core_ref, qkv_ref, out_ref, ada_ref, *outs):
    rows, size = qkv_ref.shape[0], ada_ref.shape[2]
    for number, out in enumerate(outs):
        for block in range(4):
            at = (4 * number + block) * size
            values = qkv_ref[:, at : at + size] if at < qkv_ref.shape[1] else out_ref[:, at - qkv_ref.shape[1] : at - qkv_ref.shape[1] + size]
            out[0, block * rows : block * rows + rows, :] = values.astype(LOW)
        out[0, 4 * rows :, :] = ada_ref[number].astype(LOW)


def head_parts(line, core, qkv, out, ada):
    rows, width = qkv.shape[0] // 2, out.shape[1]
    size = width // 2
    shape = (1, 4 * rows + ada.shape[1], size)
    return line.call(
        head_kernel,
        (core[None], qkv, out, ada),
        [pl.BlockSpec((rows, 3 * width), lambda i, c: (c[0], 0)),
         pl.BlockSpec((rows, width), lambda i, c: (c[0], 0)),
         pl.BlockSpec((2, ada.shape[1], size), lambda i, c: (0, 0, c[0]))],
        prefetch=1,
        grid=(1,),
        out_specs=[whole(shape)] * 2,
        out_shape=[jax.ShapeDtypeStruct(shape, LOW)] * 2,
        compiler_params=params(1),
        cost_estimate=cost(0, 2 << 20),
        name="head_parts",
    )


def load_head(table_ref, pieces, blocks, full_ref, sems, ada_ref=None, ada_sems=None):
    core = table_ref[32]
    size = pieces[0].shape[2]
    ada_rows = 0 if ada_ref is None else ada_ref.shape[0] // 16
    copies = []
    for number, piece in enumerate(pieces):
        side = core if number < 4 else 1 - core
        for index in range(4):
            owner = table_ref[number * 4 + index]
            start = pl.multiple_of(owner * 64 + side * 32, 16)
            for place, block in enumerate(blocks):
                copies.append(
                    pltpu.make_async_copy(
                        piece.at[index, block * 32 : block * 32 + 32],
                        full_ref.at[pl.ds(start, 32), place * size : place * size + size],
                        sems.at[place, number, index],
                    )
                )
            if ada_ref is not None:
                start = pl.multiple_of(owner * ada_rows, 16)
                column = pl.multiple_of(side * size, 128)
                copies.append(
                    pltpu.make_async_copy(
                        piece.at[index, 128 : 128 + ada_rows],
                        ada_ref.at[pl.ds(start, ada_rows), pl.ds(column, size)],
                        ada_sems.at[number, index],
                    )
                )
    return copies


def cut_kernel(core_ref, up_ref, down_ref, *outs):
    width = down_ref.shape[2]
    low = lax.broadcasted_iota(jnp.int32, (up_ref.shape[0], 128), 1) < 64
    for start in range(0, 2 * width, 128):
        first, second, third = (up_ref[:, 3 * start + 128 * i : 3 * start + 128 * i + 128] for i in range(3))
        lanes = slice(start, start + 128)
        outs[0][0, :, lanes] = jnp.where(low, first, second).astype(LOW)
        outs[1][0, :, lanes] = pltpu.roll(jnp.where(low, third, first), 64, 1).astype(LOW)
        outs[2][0, :, lanes] = jnp.where(low, second, third).astype(LOW)
    for part, out in enumerate(outs):
        out[0, :, 2 * width :] = down_ref[part].astype(LOW)


def cut_parts(line, core, up, down):
    rows, columns = up.shape[0] // 2, up.shape[1]
    width = down.shape[2]
    return line.call(
        cut_kernel,
        (core[None], up, down),
        [pl.BlockSpec((rows, columns), lambda i, c: (c[0], 0)),
         pl.BlockSpec((3, rows, width), lambda i, c: (0, c[0], 0))],
        prefetch=1,
        grid=(1,),
        out_specs=[whole((1, rows, 3 * width))] * 3,
        out_shape=[jax.ShapeDtypeStruct((1, rows, 3 * width), LOW)] * 3,
        compiler_params=params(1),
        cost_estimate=cost(0, 4 << 20),
        name="cut",
    )


def load_qkv(even_ref, odd_ref, pieces, w_ref, sems, ada_ref=None, ada_sems=None):
    width = w_ref.shape[0]
    adas = (None, None) if ada_ref is None else (ada_ref.at[0], ada_ref.at[1])
    semaphores = (None, None) if ada_ref is None else (ada_sems.at[0], ada_sems.at[1])
    return load_head(
        even_ref, pieces[:8], (0, 1, 2, 3), w_ref.at[:, : 2 * width], sems.at[0], adas[0], semaphores[0]
    ) + load_head(
        odd_ref, pieces[8:], (0, 1), w_ref.at[:, 2 * width :], sems.at[1], adas[1], semaphores[1]
    )


def front_kernel(group, even_ref, odd_ref, x_ref, cond_ref, *rest):
    pieces, rest = rest[:16], rest[16:]
    sums_ref, spread_ref, root_ref, cos_ref, up_ref, down_ref, *rest = rest
    act_ref, q_ref, k_ref, v_ref, pack_ref, one_ref, two_ref, w_ref, ada_ref, sems, ada_sems = rest

    @pl.when(pl.program_id(0) == 0)
    def _():
        fetch(load_qkv(even_ref, odd_ref, pieces, w_ref, sems, ada_ref, ada_sems))
        for number, out in enumerate((one_ref, two_ref)):
            scale = 1.0 + mul(cond_ref[...], ada_ref[number])
            for image in range(scale.shape[0]):
                out[image] = scale[image : image + 1]

    scale_ref = one_ref.at[pl.ds(pl.program_id(0) * group, group)]
    width = x_ref.shape[1]
    x = x_ref[...].astype(WIDE)
    inverse = lax.rsqrt(jnp.mean(x * x, axis=-1, keepdims=True) + NORM_EPS)
    act = scaled(x * inverse, scale_ref).astype(LOW)
    act_ref[...] = act.T
    v_ref[...] = mul(act, w_ref[:, 2 * width :]).astype(LOW)
    q = mul(act, w_ref[:, :width])
    k = mul(act, w_ref[:, width : 2 * width])
    sums = mul((q * q).astype(LOW), sums_ref[0]) + mul((k * k).astype(LOW), sums_ref[1])
    factor = lax.rsqrt(sums + COSINE_EPS)
    high = factor.astype(LOW)
    low = (factor - high.astype(WIDE)).astype(LOW)
    lane = lax.broadcasted_iota(jnp.int32, factor.shape, 1)
    pack = jnp.where(lane < 32, high.astype(WIDE), jnp.where(lane < 64, low.astype(WIDE), 0.0))
    pack = pack.astype(LOW)
    pack_ref[...] = pack
    q = q * mul(pack, spread_ref[0]) * root_ref[...]
    k = k * mul(pack, spread_ref[1]) * root_ref[...]
    cos_rep, up_rep, down_rep = cos_ref[...], up_ref[...], down_ref[...]
    for pair in range(width // 128):
        lanes = slice(pair * 128, pair * 128 + 128)
        q_ref[:, lanes] = rotate(q[:, lanes], cos_rep, up_rep, down_rep, 1).astype(LOW)
        k_ref[:, lanes] = rotate(k[:, lanes], cos_rep, up_rep, down_rep, 1).astype(LOW)


def front(line, tables, x, cond, pieces, sums, spread, root, turns, images):
    tokens, width = x.shape
    group = grouped(images)
    seq = tokens // images * group
    row = pl.BlockSpec((seq, width), lambda i: (i, 0))
    narrow = pl.BlockSpec((seq, 128), lambda i: (i, 0))
    full = jax.ShapeDtypeStruct((tokens, width), LOW)
    return line.call(
        functools.partial(front_kernel, group),
        (*tables, x, cond, *pieces, sums, spread, root, *turns),
        [SMEM, SMEM, row, whole(cond.shape), *[ANY] * 16,
                  whole(sums.shape), whole(spread.shape), whole(root.shape), narrow, narrow, narrow],
        grid=(images // group,),
        out_specs=[turned_block(width, seq), row, row, row, narrow, whole((images, 1, width)), whole((images, 1, width))],
        out_shape=[turned_shape(width, tokens), full, full, full, jax.ShapeDtypeStruct((tokens, 128), LOW),
                   jax.ShapeDtypeStruct((images, 1, width), WIDE), jax.ShapeDtypeStruct((images, 1, width), WIDE)],
        scratch_shapes=[pltpu.VMEM((width, 3 * width), LOW), pltpu.VMEM((2, cond.shape[1], width), LOW),
                        pltpu.SemaphoreType.DMA((2, 4, 8, 4)), pltpu.SemaphoreType.DMA((2, 8, 4))],
        compiler_params=params(1),
        cost_estimate=cost(6 * tokens * width * width, 20 << 20),
        name="front",
    )


def attend_kernel(q_ref, k_ref, v_ref, valid_ref, o_ref, turned_ref, lse_ref):
    seq, width = q_ref.shape
    valid = valid_ref[...]
    lane = lax.broadcasted_iota(jnp.int32, (seq, 128), 1)
    first = lane < 64
    totals = jnp.zeros((seq, 128), WIDE)
    zero = jnp.zeros((seq, 128), LOW)
    for pair in range(width // 128):
        lanes = slice(pair * 128, pair * 128 + 128)
        q, k = q_ref[:, lanes], k_ref[:, lanes]
        v = v_ref[:, lanes] * valid
        mixed = None
        for half in range(2):
            pick = first if half == 0 else jnp.logical_not(first)
            scores = mul_nt(jnp.where(pick, q, zero), k)
            weights = jnp.exp(scores).astype(LOW)
            right = jnp.concatenate([jnp.where(pick, v, zero), valid], axis=1)
            both = mul(weights, right)
            total = both[:, 128:]
            part = both[:, :128] / total
            mixed = part if mixed is None else mixed + part
            totals = jnp.where(lane == 2 * pair + half, total, totals)
        mixed = mixed.astype(LOW)
        o_ref[:, lanes] = mixed
        turned_ref[lanes, :] = mixed.T
    lane_ok = lane < width // 64
    lse = jnp.log(jnp.where(lane_ok, totals, 1.0))
    lse_ref[0] = lse.T[: width // 64]


def attend(line, q, k, v, valid, images):
    tokens, width = q.shape
    seq = tokens // images
    row = pl.BlockSpec((seq, width), lambda i: (i, 0))
    heads = width // 64
    return line.call(
        attend_kernel,
        (q, k, v, valid),
        [row, row, row, pl.BlockSpec((seq, 128), lambda i: (i, 0))],
        grid=(images,),
        out_specs=[row, turned_block(width, seq), pl.BlockSpec((1, heads, seq), lambda i: (i, 0, 0))],
        out_shape=[jax.ShapeDtypeStruct((tokens, width), LOW), turned_shape(width, tokens),
                   jax.ShapeDtypeStruct((images, heads, seq), WIDE)],
        compiler_params=params(1),
        cost_estimate=cost(16 * tokens * seq * width, 8 << 20),
        name="attend",
    )


def middle_kernel(table_ref, o_ref, x_ref, scale_ref, *rest):
    pieces = rest[:8]
    mid_ref, act_ref, turned_ref, w_ref, sems = rest[8:]

    @pl.when(pl.program_id(0) == 0)
    def _():
        fetch(load_head(table_ref, pieces, (2, 3), w_ref, sems))

    mid = x_ref[...].astype(WIDE) + mul(o_ref[...], w_ref[...])
    mid_ref[...] = mid
    inverse = lax.rsqrt(jnp.mean(mid * mid, axis=-1, keepdims=True) + NORM_EPS)
    act = scaled(mid * inverse, scale_ref).astype(LOW)
    act_ref[...] = act
    turned_ref[...] = act.T


def middle_block(line, table, o, x, scale, pieces, images):
    tokens, width = x.shape
    group = grouped(images)
    seq = tokens // images * group
    row = pl.BlockSpec((seq, width), lambda i: (i, 0))
    return line.call(
        middle_kernel,
        (table, o, x, scale, *pieces),
        [SMEM, row, row, pl.BlockSpec((group, 1, width), lambda i: (i, 0, 0))] + [ANY] * 8,
        grid=(images // group,),
        out_specs=[row, row, turned_block(width, seq)],
        out_shape=[jax.ShapeDtypeStruct((tokens, width), WIDE), jax.ShapeDtypeStruct((tokens, width), LOW),
                   turned_shape(width, tokens)],
        scratch_shapes=[pltpu.VMEM((width, width), LOW), pltpu.SemaphoreType.DMA((2, 8, 4))],
        compiler_params=params(1),
        cost_estimate=cost(2 * tokens * width * width, 12 << 20),
        name="middle",
    )


def part_kernel(first, last, table_ref, act_ref, dy_ref, *rest):
    rest = list(rest)
    pieces = tuple(rest.pop(0) for _ in range(8))
    if last:
        mid_ref, scale_ref = rest.pop(0), rest.pop(0)
        out_pieces = tuple(rest.pop(0) for _ in range(8))
    acc_ref = None if first else rest.pop(0)
    hid_ref, dgu_ref, turned_ref = rest.pop(0), rest.pop(0), rest.pop(0)
    if last:
        dmid_ref, db_ref, do_ref, dscale_ref = (rest.pop(0) for _ in range(4))
    else:
        da_ref = rest.pop(0)
    w_ref, sems = rest.pop(0), rest.pop(0)
    if last:
        out_ref, sems_out = rest.pop(0), rest.pop(0)

    @pl.when(pl.program_id(0) == 0)
    def _():
        copies = load_weight(table_ref, pieces, w_ref, sems)
        if last:
            copies = copies + load_head(table_ref, out_pieces, (2, 3), out_ref, sems_out)
        fetch(copies)

    width = act_ref.shape[1]
    act, dy = act_ref[...], dy_ref[...]
    size = 512
    for start in range(0, width, size):
        cols = slice(start, start + size)
        above = slice(width + start, width + start + size)
        gate = mul(act, w_ref[:, cols])
        upper = mul(act, w_ref[:, above])
        grad = mul_nt(dy, w_ref[start : start + size, 2 * width :]).astype(LOW).astype(WIDE)
        cdf = 0.5 * (1.0 + lax.erf(gate * math.sqrt(0.5)))
        bell = jnp.exp(-0.5 * gate * gate) * (1.0 / math.sqrt(2.0 * math.pi))
        gelu = gate * cdf
        hid = (gelu * upper).astype(LOW)
        hid_ref[:, cols] = hid
        turned_ref[cols, :] = hid.T
        dgu_ref[:, cols] = (grad * upper * (cdf + gate * bell)).astype(LOW)
        dgu_ref[:, above] = (grad * gelu).astype(LOW)
    total = mul_nt(dgu_ref[:, :width], w_ref[:, :width])
    total += mul_nt(dgu_ref[:, width:], w_ref[:, width : 2 * width])
    if not first:
        total += acc_ref[...]
    if not last:
        da_ref[...] = total
        return
    dmid = dy.astype(WIDE) + norm_back(total, mid_ref[...], scale_ref, dscale_ref)
    dmid_ref[...] = dmid
    low = dmid.astype(LOW)
    db_ref[...] = low
    do_ref[...] = mul_nt(low, out_ref[...]).astype(LOW)


def geglu_part(line, table, act, dy, pieces, images, acc=None, final=None):
    tokens, width = act.shape
    group = grouped(images)
    seq = tokens // images * group
    first, last = acc is None, final is not None
    row = pl.BlockSpec((seq, width), lambda i: (i, 0))
    one = pl.BlockSpec((group, 1, width), lambda i: (i, 0, 0))
    args = [table, act, dy, *pieces]
    in_specs = [SMEM, row, row] + [ANY] * 8
    if last:
        mid, scale, out_pieces = final
        args += [mid, scale, *out_pieces]
        in_specs += [row, one] + [ANY] * 8
    if not first:
        args.append(acc)
        in_specs.append(row)
    low = jax.ShapeDtypeStruct((tokens, width), LOW)
    wide = jax.ShapeDtypeStruct((tokens, width), WIDE)
    out_specs = [row, pl.BlockSpec((seq, 2 * width), lambda i: (i, 0)), turned_block(width, seq)]
    out_shape = [low, jax.ShapeDtypeStruct((tokens, 2 * width), LOW), turned_shape(width, tokens)]
    scratch = [pltpu.VMEM((width, 3 * width), LOW), SEMS]
    if last:
        out_specs += [row, row, row, one]
        out_shape += [wide, low, low, jax.ShapeDtypeStruct((images, 1, width), WIDE)]
        scratch += [pltpu.VMEM((width, width), LOW), pltpu.SemaphoreType.DMA((2, 8, 4))]
    else:
        out_specs.append(row)
        out_shape.append(wide)
    return line.call(
        functools.partial(part_kernel, first, last),
        args,
        in_specs,
        grid=(images // group,),
        out_specs=out_specs,
        out_shape=out_shape,
        scratch_shapes=scratch,
        compiler_params=params(1),
        cost_estimate=cost((12 if last else 10) * tokens * width * width, 30 << 20),
        name="geglu_part",
    )


def attend_back_kernel(q_ref, k_ref, v_ref, o_ref, do_ref, lse_ref, valid_ref, pack_ref, spread_ref,
                       root_ref, pick_ref, block_ref, cos_ref, up_ref, down_ref, dproj_ref, dhead_ref):
    seq, width = q_ref.shape
    valid = valid_ref[...]
    valid_wide = valid.astype(WIDE)
    first = lax.broadcasted_iota(jnp.int32, (seq, 128), 1) < 64
    zero = jnp.zeros((seq, 128), LOW)
    cos_rep, up_rep, down_rep = cos_ref[...], up_ref[...], down_ref[...]
    product = (do_ref[...].astype(WIDE) * o_ref[...].astype(WIDE)).astype(LOW)
    delta = mul_nt(pick_ref[...], product)
    pack = pack_ref[...]
    block = block_ref[...]
    for pair in range(width // 128):
        lanes = slice(pair * 128, pair * 128 + 128)
        q, k, v, do = q_ref[:, lanes], k_ref[:, lanes], v_ref[:, lanes], do_ref[:, lanes]
        k_turned = (k * valid).T
        dv = dk = None
        dq_parts = []
        for half in range(2):
            head = 2 * pair + half
            pick = first if half == 0 else jnp.logical_not(first)
            q_one = jnp.where(pick, q, zero)
            do_one = jnp.where(pick, do, zero)
            weights = jnp.exp(mul_nt(k, q_one) - lse_ref[0, head : head + 1, :])
            grads = mul_nt(v, do_one)
            dscore = (weights * (grads - delta[head : head + 1, :])).astype(LOW)
            part_v = mul(weights.astype(LOW), do_one)
            part_k = mul(dscore, q_one)
            dv = part_v if dv is None else dv + part_v
            dk = part_k if dk is None else dk + part_k
            dq_parts.append(mul(k_turned[half * 64 : half * 64 + 64], dscore))
        dq = jnp.concatenate(dq_parts, axis=0).T
        dk = dk * valid_wide
        root = root_ref[:, lanes]
        for side, (grad, value) in enumerate(((dq, q), (dk, k))):
            value = value.astype(WIDE)
            inner = mul((grad * value).astype(LOW), block)
            total = jnp.sum(inner, axis=0, keepdims=True)
            if side == 0:
                head_total = total
            else:
                dhead_ref[0, :, lanes] = head_total + total
            factor = mul(pack, spread_ref[side, :, lanes])
            back = factor * (root * grad - value * (inner / root))
            back = rotate(back, cos_rep, up_rep, down_rep, -1)
            dproj_ref[:, side * width + pair * 128 : side * width + pair * 128 + 128] = back.astype(LOW)
        dproj_ref[:, 2 * width + pair * 128 : 2 * width + pair * 128 + 128] = (dv * valid_wide).astype(LOW)


def attend_back(line, q, k, v, o, do, lse, valid, pack, spread, root, pick, block, turns, images):
    tokens, width = q.shape
    seq = tokens // images
    heads = width // 64
    row = pl.BlockSpec((seq, width), lambda i: (i, 0))
    narrow = pl.BlockSpec((seq, 128), lambda i: (i, 0))
    return line.call(
        attend_back_kernel,
        (q, k, v, o, do, lse, valid, pack, spread, root, pick, block, *turns),
        [row, row, row, row, row, pl.BlockSpec((1, heads, seq), lambda i: (i, 0, 0)), narrow, narrow,
                  whole(spread.shape), whole(root.shape), whole(pick.shape), whole(block.shape),
                  narrow, narrow, narrow],
        grid=(images,),
        out_specs=[pl.BlockSpec((seq, 3 * width), lambda i: (i, 0)),
                   pl.BlockSpec((1, 1, width), lambda i: (i, 0, 0))],
        out_shape=[jax.ShapeDtypeStruct((tokens, 3 * width), LOW),
                   jax.ShapeDtypeStruct((images, 1, width), WIDE)],
        compiler_params=params(1),
        cost_estimate=cost(40 * tokens * seq * width, 20 << 20),
        name="attend_back",
    )


def input_kernel(even_ref, odd_ref, dproj_ref, x_ref, dmid_ref, scale_ref, *rest):
    pieces = rest[:16]
    out_ref, dscale_ref, w_ref, sems = rest[16:]

    @pl.when(pl.program_id(0) == 0)
    def _():
        fetch(load_qkv(even_ref, odd_ref, pieces, w_ref, sems))

    width = x_ref.shape[1]
    grad = mul_nt(dproj_ref[:, :width], w_ref[:, :width])
    grad += mul_nt(dproj_ref[:, width : 2 * width], w_ref[:, width : 2 * width])
    grad += mul_nt(dproj_ref[:, 2 * width :], w_ref[:, 2 * width :])
    x = x_ref[...].astype(WIDE)
    out_ref[...] = (dmid_ref[...] + norm_back(grad, x, scale_ref, dscale_ref)).astype(LOW)


def input_block(line, tables, dproj, x, dmid, scale, pieces, images):
    tokens, width = x.shape
    group = grouped(images)
    seq = tokens // images * group
    row = pl.BlockSpec((seq, width), lambda i: (i, 0))
    one = pl.BlockSpec((group, 1, width), lambda i: (i, 0, 0))
    return line.call(
        input_kernel,
        (*tables, dproj, x, dmid, scale, *pieces),
        [SMEM, SMEM, pl.BlockSpec((seq, 3 * width), lambda i: (i, 0)), row, row, one] + [ANY] * 16,
        grid=(images // group,),
        out_specs=[row, one],
        out_shape=[jax.ShapeDtypeStruct((tokens, width), LOW), jax.ShapeDtypeStruct((images, 1, width), WIDE)],
        scratch_shapes=[pltpu.VMEM((width, 3 * width), LOW), pltpu.SemaphoreType.DMA((2, 4, 8, 4))],
        compiler_params=params(1),
        cost_estimate=cost(6 * tokens * width * width, 24 << 20),
        name="input_grad",
    )


def result_kernel(even_ref, odd_ref, h0, h1, h2, mid_ref, *rest):
    pieces, out_ref, w_ref, sems = rest[:24], rest[24], rest[25], rest[26]
    width = mid_ref.shape[1]

    @pl.when(pl.program_id(0) == 0)
    def _():
        copies = []
        for part in range(3):
            ref = pieces[8 * part : 8 * part + 8]
            down = tuple(piece.at[:, :, 2 * width : 3 * width] for piece in ref)
            table_ref = odd_ref if part % 2 == 0 else even_ref
            copies += load_weight(table_ref, down, w_ref.at[part], sems.at[part])
        fetch(copies)

    total = mid_ref[...]
    for part, hid_ref in enumerate((h0, h1, h2)):
        total += mul(hid_ref[...], w_ref[part])
    out_ref[...] = total.astype(LOW)


def result_block(line, tables, hids, mid, pieces, images, place, places):
    tokens, width = mid.shape
    group = grouped(images)
    seq = tokens // images * group
    steps = images // group // places
    row = pl.BlockSpec((seq, width), lambda i: (place * steps + i, 0))
    return line.call(
        result_kernel,
        (*tables, *hids, mid, *[piece for part in pieces for piece in part]),
        [SMEM, SMEM, row, row, row, row] + [ANY] * 24,
        grid=(steps,),
        out_specs=pl.BlockSpec((seq, width), lambda i: (i, 0)),
        out_shape=jax.ShapeDtypeStruct((tokens // places, width), LOW),
        scratch_shapes=[pltpu.VMEM((3, width, width), LOW), pltpu.SemaphoreType.DMA((3, 8, 4))],
        compiler_params=params(1),
        cost_estimate=cost(6 * tokens * width * width, 20 << 20),
        name="result",
    )


def weight_kernel(lefts, table_ref, *refs):
    refs = list(refs)
    acts = [refs.pop(0) for _ in range(max(lefts) + 1)]
    grads = [refs.pop(0) for _ in lefts]
    outs = [refs.pop(0) for _ in range(8)]
    turned_ref, sems = refs
    rows = outs[0].shape[1]
    half = outs[0].shape[2]
    depth = turned_ref.shape[1]
    core = table_ref[32]
    step = pl.program_id(0)

    def copy(number, index):
        start = pl.multiple_of(index * 4 * rows, 16)
        return pltpu.make_async_copy(
            acts[number].at[pl.ds(start, 4 * rows)],
            turned_ref.at[number, index * 4 * rows : index * 4 * rows + 4 * rows],
            sems.at[number, index],
        )

    @pl.when(step == 0)
    def _():
        for number in range(len(acts)):
            for index in range(4):
                copy(number, index).start()

    for span, (left, grad_ref) in enumerate(zip(lefts, grads)):
        @pl.when(step == span)
        def _(span=span, left=left, grad_ref=grad_ref):
            if left not in lefts[:span]:
                for index in range(4):
                    copy(left, index).wait()
            for side in range(2):
                place = pl.multiple_of((core if side == 0 else 1 - core) * half, half)
                grad = grad_ref[:, pl.ds(place, half)]
                for piece in range(4):
                    parts = []
                    for index in range(4):
                        start = table_ref[side * 16 + piece * 4 + index] * rows
                        parts.append(turned_ref[left, pl.ds(pl.multiple_of(start, 16), rows), :])
                    total = mul(jnp.concatenate(parts, axis=0), grad)
                    out = outs[4 * side + piece]
                    out[...] = total.reshape(out.shape).astype(LOW)


def weight_halves(line, table, acts, spans):
    depth, tokens = acts[0].shape
    rows = depth // 16
    wide = spans[0][1].shape[1] // spans[0][3]
    half = wide // 2
    count = len(spans)

    def grad_spec(number, span):
        return pl.BlockSpec((tokens, wide), lambda m, t: (0, span))

    tile = pl.BlockSpec((4, rows, half), lambda m, t: (0, 0, m))
    shape = jax.ShapeDtypeStruct((4, rows, count * half), LOW)
    size = 2 * (tokens * (len(acts) * depth + count * wide) + depth * count * wide)
    outs = line.call(
        functools.partial(weight_kernel, [span[0] for span in spans]),
        (table, *acts, *[span[1] for span in spans]),
        [ANY for _ in acts] + [grad_spec(number, span[2]) for number, span in enumerate(spans)],
        prefetch=1,
        grid=(count,),
        out_specs=[tile] * 8,
        out_shape=[shape] * 8,
        scratch_shapes=[
            pltpu.VMEM((len(acts), depth, tokens), LOW), pltpu.SemaphoreType.DMA((len(acts), 4))
        ],
        compiler_params=params(1),
        cost_estimate=cost(2 * tokens * depth * count * wide, size),
        name="weight_grad",
    )
    return outs[:4], outs[4:]


def adam(weight, first, second, gradient, factor, rate, decay):
    clipped = gradient * factor
    new_first = BETA_ONE * first + (1.0 - BETA_ONE) * clipped
    new_second = BETA_TWO * second + (1.0 - BETA_TWO) * clipped * clipped
    denominator = jnp.sqrt(new_second / (1.0 - BETA_TWO**STEP)) + ADAM_EPS
    new_weight = (
        weight * (1.0 - rate * decay) - rate * (new_first / (1.0 - BETA_ONE**STEP)) / denominator
    )
    return (new_weight, new_first, new_second)


def adam_kernel(core_ref, total_ref, *refs):
    refs = list(refs)
    ada, qkv, out, up, down, scale = ([refs.pop(0) for _ in range(3)] for _ in range(6))
    ada_grad, head_grad = refs.pop(0), refs.pop(0)
    mines = [refs.pop(0) for _ in range(4)]
    others = [refs.pop(0) for _ in range(4)]
    norm_ref = refs.pop(0)
    new_ada, new_qkv, new_out, new_up, new_down, new_scale = ([refs.pop(0) for _ in range(3)] for _ in range(6))
    own_first = core_ref[0] == 0
    head = head_grad[...]
    total = total_ref[0:1, 0:1] + jnp.sum(head * head, axis=1, keepdims=True)
    norm = jnp.sqrt(total)
    factor = jnp.minimum(1.0, CLIP / (norm + 1e-06))

    def update(news, olds, at, gradient, rate, decay):
        weight, first, second = (ref[at] for ref in olds)
        for ref, value in zip(news, adam(weight, first, second, gradient, factor, rate, decay)):
            ref[at] = value

    @pl.when(pl.program_id(0) == 0)
    def _():
        norm_ref[...] = jnp.broadcast_to(norm, norm_ref.shape)
        update(new_scale, scale, (slice(None),) * 2, head, SCALE_RATE, 0.0)
        for index in range(ada_grad.shape[0]):
            update(new_ada, ada, (index,), ada_grad[index], RATE, DECAY)

    def columns(number, span):
        size = mines[0].shape[1] // 3
        mine = mines[number][:, span * size : span * size + size].astype(WIDE)
        other = others[number][:, span * size : span * size + size].astype(WIDE)
        return jnp.where(own_first, mine, other), jnp.where(own_first, other, mine)

    def by_halves(news, olds, number, spans, rate):
        for place, span in enumerate(spans):
            for half, gradient in enumerate(columns(number, span)):
                size = gradient.shape[1]
                start = (2 * place + half) * size
                update(news, olds, (slice(None), slice(start, start + size)), gradient, rate, DECAY)

    by_halves(new_qkv, qkv, 3, (0, 1, 2), RATE)
    by_halves(new_out, out, 2, (3,), OUTPUT_RATE)
    for part in range(3):
        for half, gradient in enumerate(columns(part, 2)):
            size = gradient.shape[1]
            update(new_down, down, (part, slice(None), slice(half * size, half * size + size)), gradient, RATE, DECAY)
    low = lax.broadcasted_iota(jnp.int32, (up[0].shape[0], 128), 1) < 64
    for span in range(2):
        parts = [columns(part, span) for part in range(3)]
        size = parts[0][0].shape[1]
        for half in range(2):
            for lane in range(0, size, 128):
                one, two, three = (parts[part][half][:, lane : lane + 128] for part in range(3))
                turned = pltpu.roll(two, 64, 1)
                start = 3 * ((2 * span + half) * size + lane)
                pieces = (jnp.where(low, one, turned), jnp.where(low, three, one), jnp.where(low, turned, three))
                for number, gradient in enumerate(pieces):
                    at = (slice(None), slice(start + 128 * number, start + 128 * number + 128))
                    update(new_up, up, at, gradient, RATE, DECAY)


def adam_all(line, core, total, ada, qkv, out, up, down, scale, ada_grad, head_grad, mines, others):
    steps = 4
    args = [core[None], total]
    in_specs = [SMEM, whole(total.shape)]
    out_specs = [whole(total.shape)]
    out_shape = [jax.ShapeDtypeStruct(total.shape, WIDE)]

    def by_rows(array):
        shape = array.shape[:-2] + (array.shape[-2] // steps, array.shape[-1])
        lead = (0,) * (array.ndim - 2)
        return pl.BlockSpec(shape, lambda i: lead + (i, 0))

    for group, cut in ((ada, False), (qkv, True), (out, True), (up, True), (down, True), (scale, False)):
        for array in group:
            spec = by_rows(array) if cut else whole(array.shape)
            args.append(array)
            in_specs.append(spec)
            out_specs.append(spec)
            out_shape.append(jax.ShapeDtypeStruct(array.shape, WIDE))
    args += [ada_grad, head_grad, *mines, *others]
    in_specs += [whole(ada_grad.shape), whole(head_grad.shape)] + [by_rows(m) for m in (*mines, *others)]
    return line.call(
        adam_kernel,
        args,
        in_specs,
        grid=(steps,),
        out_specs=out_specs,
        out_shape=out_shape,
        compiler_params=params(1),
        cost_estimate=cost(0, 30 << 20),
        name="adamw",
    )


def turn_kernel(shapes_ref, rates_ref, cos_ref, up_ref, down_ref, valid_ref):
    image = pl.program_id(0)
    height, width = shapes_ref[image, 0], shapes_ref[image, 1]
    shape = cos_ref.shape
    slot = lax.broadcasted_iota(jnp.int32, shape, 0)
    place = slot.astype(WIDE)
    wide = width.astype(WIDE)
    row = jnp.floor((place + 0.5) / wide)
    angle = row * rates_ref[0:1, :] + (place - row * wide) * rates_ref[1:2, :]
    lane = lax.broadcasted_iota(jnp.int32, shape, 1) % 64
    cosine, sine = jnp.cos(angle), jnp.sin(angle)
    cos_ref[...] = jnp.where(lane < 32, cosine, 1.0)
    up_ref[...] = jnp.where(lane < 16, -sine, 0.0)
    down_ref[...] = jnp.where((lane >= 16) & (lane < 32), sine, 0.0)
    valid_ref[...] = jnp.where(slot < height * width, 1.0, 0.0).astype(LOW)


def turn_tables(line, shapes, seq_len, head_dim):
    images = shapes.shape[0]
    count = head_dim // 8
    frequency = ROPE_BASE ** (-jnp.arange(count, dtype=WIDE) / count)
    none = jnp.zeros((count,), WIDE)
    blank = jnp.zeros((head_dim // 2,), WIDE)
    rates = jnp.stack(
        [
            jnp.concatenate([frequency, none, frequency, none, blank] * 2),
            jnp.concatenate([none, frequency, none, frequency, blank] * 2),
        ]
    )
    block = pl.BlockSpec((seq_len, 128), lambda i: (i, 0))
    wide = jax.ShapeDtypeStruct((images * seq_len, 128), WIDE)
    *turns, valid = line.call(
        turn_kernel,
        (shapes, rates),
        [SMEM, whole(rates.shape)],
        grid=(images,),
        out_specs=[block] * 4,
        out_shape=[wide, wide, wide, jax.ShapeDtypeStruct(wide.shape, LOW)],
        compiler_params=params(1),
        cost_estimate=cost(0, 2 << 20),
        name="turns",
    )
    return tuple(turns), valid


def head_matrices(width, head_dim):
    heads = width // head_dim
    owner = np.arange(width) // head_dim
    sums = np.zeros((2, width, 128), np.float32)
    spread = np.zeros((2, 128, width), np.float32)
    for side in range(2):
        for copy in range(2):
            sums[side, np.arange(width), side * heads + copy * 2 * heads + owner] = 1.0
            spread[side, side * heads + copy * 2 * heads + owner, np.arange(width)] = 1.0
    pick = np.zeros((heads, width), np.float32)
    pick[owner, np.arange(width)] = 1.0
    block = np.kron(np.eye(128 // head_dim), np.ones((head_dim, head_dim)))
    return tuple(jnp.asarray(m, LOW) for m in (sums, spread, pick, block))


def finish_wide(net, ada, qkv, out, up, down, scale, grad_ada, head_grad, mines, others):
    def columns(number, span):
        size = mines[0].shape[1] // 3
        mine = mines[number][:, span * size : span * size + size]
        other = others[number][:, span * size : span * size + size]
        pair = [jnp.where(net.core == 0, mine, other), jnp.where(net.core == 0, other, mine)]
        return jnp.concatenate(pair, axis=1).astype(WIDE)

    grad_up = [
        jnp.concatenate([columns(part, span) for span in range(2)], axis=1).reshape(-1, 2, 16, 64)
        for part in range(3)
    ]
    gradients = [
        jnp.concatenate([columns(3, span) for span in range(3)], axis=1),
        columns(2, 3),
        jnp.stack(grad_up, axis=3).reshape(-1, up[0].shape[1]),
        jnp.concatenate([columns(part, 2) for part in range(3)], axis=0),
    ]
    gradients = [grad_ada] + [net.split_sub(gradient) for gradient in gradients]
    total = lax.psum(sum(jnp.sum(gradient * gradient) for gradient in gradients), "fsdp")
    head_grad = head_grad[0]
    norm = jnp.sqrt(total + jnp.sum(head_grad * head_grad))
    factor = jnp.minimum(1.0, CLIP / (norm + 1e-06))
    rates = (RATE, RATE, OUTPUT_RATE, RATE, RATE)
    news = [norm]
    for group, gradient, rate in zip((ada, qkv, out, up, down), gradients, rates):
        news += adam(*group, gradient, factor, rate, DECAY)
    news += adam(*scale, head_grad, factor, SCALE_RATE, 0.0)
    return tuple(news)


def local(
    tokens,
    condition,
    shapes,
    cotangent,
    ada_weight,
    ada_first,
    ada_second,
    qkv_weight,
    qkv_first,
    qkv_second,
    out_weight,
    out_first,
    out_second,
    up_weight,
    up_first,
    up_second,
    down_weight,
    down_first,
    down_second,
    head_scale,
    scale_first,
    scale_second,
    *,
    dp_size,
    fsdp_size,
):
    net = Net(fsdp_size, dp_size)
    line = Line()
    core = net.core
    images = shapes.shape[0]
    width = tokens.shape[1]
    seq_len = tokens.shape[0] // images
    head_count = head_scale.shape[0]
    head_dim = width // head_count
    small = net.sub == 1
    even, odd = net.tables

    ada_joined = net.join_sub(ada_weight.transpose(1, 0, 2)).transpose(1, 0, 2) if net.sub > 1 else ada_weight
    half_qk, half_vo = head_parts(
        line, core, net.join_sub(qkv_weight), net.join_sub(out_weight), ada_joined
    )
    get_qk = Gather(net, line, 0, half_qk)
    get_vo = Gather(net, line, 1, half_vo)
    down_joined = net.join_sub(down_weight).reshape(3, -1, width)
    halves = cut_parts(line, core, net.join_sub(up_weight), down_joined)
    turns, valid = turn_tables(line, shapes, seq_len, head_dim)
    sums, spread, pick, block = head_matrices(width, head_dim)
    root = jnp.repeat(jnp.sqrt(head_scale), head_dim)[None]

    get_qk.second()
    get_vo.second()
    get_qk.third()
    get_vo.third()
    get_mlp = [Gather(net, line, 1, halves[0])]
    get_qk.fourth()
    get_qk.fifth()
    get_mlp[0].second()
    get_vo.fourth()
    get_vo.fifth()
    get_qk.finish()
    get_mlp[0].third()
    get_vo.finish()
    get_mlp.append(Gather(net, line, 0, halves[1]))

    qkv_pieces = get_qk.pieces + get_vo.pieces
    act_one, q, k, v, pack, scale_one, scale_two = front(
        line, net.tables, tokens, condition, qkv_pieces, sums, spread, root, turns, images
    )
    get_mlp[0].fourth()
    get_mlp[0].fifth()
    get_mlp[1].second()
    o, o_turned, lse = attend(line, q, k, v, valid, images)
    get_mlp[0].finish()
    get_mlp[1].third()
    get_mlp.append(Gather(net, line, 1, halves[2]))
    mid, act_two, act_two_turned = middle_block(
        line, odd, o, tokens, scale_two, get_vo.pieces, images
    )
    get_mlp[1].fourth()
    get_mlp[1].fifth()
    get_mlp[2].second()

    def put(parity, acts, spans):
        return Scatter(net, line, parity, *weight_halves(line, net.tables[parity], acts, spans))

    def mlp_spans(hid_turned, dgu):
        return ((act_two_turned, hid_turned), ((0, dgu, 0, 2), (0, dgu, 1, 2), (1, cotangent, 0, 1)))

    hid0, dgu0, turned0, acc = geglu_part(line, odd, act_two, cotangent, get_mlp[0].pieces, images)
    get_mlp[1].finish()
    get_mlp[2].third()
    put0 = put(0, *mlp_spans(turned0, dgu0))
    hid1, dgu1, turned1, acc = geglu_part(
        line, even, act_two, cotangent, get_mlp[1].pieces, images, acc
    )
    get_mlp[2].fourth()
    get_mlp[2].fifth()
    put0.first()
    put1 = put(1, *mlp_spans(turned1, dgu1))
    get_mlp[2].finish()
    put0.second()
    hid2, dgu2, turned2, dmid, db, do, dscale_two = geglu_part(
        line, odd, act_two, cotangent, get_mlp[2].pieces, images, acc,
        (mid, scale_two, get_vo.pieces),
    )
    put0.third()
    put1.first()
    acts2, spans2 = mlp_spans(turned2, dgu2)
    put2 = put(0, acts2 + (o_turned,), spans2 + ((2, db, 0, 1),))
    put0.fourth()
    put1.second()
    dproj, dhead = attend_back(
        line, q, k, v, o, do, lse, valid, pack, spread, root, pick, block, turns, images
    )
    put0.finish()
    put1.third()
    put2.first()
    put_qkv = put(1, (act_one,), tuple((0, dproj, span, 3) for span in range(3)))
    put1.fourth()
    put2.second()

    def result(place):
        return result_block(
            line, net.tables, (hid0, hid1, hid2), mid, [get.pieces for get in get_mlp], images,
            place, places,
        )

    places = 2 if images % (2 * grouped(images)) == 0 else 1
    outputs = [result(0)]
    put1.finish()
    put_qkv.first()
    put2.third()
    input_grad, dscale_one = input_block(
        line, net.tables, dproj, tokens, dmid, scale_one, qkv_pieces, images
    )
    put_qkv.second()
    put2.fourth()

    dhead = jnp.sum(dhead.reshape(images, head_count, head_dim)[:, :, 0], axis=0) / (2.0 * head_scale)
    rows = jnp.concatenate([dscale_one[:, 0], dscale_two[:, 0], condition.astype(WIDE)], axis=1)
    if small:
        dhead = jnp.pad(dhead[None], ((0, 7), (0, 128 - head_count)))
        rows = jnp.concatenate([rows.reshape(1, -1, 128), dhead[None]], axis=1)
        late = SmallGather(net, line, rows)
    if places > 1:
        outputs.append(result(1))
    block_output = jnp.concatenate(outputs, axis=0)
    if small:
        late.second()
        put_qkv.third()
        put2.finish()
        late.step()
        rows = late.held[:, :-8].reshape(16 * images, -1)
        head_grad = jnp.sum(late.held[:, -8, :head_count], axis=0)
    else:
        put_qkv.third()
        put2.finish()
        rows = lax.all_gather(rows, "fsdp", axis=0, tiled=True)
        head_grad = lax.psum(dhead, "fsdp")
    own_rows = ada_weight.shape[1]
    own_start = 2 * width + lax.axis_index("fsdp") * own_rows
    cond_own = lax.dynamic_slice_in_dim(rows, own_start, own_rows, axis=1)
    grad_ada = jnp.dot(cond_own.T, rows[:, : 2 * width], precision=PRECISE)
    head_grad = jnp.pad(head_grad, (0, width - head_count))[None]
    grad_small = jnp.concatenate([grad_ada.reshape(-1, width), head_grad])
    grad_small = grad_small + net.swap(grad_small)
    grad_ada = grad_small[:-1].reshape(own_rows, 2, width).transpose(1, 0, 2)
    head_grad = grad_small[-1:, :head_count]

    put_qkv.fourth()
    put_qkv.finish()
    puts = (put0, put1, put2, put_qkv)
    mines = tuple(each.mine for each in puts)
    others = tuple(each.other for each in puts)
    ada = (ada_weight, ada_first, ada_second)
    qkv = (qkv_weight, qkv_first, qkv_second)
    out = (out_weight, out_first, out_second)
    up = (up_weight, up_first, up_second)
    down = (down_weight, down_first, down_second)
    scale = (head_scale, scale_first, scale_second)
    if not small:
        return (block_output, input_grad) + finish_wide(
            net, ada, qkv, out, up, down, scale, grad_ada, head_grad, mines, others
        )
    local_squares = sum(each.square for each in puts) + 0.5 * jnp.sum(grad_ada * grad_ada)
    total = net.total(local_squares)
    rows = down_weight.shape[0] // 3
    news = adam_all(
        line, core, total, ada, qkv, out, up,
        tuple(array.reshape(3, rows, width) for array in down),
        tuple(array[None] for array in scale), grad_ada, head_grad, mines, others,
    )
    return (
        block_output,
        input_grad,
        news[0][0, 0],
        *news[1:13],
        *[array.reshape(down_weight.shape) for array in news[13:16]],
        *[array[0] for array in news[16:19]],
    )


def solution(mesh):
    tokens = P(("dp", "fsdp"), None)
    ada = P(None, "fsdp", None)
    rows = P("fsdp", None)
    return jax.shard_map(
        functools.partial(local, dp_size=mesh.shape["dp"], fsdp_size=mesh.shape["fsdp"]),
        mesh=mesh,
        in_specs=(tokens,) * 4 + (ada,) * 3 + (rows,) * 12 + (P(),) * 3,
        out_specs=(tokens, tokens, P()) + (ada,) * 3 + (rows,) * 12 + (P(),) * 3,
        check_vma=False,
    )
```

time: 705 us -> 515 us (0.73)
  waiting for transfers between devices: 245 us -> 103 us
  other arithmetic: 38.6 us -> 7.67 us
  local copies, waits for them, and re-layouts: 57.4 us -> 31.7 us
  starting transfers between devices: 62.8 us -> 87.5 us
    ppermute x48 -> x57, waiting for transfers between devices: 245 us -> 103 us  [exchange(): return lax.ppermute(array, AXES, pairs)]
    concatenate x8 -> x3, local copies, waits for them, and re-layouts: 27.2 us -> 1.11 us  [the longest x1 0.94 us: step(): self.held = jnp.concatenate([self.held, *got], axis=0)]
    unnamed x105 -> x211, local copies, waits for them, and re-layouts: 8.31 us -> 26.5 us
    ppermute x20 -> x42, starting transfers between devices: 4.42 us -> 19.7 us  [swap(): return lax.ppermute(array, AXES, pairs)]
    slice x17 -> x3, local copies, waits for them, and re-layouts: 12.9 us -> 0.66 us  [the longest x1 0.58 us: local(): head_grad = grad_small[-1:, :head_count]]
    sub x6 -> x0, other arithmetic: 10.5 us -> none  [adamw(): weight * (1.0 - rate * decay)]
    ppermute x48 -> x57, starting transfers between devices: 58.3 us -> 67.7 us  [exchange(): return lax.ppermute(array, AXES, pairs)]
    concatenate x24 -> x6, other arithmetic: 13.3 us -> 4.25 us  [the longest x1 3.03 us: local(): block_output = jnp.concatenate(outputs, axis=0)]
  transfers between devices with their start and end apart: 68 -> 99, of which waited for: 25 -> 15; matrix products, arithmetic and copies ran while one was open for 12% -> 3% of each run, Pallas kernels for 31% -> 51%
where the time goes in v2:
time: 515 us; the launch traced here: 505 us
  Pallas kernels  272 us (53%)
  waiting for transfers between devices  103 us (20%)
  starting transfers between devices  87.5 us (17%)
  local copies, waits for them, and re-layouts  31.7 us (6%)
  other arithmetic  7.67 us (1%)
    pallas_call x48, Pallas kernels, call(): pl.pallas_call(body, **kwargs)(*args[:prefetch], *deps, *args[prefetch:])  272 us
    ppermute x57, waiting for transfers between devices, exchange(): return lax.ppermute(array, AXES, pairs)  103 us
    ppermute x57, starting transfers between devices, exchange(): return lax.ppermute(array, AXES, pairs)  67.7 us
    unnamed x211, local copies, waits for them, and re-layouts  26.5 us
    ppermute x42, starting transfers between devices, swap(): return lax.ppermute(array, AXES, pairs)  19.7 us
  transfers between devices with their start and end apart: 99, of which 15 were waited for; matrix products, arithmetic and copies ran while one was open for 3% of the time, Pallas kernels for 51%

profile of v2, /device:TPU:0, one launch (start us, length us, event | category | flops | bytes accessed | tf_op | source)
XLA Modules:
  0.0 505.5 jit_solution(324764074140307800)
XLA Ops:
  0.7 1.9 head_parts.1
  2.5 4.0 collective-permute-start
  6.8 1.3 copy.47.refs_1_
  8.1 2.1 cut.1
  10.8 3.8 turns.1
  15.8 1.6 collective-permute-start.2
  17.8 11.6 %collective-permute-done.1.refs_2_ = bf16[1,176,512]{2,1,0:T(8,128)(2,1)S(1)} collective-permute-done((bf16[1,176,512]{2,1,0:T(8,128)(2,1)S(1)}, bf16[1,176,512]{2,1,0:T(8,128)(2,1)S(1)}, u32[]{:S(2)}, u32[]{:S(2)}) %collective-permute-start.1) | collective-permute-done | bytes 180256 | tf_op jit(solution)/shard_map/ppermute | solution.py:51
  30.8 1.5 collective-permute-start.4
  32.4 13.2 %collective-permute-done.3.refs_2_ = bf16[2,176,512]{2,1,0:T(8,128)(2,1)S(1)} collective-permute-done((bf16[2,176,512]{2,1,0:T(8,128)(2,1)S(1)}, bf16[2,176,512]{2,1,0:T(8,128)(2,1)S(1)}, u32[]{:S(2)}, u32[]{:S(2)}) %collective-permute-start.3) | collective-permute-done | bytes 360480 | tf_op jit(solution)/shard_map/ppermute | solution.py:51
  46.6 1.6 collective-permute-start.8
  48.2 1.5 collective-permute-start.12
  49.7 5.2 %collective-permute-done.6.refs_2_ = bf16[1,32,3072]{2,1,0:T(8,128)(2,1)S(1)} collective-permute-done((bf16[1,32,3072]{2,1,0:T(8,128)(2,1)S(1)}, bf16[1,32,3072]{2,1,0:T(8,128)(2,1)S(1)}, u32[]{:S(2)}, u32[]{:S(2)}) %collective-permute-start.6) | collective-permute-done | bytes 196640 | tf_op jit(solution)/shard_map/ppermute | solution.py:51
  54.9 8.6 %collective-permute-done.7.refs_14_.refs_6_.refs_15_.refs_16_ = bf16[4,176,512]{2,1,0:T(8,128)(2,1)S(1)} collective-permute-done((bf16[4,176,512]{2,1,0:T(8,128)(2,1)S(1)}, bf16[4,176,512]{2,1,0:T(8,128)(2,1)S(1)}, u32[]{:S(2)}, u32[]{:S(2)}) %collective-permute-start.7) | collective-permute-done | bytes 720928 | tf_op jit(solution)/shard_map/ppermute | solution.py:51
  64.8 1.6 collective-permute-start.14
  67.0 13.5 %collective-permute-done.9.refs_8_.refs_10_ = bf16[4,176,512]{2,1,0:T(8,128)(2,1)} collective-permute-done((bf16[4,176,512]{2,1,0:T(8,128)(2,1)S(1)}, bf16[4,176,512]{2,1,0:T(8,128)(2,1)}, u32[]{:S(2)}, u32[]{:S(2)}) %collective-permute-start.9) | collective-permute-done | bytes 720928 | tf_op jit(solution)/shard_map/ppermute | solution.py:51
  83.6 1.6 collective-permute-start.20
  86.4 23.4 %front.1 = (bf16[1024,1024]{1,0:T(8,128)(2,1)}, bf16[1024,1024]{1,0:T(8,128)(2,1)}, bf16[1024,1024]{1,0:T(8,128)(2,1)}, bf16[1024,1024]{1,0:T(8,128)(2,1)}, bf16...) custom-call(f32[8,128]{1,0:T(8,128)} %copy-done.59, ...), custom_call_target="tpu_custom_call" | custom-call | flops 6442450944 | bytes 20971520 | tf_op jit(solution)/shard_map/front/pallas_call | solution.py:133
  112.0 7.7 %collective-permute-done.22.refs_2_ = bf16[1,32,3072]{2,1,0:T(8,128)(2,1)S(1)} collective-permute-done((bf16[1,32,3072]{2,1,0:T(8,128)(2,1)S(1)}, bf16[1,32,3072]{2,1,0:T(8,128)(2,1)S(1)}, u32[]{:S(2)}, u32[]{:S(2)}) %collective-permute-start.22) | collective-permute-done | bytes 196640 | tf_op jit(solution)/shard_map/ppermute | solution.py:51
  121.5 8.7 %attend.1 = (bf16[1024,1024]{1,0:T(8,128)(2,1)}, bf16[1024,1024]{1,0:T(8,128)(2,1)}, f32[4,16,256]{2,1,0:T(8,128)}, f32[8,128]{1,0:T(8,128)}) custom-call(f32[8,128]{1,0:T(8,128)} %copy-done.67, bf16[1024,1024]{1,0:T(8,128)(2,1)} %get-tuple-element.330.refs_1_, bf16[1024,1024]{1,0:T(8,128)(2,1)} %get-tuple-element.331.refs_2_, ...), custom_call_target="tpu_custom_call" | custom-call | flops 4294967296 | bytes 8388608 | tf_op jit(solution)/shard_map/attend/pallas_call | solution.py:133
  134.0 5.4 %collective-permute-start.31 = (bf16[4,32,3072]{2,1,0:T(8,128)(2,1)S(1)}, bf16[4,32,3072]{2,1,0:T(8,128)(2,1)S(1)}, u32[]{:S(2)}, u32[]{:S(2)}) collective-permute-start(bf16[4,32,3072]{2,1,0:T(8,128)(2,1)S(1)} %collective-permute-done.23.refs_7_.refs_10_), channel_id=1, source_target_pairs={{0,16},{1,17},{2,18},{3,19},{4,20},{5,21},{6,22},{7,23},{8,24},{9,... | collective-permute-start | bytes 2359304 | tf_op jit(solution)/shard_map/ppermute | solution.py:62
  140.5 8.9 %middle.1 = (f32[1024,1024]{1,0:T(8,128)}, bf16[1024,1024]{1,0:T(8,128)(2,1)}, bf16[1024,1024]{1,0:T(8,128)(2,1)}, f32[8,128]{1,0:T(8,128)}) custom-call(f32[8,128]{1,0:T(8,128)} %copy-done.46, s32[33]{0:T(128)} %pad_add_fusion.refs_2_.refs_1_.refs_0_, bf16[1024,1024]{1,0:T(8,128)(2,1)} %get-tuple-element.345.refs_2_.refs_4_, bf16[1024,1024]{1,0:T(8,128)(2,1)} %refs_4_.4, ...), custom_call_target="tpu_custom_call" | custom-call | flops 2147483648 | bytes 12582912 | tf_op jit(solution)/shard_map/middle/pallas_call | solution.py:133
  149.5 4.0 collective-permute-start.35
  156.2 2.0 collective-permute-start.36
  158.3 18.1 %geglu_part.3 = (bf16[1024,1024]{1,0:T(8,128)(2,1)}, bf16[1024,2048]{1,0:T(8,128)(2,1)}, bf16[1024,1024]{1,0:T(8,128)(2,1)}, f32[1024,1024]{1,0:T(8,128)}, f32[8,128]{1,0:T(8,128)}) custom-call(f32[8,128]{1,0:T(8,128)} %copy-done.66, s32[33]{0:T(128)} %pad_add_fusion.refs_2_.refs_1_.refs_0_, bf16[1024,1024]{1,0:T(8,128)(2,1)} %get-tuple-element.353.refs_2_, ...), custom_call_target="tpu_custom_call" | custom-call | flops 10737418240 | bytes 31457280 | tf_op jit(solution)/shard_map/geglu_part/pallas_call | solution.py:133
  181.5 14.1 %weight_grad.4 = (bf16[4,64,1536]{2,1,0:T(8,128)(2,1)}, bf16[4,64,1536]{2,1,0:T(8,128)(2,1)}, bf16[4,64,1536]{2,1,0:T(8,128)(2,1)}, bf16[4,64,1536]{2,1,0:T(8,12...) custom-call(s32[33]{0:T(128)} %pad_add_fusion.1.refs_1_.refs_0_, ...), custom_call_target="tpu_custom_call" | custom-call | flops 6442450944 | bytes 16777216 | tf_op jit(solution)/shard_map/weight_grad/pallas_call | solution.py:133
  196.6 19.5 %geglu_part.4 = (bf16[1024,1024]{1,0:T(8,128)(2,1)}, bf16[1024,2048]{1,0:T(8,128)(2,1)}, bf16[1024,1024]{1,0:T(8,128)(2,1)}, f32[1024,1024]{1,0:T(8,128)}, f32[8,128]{1,0:T(8,128)}) custom-call(f32[8,128]{1,0:T(8,128)} %get-tuple-element.365.refs_0_, s32[33]{0:T(128)} %pad_add_fusion.1.refs_1_.refs_0_, bf16[1024,1024]{1,0:T(8,128)(2,1)} %get-tuple-element.353.refs_2_, ...), custom_call_target="tpu_custom_call" | custom-call | flops 10737418240 | bytes 31457280 | tf_op jit(solution)/shard_map/geglu_part/pallas_call | solution.py:133
  216.2 1.6 collective-permute-start.42
  219.6 13.9 %weight_grad.5 = (bf16[4,64,1536]{2,1,0:T(8,128)(2,1)}, bf16[4,64,1536]{2,1,0:T(8,128)(2,1)}, bf16[4,64,1536]{2,1,0:T(8,128)(2,1)}, bf16[4,64,1536]{2,1,0:T(8,12...) custom-call(s32[33]{0:T(128)} %pad_add_fusion.refs_2_.refs_1_.refs_0, ...), custom_call_target="tpu_custom_call" | custom-call | flops 6442450944 | bytes 16777216 | tf_op jit(solution)/shard_map/weight_grad/pallas_call | solution.py:133
  234.4 1.7 collective-permute-start.50
  237.0 9.0 %collective-permute-done.48.refs_3_ = bf16[4,64,1536]{2,1,0:T(8,128)(2,1)S(1)} collective-permute-done((bf16[4,64,1536]{2,1,0:T(8,128)(2,1)S(1)}, bf16[4,64,1536]{2,1,0:T(8,128)(2,1)S(1)}, u32[]{:S(2)}, u32[]{:S(2)}) %collective-permute-start.48) | collective-permute-done | bytes 786464 | tf_op jit(solution)/shard_map/ppermute | solution.py:51
  248.5 26.1 %geglu_part.5 = (bf16[1024,1024]{1,0:T(8,128)(2,1)}, bf16[1024,2048]{1,0:T(8,128)(2,1)}, bf16[1024,1024]{1,0:T(8,128)(2,1)}, f32[1024,1024]{1,0:T(8,128)}, bf16[...) custom-call(f32[8,128]{1,0:T(8,128)} %copy-done.65, ...), custom_call_target="tpu_custom_call" | custom-call | flops 12884901888 | bytes 31457280 | tf_op jit(solution)/shard_map/geglu_part/pallas_call | solution.py:133
  277.5 1.7 collective-permute-start.54
  280.5 17.1 %weight_grad.6 = (bf16[4,64,2048]{2,1,0:T(8,128)(2,1)}, bf16[4,64,2048]{2,1,0:T(8,128)(2,1)}, bf16[4,64,2048]{2,1,0:T(8,128)(2,1)}, bf16[4,64,2048]{2,1,0:T(8,12...) custom-call(s32[33]{0:T(128)} %pad_add_fusion.1.refs_1_.refs_0_, ...), custom_call_target="tpu_custom_call" | custom-call | flops 8589934592 | bytes 23068672 | tf_op jit(solution)/shard_map/weight_grad/pallas_call | solution.py:133
  300.4 1.8 collective-permute-start.58
  303.8 30.4 %attend_back.1 = (bf16[1024,3072]{1,0:T(8,128)(2,1)}, f32[4,1,1024]{2,1,0:T(1,128)}, f32[8,128]{1,0:T(8,128)}) custom-call(f32[8,128]{1,0:T(8,128)} %copy-done.63, bf16[1024,1024]{1,0:T(8,128)(2,1)} %get-tuple-element.330.refs_1_, bf16[1024,1024]{1,0:T(8,128)(2,1)} %get-tuple-element.331.refs_2_, bf16[1024,1024]{1,0:T(8,128)(2,1)} %get-tuple-element.332.refs_3_, ...), custom_call_target="tpu_custom_call" | custom-call | flops 10737418240 | bytes 20971520 | tf_op jit(solution)/shard_map/attend_back/pallas_call | solution.py:133
  339.3 1.4 reduce.2
  340.7 1.4 reshape.78
  343.6 14.1 %weight_grad.7 = (bf16[4,64,1536]{2,1,0:T(8,128)(2,1)}, bf16[4,64,1536]{2,1,0:T(8,128)(2,1)}, bf16[4,64,1536]{2,1,0:T(8,128)(2,1)}, bf16[4,64,1536]{2,1,0:T(8,12...) custom-call(s32[33]{0:T(128)} %pad_add_fusion.refs_2_.refs_1_.refs_0, ...), custom_call_target="tpu_custom_call" | custom-call | flops 6442450944 | bytes 14680064 | tf_op jit(solution)/shard_map/weight_grad/pallas_call | solution.py:133
  359.2 1.3 fold.18
  362.0 1.9 collective-permute-start.67
  363.8 10.8 %result.2 = (bf16[512,1024]{1,0:T(8,128)(2,1)}, f32[8,128]{1,0:T(8,128)}) custom-call(f32[8,128]{1,0:T(8,128)} %copy-done.45, s32[33]{0:T(128)} %pad_add_fusion.1.refs_1_.refs_0_, s32[33]{0:T(128)} %pad_add_fusion.refs_2_.refs_1_.refs_0_, bf16[1024,1024]{1,0:T(8,128)(2,1)} %get-tuple-element.456.refs_3_, bf16[1024,1024]{1,0:T(8,128)(2,1)} %get-tuple-element.457.refs_4_, ...), custom_call_target="tpu_custom_call" | custom-call | flops 6442450944 | bytes 20971520 | tf_op jit(solution)/shard_map/result/pallas_call | solution.py:133
  375.7 1.4 fold_pair.7
  382.8 18.0 %input_grad.1 = (bf16[1024,1024]{1,0:T(8,128)(2,1)}, f32[4,1,1024]{2,1,0:T(1,128)}, f32[8,128]{1,0:T(8,128)}) custom-call(f32[8,128]{1,0:T(8,128)} %copy-done.42, s32[33]{0:T(128)} %pad_add_fusion.1.refs_1_.refs_0_, s32[33]{0:T(128)} %pad_add_fusion.refs_2_.refs_1_.refs_0_, bf16[1024,3072]{1,0:T(8,128)(2,1)} %get-tuple-element.446.refs_3_.refs_4_.refs_5_, ...), custom_call_target="tpu_custom_call" | custom-call | flops 6442450944 | bytes 25165824 | tf_op jit(solution)/shard_map/input_grad/pallas_call | solution.py:133
  402.4 2.3 fold.20
  404.7 1.4 collective-permute-start.80
  406.1 1.8 fold.21
  410.4 1.5 collective-permute-start.78
  412.0 10.7 %result.3 = (bf16[512,1024]{1,0:T(8,128)(2,1)}, f32[8,128]{1,0:T(8,128)}) custom-call(f32[8,128]{1,0:T(8,128)} %copy-done.39, s32[33]{0:T(128)} %pad_add_fusion.1.refs_1_.refs_0_, s32[33]{0:T(128)} %pad_add_fusion.refs_2_.refs_1_.refs_0_, bf16[1024,1024]{1,0:T(8,128)(2,1)} %get-tuple-element.456.refs_3_, bf16[1024,1024]{1,0:T(8,128)(2,1)} %get-tuple-element.457.refs_4_, ...), custom_call_target="tpu_custom_call" | custom-call | flops 6442450944 | bytes 20971520 | tf_op jit(solution)/shard_map/result/pallas_call | solution.py:133
  423.3 1.8 collective-permute-start.81
  427.6 1.3 collective-permute-start.83
  429.0 2.5 collective-permute-start.84
  433.3 11.4 %collective-permute-done.81 = bf16[1,64,2048]{2,1,0:T(8,128)(2,1)} collective-permute-done((bf16[1,64,2048]{2,1,0:T(8,128)(2,1)}, bf16[1,64,2048]{2,1,0:T(8,128)(2,1)}, u32[]{:S(2)}, u32[]{:S(2)}) %collective-permute-start.81) | collective-permute-done | bytes 262176 | tf_op jit(solution)/shard_map/ppermute | solution.py:51
  445.9 2.6 collective-permute-done.83
  452.4 2.7 collective-permute-start.85
  455.1 10.0 %collective-permute-done.85.refs_2_ = bf16[2,64,1536]{2,1,0:T(8,128)(2,1)S(1)} collective-permute-done((bf16[2,64,1536]{2,1,0:T(8,128)(2,1)S(1)}, bf16[2,64,1536]{2,1,0:T(8,128)(2,1)S(1)}, u32[]{:S(2)}, u32[]{:S(2)}) %collective-permute-start.85) | collective-permute-done | bytes 393248 | tf_op jit(solution)/shard_map/ppermute | solution.py:51
  465.2 2.4 collective-permute-start.86
  469.3 4.6 collective-permute-done.86
  476.7 1.5 collective-permute-start.90
  479.0 2.1 collective-permute-done.90
  481.1 2.4 collective-permute-start.92
  483.5 2.0 collective-permute-start.93
  486.5 2.3 collective-permute-done.93
  488.9 3.0 pad_maximum_fusion
  494.8 10.3 %adamw.1 = (f32[1,128]{1,0:T(1,128)}, f32[2,48,1024]{2,1,0:T(8,128)}, f32[2,48,1024]{2,1,0:T(8,128)}, f32[2,48,1024]{2,1,0:T(8,128)}, f32[64,3072]{1,0:T(8,128)}...) custom-call(f32[8,128]{1,0:T(8,128)} %copy-done.36, ...), custom_call_target="tpu_custom_call" | custom-call | bytes 31457280 | tf_op jit(solution)/shard_map/adamw/pallas_call | solution.py:133
  (434 shorter events, 81.3 us)
Async XLA Ops:
  30.2 16.3 %collective-permute-start.5 = (bf16[4,176,512]{2,1,0:T(8,128)(2,1)S(1)}, bf16[4,176,512]{2,1,0:T(8,128)(2,1)S(1)}, u32[]{:S(2)}, u32[]{:S(2)}) collective-permute-start(bf16[4,176,512]{2,1,0:T(8,128)(2,1)S(1)} %get-tuple-element.299.refs_5_.refs_7_), channel_id=1, source_target_pairs={{0,2},{1,3},{2,0},{3,1},{4,6},{5,7},{6,4},{7,5},{8,10},{9,11},{10,... | collective-permute-start | bytes 2162696 | tf_op jit(solution)/shard_map/ppermute | solution.py:51
  30.8 17.3 %collective-permute-start.4 = (bf16[4,176,512]{2,1,0:T(8,128)(2,1)S(1)}, bf16[4,176,512]{2,1,0:T(8,128)(2,1)S(1)}, u32[]{:S(2)}, u32[]{:S(2)}) collective-permute-start(bf16[4,176,512]{2,1,0:T(8,128)(2,1)S(1)} %get-tuple-element.299.refs_5_.refs_7_), channel_id=1, source_target_pairs={{0,1},{1,0},{2,3},{3,2},{4,5},{5,4},{6,7},{7,6},{8,9},{9,8},{10,11... | collective-permute-start | bytes 2162696 | tf_op jit(solution)/shard_map/ppermute | solution.py:51
  45.9 17.6 %collective-permute-start.7 = (bf16[4,176,512]{2,1,0:T(8,128)(2,1)S(1)}, bf16[4,176,512]{2,1,0:T(8,128)(2,1)S(1)}, u32[]{:S(2)}, u32[]{:S(2)}) collective-permute-start(bf16[4,176,512]{2,1,0:T(8,128)(2,1)S(1)} %get-tuple-element.304.refs_13_.refs_5_.refs_14_.refs_15_), channel_id=1, source_target_pairs={{0,2},{1,3},{2,0},{3,1},{4,6},{5,7},{6,4},{7,5},{8,10},{9,11},{10,... | collective-permute-start | bytes 2162696 | tf_op jit(solution)/shard_map/ppermute | solution.py:51
  46.6 18.3 %collective-permute-start.10 = (bf16[4,176,512]{2,1,0:T(8,128)(2,1)S(1)}, bf16[4,176,512]{2,1,0:T(8,128)(2,1)S(1)}, u32[]{:S(2)}, u32[]{:S(2)}) collective-permute-start(bf16[4,176,512]{2,1,0:T(8,128)(2,1)S(1)} %get-tuple-element.299.refs_5_.refs_7_), channel_id=1, source_target_pairs={{0,16},{1,17},{2,18},{3,19},{4,20},{5,21},{6,22},{7,23},{8,24},{9,... | collective-permute-start | bytes 2162696 | tf_op jit(solution)/shard_map/ppermute | solution.py:62
  46.6 19.8 %collective-permute-start.8 = (bf16[4,176,512]{2,1,0:T(8,128)(2,1)S(1)}, bf16[4,176,512]{2,1,0:T(8,128)(2,1)}, u32[]{:S(2)}, u32[]{:S(2)}) collective-permute-start(bf16[4,176,512]{2,1,0:T(8,128)(2,1)S(1)} %get-tuple-element.304.refs_13_.refs_5_.refs_14_.refs_15_), channel_id=1, source_target_pairs={{0,1},{1,0},{2,3},{3,2},{4,5},{5,4},{6,7},{7,6},{8,9},{9,8},{10,11... | collective-permute-start | bytes 2162696 | tf_op jit(solution)/shard_map/ppermute | solution.py:51
  48.2 18.3 %collective-permute-start.12 = (bf16[4,176,512]{2,1,0:T(8,128)(2,1)S(1)}, bf16[4,176,512]{2,1,0:T(8,128)(2,1)S(1)}, u32[]{:S(2)}, u32[]{:S(2)}) collective-permute-start(bf16[4,176,512]{2,1,0:T(8,128)(2,1)S(1)} %collective-permute-done.5.refs_7_.refs_9_), channel_id=1, source_target_pairs={{0,16},{1,17},{2,18},{3,19},{4,20},{5,21},{6,22},{7,23},{8,24},{9,... | collective-permute-start | bytes 2162696 | tf_op jit(solution)/shard_map/ppermute | solution.py:62
  63.5 17.0 %collective-permute-start.9 = (bf16[4,176,512]{2,1,0:T(8,128)(2,1)S(1)}, bf16[4,176,512]{2,1,0:T(8,128)(2,1)}, u32[]{:S(2)}, u32[]{:S(2)}) collective-permute-start(bf16[4,176,512]{2,1,0:T(8,128)(2,1)S(1)} %collective-permute-done.4.refs_6_.refs_8_), channel_id=1, source_target_pairs={{0,2},{1,3},{2,0},{3,1},{4,6},{5,7},{6,4},{7,5},{8,10},{9,11},{10,... | collective-permute-start | bytes 2162696 | tf_op jit(solution)/shard_map/ppermute | solution.py:51
  64.8 16.7 %collective-permute-start.14 = (bf16[4,176,512]{2,1,0:T(8,128)(2,1)S(1)}, bf16[4,176,512]{2,1,0:T(8,128)(2,1)}, u32[]{:S(2)}, u32[]{:S(2)}) collective-permute-start(bf16[4,176,512]{2,1,0:T(8,128)(2,1)S(1)} %collective-permute-done.7.refs_14_.refs_6_.refs_15_.refs_16_), channel_id=1, source_target_pairs={{0,1},{1,0},{2,3},{3,2},{4,5},{5,4},{6,7},{7,6},{8,9},{9,8},{10,11... | collective-permute-start | bytes 2162696 | tf_op jit(solution)/shard_map/ppermute | solution.py:51
  66.4 16.5 %collective-permute-start.17 = (bf16[4,176,512]{2,1,0:T(8,128)(2,1)}, bf16[4,176,512]{2,1,0:T(8,128)(2,1)}, u32[]{:S(2)}, u32[]{:S(2)}) collective-permute-start(bf16[4,176,512]{2,1,0:T(8,128)(2,1)} %collective-permute-done.8.refs_15_.refs_7_.refs_16_.refs_17_), channel_id=1, source_target_pairs={{0,16},{1,17},{2,18},{3,19},{4,20},{5,21},{6,22},{7,23},{8,24},{9,... | collective-permute-start | bytes 2162696 | tf_op jit(solution)/shard_map/ppermute | solution.py:62
  66.5 17.1 %collective-permute-start.16 = (bf16[4,176,512]{2,1,0:T(8,128)(2,1)S(1)}, bf16[4,176,512]{2,1,0:T(8,128)(2,1)}, u32[]{:S(2)}, u32[]{:S(2)}) collective-permute-start(bf16[4,176,512]{2,1,0:T(8,128)(2,1)S(1)} %collective-permute-done.7.refs_14_.refs_6_.refs_15_.refs_16_), channel_id=1, source_target_pairs={{0,16},{1,17},{2,18},{3,19},{4,20},{5,21},{6,22},{7,23},{8,24},{9,... | collective-permute-start | bytes 2162696 | tf_op jit(solution)/shard_map/ppermute | solution.py:62
  83.0 26.8 %collective-permute-start.21 = (bf16[4,32,3072]{2,1,0:T(8,128)(2,1)S(1)}, bf16[4,32,3072]{2,1,0:T(8,128)(2,1)S(1)}, u32[]{:S(2)}, u32[]{:S(2)}) collective-permute-start(bf16[4,32,3072]{2,1,0:T(8,128)(2,1)S(1)} %get-tuple-element.325.refs_4_.refs_7_), channel_id=1, source_target_pairs={{0,1},{1,0},{2,3},{3,2},{4,5},{5,4},{6,7},{7,6},{8,9},{9,8},{10,11... | collective-permute-start | bytes 2359304 | tf_op jit(solution)/shard_map/ppermute | solution.py:51
  83.6 26.8 %collective-permute-start.20 = (bf16[4,32,3072]{2,1,0:T(8,128)(2,1)S(1)}, bf16[4,32,3072]{2,1,0:T(8,128)(2,1)S(1)}, u32[]{:S(2)}, u32[]{:S(2)}) collective-permute-start(bf16[4,32,3072]{2,1,0:T(8,128)(2,1)S(1)} %get-tuple-element.325.refs_4_.refs_7_), channel_id=1, source_target_pairs={{0,2},{1,3},{2,0},{3,1},{4,6},{5,7},{6,4},{7,5},{8,10},{9,11},{10,... | collective-permute-start | bytes 2359304 | tf_op jit(solution)/shard_map/ppermute | solution.py:51
  86.4 43.8 %collective-permute-start.24 = (bf16[4,32,3072]{2,1,0:T(8,128)(2,1)S(1)}, bf16[4,32,3072]{2,1,0:T(8,128)(2,1)S(1)}, u32[]{:S(2)}, u32[]{:S(2)}) collective-permute-start(bf16[4,32,3072]{2,1,0:T(8,128)(2,1)S(1)} %get-tuple-element.325.refs_4_.refs_7_), channel_id=1, source_target_pairs={{0,16},{1,17},{2,18},{3,19},{4,20},{5,21},{6,22},{7,23},{8,24},{9,... | collective-permute-start | bytes 2359304 | tf_op jit(solution)/shard_map/ppermute | solution.py:62
  109.8 20.4 %collective-permute-start.26 = (bf16[4,32,3072]{2,1,0:T(8,128)(2,1)S(1)}, bf16[4,32,3072]{2,1,0:T(8,128)(2,1)S(1)}, u32[]{:S(2)}, u32[]{:S(2)}) collective-permute-start(bf16[4,32,3072]{2,1,0:T(8,128)(2,1)S(1)} %collective-permute-done.21.refs_6_.refs_9_), channel_id=1, source_target_pairs={{0,16},{1,17},{2,18},{3,19},{4,20},{5,21},{6,22},{7,23},{8,24},{9,... | collective-permute-start | bytes 2359304 | tf_op jit(solution)/shard_map/ppermute | solution.py:62
  110.4 19.8 %collective-permute-start.25 = (bf16[4,32,3072]{2,1,0:T(8,128)(2,1)S(1)}, bf16[4,32,3072]{2,1,0:T(8,128)(2,1)S(1)}, u32[]{:S(2)}, u32[]{:S(2)}) collective-permute-start(bf16[4,32,3072]{2,1,0:T(8,128)(2,1)S(1)} %collective-permute-done.20.refs_5_.refs_8_), channel_id=1, source_target_pairs={{0,16},{1,17},{2,18},{3,19},{4,20},{5,21},{6,22},{7,23},{8,24},{9,... | collective-permute-start | bytes 2359304 | tf_op jit(solution)/shard_map/ppermute | solution.py:62
  110.5 19.8 %collective-permute-start.23 = (bf16[4,32,3072]{2,1,0:T(8,128)(2,1)S(1)}, bf16[4,32,3072]{2,1,0:T(8,128)(2,1)S(1)}, u32[]{:S(2)}, u32[]{:S(2)}) collective-permute-start(bf16[4,32,3072]{2,1,0:T(8,128)(2,1)S(1)} %collective-permute-done.20.refs_5_.refs_8_), channel_id=1, source_target_pairs={{0,1},{1,0},{2,3},{3,2},{4,5},{5,4},{6,7},{7,6},{8,9},{9,8},{10,11... | collective-permute-start | bytes 2359304 | tf_op jit(solution)/shard_map/ppermute | solution.py:51
  132.0 17.4 %collective-permute-start.29 = (bf16[4,32,3072]{2,1,0:T(8,128)(2,1)S(1)}, bf16[4,32,3072]{2,1,0:T(8,128)(2,1)S(1)}, u32[]{:S(2)}, u32[]{:S(2)}) collective-permute-start(bf16[4,32,3072]{2,1,0:T(8,128)(2,1)S(1)} %get-tuple-element.348.refs_4_.refs_15_), channel_id=1, source_target_pairs={{0,2},{1,3},{2,0},{3,1},{4,6},{5,7},{6,4},{7,5},{8,10},{9,11},{10,... | collective-permute-start | bytes 2359304 | tf_op jit(solution)/shard_map/ppermute | solution.py:51
  133.2 16.3 %collective-permute-start.28 = (bf16[4,32,3072]{2,1,0:T(8,128)(2,1)S(1)}, bf16[4,32,3072]{2,1,0:T(8,128)(2,1)S(1)}, u32[]{:S(2)}, u32[]{:S(2)}) collective-permute-start(bf16[4,32,3072]{2,1,0:T(8,128)(2,1)S(1)} %get-tuple-element.348.refs_4_.refs_15_), channel_id=1, source_target_pairs={{0,1},{1,0},{2,3},{3,2},{4,5},{5,4},{6,7},{7,6},{8,9},{9,8},{10,11... | collective-permute-start | bytes 2359304 | tf_op jit(solution)/shard_map/ppermute | solution.py:51
  134.0 22.3 %collective-permute-start.31 = (bf16[4,32,3072]{2,1,0:T(8,128)(2,1)S(1)}, bf16[4,32,3072]{2,1,0:T(8,128)(2,1)S(1)}, u32[]{:S(2)}, u32[]{:S(2)}) collective-permute-start(bf16[4,32,3072]{2,1,0:T(8,128)(2,1)S(1)} %collective-permute-done.23.refs_7_.refs_10_), channel_id=1, source_target_pairs={{0,16},{1,17},{2,18},{3,19},{4,20},{5,21},{6,22},{7,23},{8,24},{9,... | collective-permute-start | bytes 2359304 | tf_op jit(solution)/shard_map/ppermute | solution.py:62
  140.5 36.6 %collective-permute-start.33 = (bf16[4,32,3072]{2,1,0:T(8,128)(2,1)S(1)}, bf16[4,32,3072]{2,1,0:T(8,128)(2,1)}, u32[]{:S(2)}, u32[]{:S(2)}) collective-permute-start(bf16[4,32,3072]{2,1,0:T(8,128)(2,1)S(1)} %get-tuple-element.348.refs_4_.refs_15_), channel_id=1, source_target_pairs={{0,16},{1,17},{2,18},{3,19},{4,20},{5,21},{6,22},{7,23},{8,24},{9,... | collective-permute-start | bytes 2359304 | tf_op jit(solution)/shard_map/ppermute | solution.py:62
  149.5 27.6 %collective-permute-start.35 = (bf16[4,32,3072]{2,1,0:T(8,128)(2,1)S(1)}, bf16[4,32,3072]{2,1,0:T(8,128)(2,1)S(1)}, u32[]{:S(2)}, u32[]{:S(2)}) collective-permute-start(bf16[4,32,3072]{2,1,0:T(8,128)(2,1)S(1)} %collective-permute-done.29.refs_6_.refs_17_), channel_id=1, source_target_pairs={{0,16},{1,17},{2,18},{3,19},{4,20},{5,21},{6,22},{7,23},{8,24},{9,... | collective-permute-start | bytes 2359304 | tf_op jit(solution)/shard_map/ppermute | solution.py:62
  153.5 23.6 %collective-permute-start.34 = (bf16[4,32,3072]{2,1,0:T(8,128)(2,1)S(1)}, bf16[4,32,3072]{2,1,0:T(8,128)(2,1)}, u32[]{:S(2)}, u32[]{:S(2)}) collective-permute-start(bf16[4,32,3072]{2,1,0:T(8,128)(2,1)S(1)} %collective-permute-done.28.refs_5_.refs_16_), channel_id=1, source_target_pairs={{0,16},{1,17},{2,18},{3,19},{4,20},{5,21},{6,22},{7,23},{8,24},{9,... | collective-permute-start | bytes 2359304 | tf_op jit(solution)/shard_map/ppermute | solution.py:62
  153.6 22.8 %collective-permute-start.32 = (bf16[4,32,3072]{2,1,0:T(8,128)(2,1)S(1)}, bf16[4,32,3072]{2,1,0:T(8,128)(2,1)}, u32[]{:S(2)}, u32[]{:S(2)}) collective-permute-start(bf16[4,32,3072]{2,1,0:T(8,128)(2,1)S(1)} %collective-permute-done.28.refs_5_.refs_16_), channel_id=1, source_target_pairs={{0,2},{1,3},{2,0},{3,1},{4,6},{5,7},{6,4},{7,5},{8,10},{9,11},{10,... | collective-permute-start | bytes 2359304 | tf_op jit(solution)/shard_map/ppermute | solution.py:51
  156.2 20.9 %collective-permute-start.36 = (bf16[2,32,3072]{2,1,0:T(8,128)(2,1)S(1)}, bf16[2,32,3072]{2,1,0:T(8,128)(2,1)S(1)}, u32[]{:S(2)}, u32[]{:S(2)}) collective-permute-start(bf16[2,32,3072]{2,1,0:T(8,128)(2,1)S(1)} %get-tuple-element.360.refs_1_), channel_id=1, source_target_pairs={{0,4},{1,5},{2,6},{3,7},{4,0},{5,1},{6,2},{7,3},{8,12},{9,13},{10,... | collective-permute-start | bytes 1179656 | tf_op jit(solution)/shard_map/ppermute | solution.py:51
  176.4 19.3 %collective-permute-start.37 = (bf16[4,32,3072]{2,1,0:T(8,128)(2,1)}, bf16[4,32,3072]{2,1,0:T(8,128)(2,1)S(1)}, u32[]{:S(2)}, u32[]{:S(2)}) collective-permute-start(bf16[4,32,3072]{2,1,0:T(8,128)(2,1)} %collective-permute-done.32.refs_7_.refs_18_), channel_id=1, source_target_pairs={{0,16},{1,17},{2,18},{3,19},{4,20},{5,21},{6,22},{7,23},{8,24},{9,... | collective-permute-start | bytes 2359304 | tf_op jit(solution)/shard_map/ppermute | solution.py:62
  178.8 37.3 %collective-permute-start.39 = (bf16[4,32,3072]{2,1,0:T(8,128)(2,1)S(1)}, bf16[4,32,3072]{2,1,0:T(8,128)(2,1)S(1)}, u32[]{:S(2)}, u32[]{:S(2)}) collective-permute-start(bf16[4,32,3072]{2,1,0:T(8,128)(2,1)S(1)} %get-tuple-element.368.refs_4_.refs_23_), channel_id=1, source_target_pairs={{0,1},{1,0},{2,3},{3,2},{4,5},{5,4},{6,7},{7,6},{8,9},{9,8},{10,11... | collective-permute-start | bytes 2359304 | tf_op jit(solution)/shard_map/ppermute | solution.py:51
  179.9 36.3 %collective-permute-start.38 = (bf16[4,32,3072]{2,1,0:T(8,128)(2,1)S(1)}, bf16[4,32,3072]{2,1,0:T(8,128)(2,1)S(1)}, u32[]{:S(2)}, u32[]{:S(2)}) collective-permute-start(bf16[4,32,3072]{2,1,0:T(8,128)(2,1)S(1)} %get-tuple-element.368.refs_4_.refs_23_), channel_id=1, source_target_pairs={{0,2},{1,3},{2,0},{3,1},{4,6},{5,7},{6,4},{7,5},{8,10},{9,11},{10,... | collective-permute-start | bytes 2359304 | tf_op jit(solution)/shard_map/ppermute | solution.py:51
  181.0 52.6 %collective-permute-start.43 = (bf16[4,32,3072]{2,1,0:T(8,128)(2,1)S(1)}, bf16[4,32,3072]{2,1,0:T(8,128)(2,1)}, u32[]{:S(2)}, u32[]{:S(2)}) collective-permute-start(bf16[4,32,3072]{2,1,0:T(8,128)(2,1)S(1)} %get-tuple-element.368.refs_4_.refs_23_), channel_id=1, source_target_pairs={{0,16},{1,17},{2,18},{3,19},{4,20},{5,21},{6,22},{7,23},{8,24},{9,... | collective-permute-start | bytes 2359304 | tf_op jit(solution)/shard_map/ppermute | solution.py:62
  195.6 22.2 %collective-permute-start.40 = (bf16[4,64,1536]{2,1,0:T(8,128)(2,1)}, bf16[4,64,1536]{2,1,0:T(8,128)(2,1)S(1)}, u32[]{:S(2)}, u32[]{:S(2)}) collective-permute-start(bf16[4,64,1536]{2,1,0:T(8,128)(2,1)} %get-tuple-element.374), channel_id=1, source_target_pairs={{0,16},{1,17},{2,18},{3,19},{4,20},{5,21},{6,22},{7,23},{8,24},{9,... | collective-permute-start | bytes 2359304 | tf_op jit(solution)/shard_map/ppermute | solution.py:62
  195.7 22.1 %collective-permute-start.41 = (bf16[4,64,1536]{2,1,0:T(8,128)(2,1)}, bf16[4,64,1536]{2,1,0:T(8,128)(2,1)S(1)}, u32[]{:S(2)}, u32[]{:S(2)}) collective-permute-start(bf16[4,64,1536]{2,1,0:T(8,128)(2,1)} %get-tuple-element.375), channel_id=1, source_target_pairs={{0,16},{1,17},{2,18},{3,19},{4,20},{5,21},{6,22},{7,23},{8,24},{9,... | collective-permute-start | bytes 2359304 | tf_op jit(solution)/shard_map/ppermute | solution.py:62
  216.2 17.8 %collective-permute-start.42 = (bf16[4,32,3072]{2,1,0:T(8,128)(2,1)S(1)}, bf16[4,32,3072]{2,1,0:T(8,128)(2,1)}, u32[]{:S(2)}, u32[]{:S(2)}) collective-permute-start(bf16[4,32,3072]{2,1,0:T(8,128)(2,1)S(1)} %collective-permute-done.38.refs_5_.refs_24_), channel_id=1, source_target_pairs={{0,1},{1,0},{2,3},{3,2},{4,5},{5,4},{6,7},{7,6},{8,9},{9,8},{10,11... | collective-permute-start | bytes 2359304 | tf_op jit(solution)/shard_map/ppermute | solution.py:51
  218.9 15.5 %collective-permute-start.46 = (bf16[4,64,1536]{2,1,0:T(8,128)(2,1)}, bf16[4,64,1536]{2,1,0:T(8,128)(2,1)S(1)}, u32[]{:S(2)}, u32[]{:S(2)}) collective-permute-start(bf16[4,64,1536]{2,1,0:T(8,128)(2,1)} %get-tuple-element.380), channel_id=1, source_target_pairs={{0,16},{1,17},{2,18},{3,19},{4,20},{5,21},{6,22},{7,23},{8,24},{9,... | collective-permute-start | bytes 2359304 | tf_op jit(solution)/shard_map/ppermute | solution.py:62
  219.0 15.4 %collective-permute-start.45 = (bf16[4,32,3072]{2,1,0:T(8,128)(2,1)S(1)}, bf16[4,32,3072]{2,1,0:T(8,128)(2,1)S(1)}, u32[]{:S(2)}, u32[]{:S(2)}) collective-permute-start(bf16[4,32,3072]{2,1,0:T(8,128)(2,1)S(1)} %collective-permute-done.39.refs_6_.refs_25_), channel_id=1, source_target_pairs={{0,16},{1,17},{2,18},{3,19},{4,20},{5,21},{6,22},{7,23},{8,24},{9,... | collective-permute-start | bytes 2359304 | tf_op jit(solution)/shard_map/ppermute | solution.py:62
  219.5 16.7 %collective-permute-start.44 = (bf16[4,32,3072]{2,1,0:T(8,128)(2,1)S(1)}, bf16[4,32,3072]{2,1,0:T(8,128)(2,1)S(1)}, u32[]{:S(2)}, u32[]{:S(2)}) collective-permute-start(bf16[4,32,3072]{2,1,0:T(8,128)(2,1)S(1)} %collective-permute-done.38.refs_5_.refs_24_), channel_id=1, source_target_pairs={{0,16},{1,17},{2,18},{3,19},{4,20},{5,21},{6,22},{7,23},{8,24},{9,... | collective-permute-start | bytes 2359304 | tf_op jit(solution)/shard_map/ppermute | solution.py:62
  234.4 40.2 %collective-permute-start.50 = (bf16[4,64,1536]{2,1,0:T(8,128)(2,1)S(1)}, bf16[4,64,1536]{2,1,0:T(8,128)(2,1)S(1)}, u32[]{:S(2)}, u32[]{:S(2)}) collective-permute-start(bf16[4,64,1536]{2,1,0:T(8,128)(2,1)S(1)} %get-tuple-element.398), channel_id=1, source_target_pairs={{0,2},{1,3},{2,0},{3,1},{4,6},{5,7},{6,4},{7,5},{8,10},{9,11},{10,... | collective-permute-start | bytes 2359304 | tf_op jit(solution)/shard_map/ppermute | solution.py:51
  236.2 40.4 %collective-permute-start.52 = (bf16[4,64,1536]{2,1,0:T(8,128)(2,1)}, bf16[4,64,1536]{2,1,0:T(8,128)(2,1)S(1)}, u32[]{:S(2)}, u32[]{:S(2)}) collective-permute-start(bf16[4,64,1536]{2,1,0:T(8,128)(2,1)} %get-tuple-element.403), channel_id=1, source_target_pairs={{0,16},{1,17},{2,18},{3,19},{4,20},{5,21},{6,22},{7,23},{8,24},{9,... | collective-permute-start | bytes 2359304 | tf_op jit(solution)/shard_map/ppermute | solution.py:62
  237.0 39.5 %collective-permute-start.53 = (bf16[4,64,1536]{2,1,0:T(8,128)(2,1)}, bf16[4,64,1536]{2,1,0:T(8,128)(2,1)S(1)}, u32[]{:S(2)}, u32[]{:S(2)}) collective-permute-start(bf16[4,64,1536]{2,1,0:T(8,128)(2,1)} %get-tuple-element.404), channel_id=1, source_target_pairs={{0,16},{1,17},{2,18},{3,19},{4,20},{5,21},{6,22},{7,23},{8,24},{9,... | collective-permute-start | bytes 2359304 | tf_op jit(solution)/shard_map/ppermute | solution.py:62
  247.0 27.6 %collective-permute-start.51 = (bf16[4,64,1536]{2,1,0:T(8,128)(2,1)S(1)}, bf16[4,64,1536]{2,1,0:T(8,128)(2,1)S(1)}, u32[]{:S(2)}, u32[]{:S(2)}) collective-permute-start(bf16[4,64,1536]{2,1,0:T(8,128)(2,1)S(1)} %get-tuple-element.399), channel_id=1, source_target_pairs={{0,1},{1,0},{2,3},{3,2},{4,5},{5,4},{6,7},{7,6},{8,9},{9,8},{10,11... | collective-permute-start | bytes 2359304 | tf_op jit(solution)/shard_map/ppermute | solution.py:51
  276.9 22.8 %collective-permute-start.55 = (bf16[4,64,1536]{2,1,0:T(8,128)(2,1)}, bf16[4,64,1536]{2,1,0:T(8,128)(2,1)S(1)}, u32[]{:S(2)}, u32[]{:S(2)}) collective-permute-start(bf16[4,64,1536]{2,1,0:T(8,128)(2,1)} %get-tuple-element.409), channel_id=1, source_target_pairs={{0,16},{1,17},{2,18},{3,19},{4,20},{5,21},{6,22},{7,23},{8,24},{9,... | collective-permute-start | bytes 2359304 | tf_op jit(solution)/shard_map/ppermute | solution.py:62
  277.0 23.4 %collective-permute-start.56 = (bf16[4,64,1536]{2,1,0:T(8,128)(2,1)}, bf16[4,64,1536]{2,1,0:T(8,128)(2,1)S(1)}, u32[]{:S(2)}, u32[]{:S(2)}) collective-permute-start(bf16[4,64,1536]{2,1,0:T(8,128)(2,1)} %get-tuple-element.407), channel_id=1, source_target_pairs={{0,16},{1,17},{2,18},{3,19},{4,20},{5,21},{6,22},{7,23},{8,24},{9,... | collective-permute-start | bytes 2359304 | tf_op jit(solution)/shard_map/ppermute | solution.py:62
  277.5 20.3 %collective-permute-start.54 = (bf16[2,64,1536]{2,1,0:T(8,128)(2,1)}, bf16[2,64,1536]{2,1,0:T(8,128)(2,1)S(1)}, u32[]{:S(2)}, u32[]{:S(2)}) collective-permute-start(bf16[2,64,1536]{2,1,0:T(8,128)(2,1)} %get-tuple-element.417), channel_id=1, source_target_pairs={{0,4},{1,5},{2,6},{3,7},{4,0},{5,1},{6,2},{7,3},{8,12},{9,13},{10,... | collective-permute-start | bytes 1179656 | tf_op jit(solution)/shard_map/ppermute | solution.py:51
  279.2 23.0 %collective-permute-start.57 = (bf16[4,64,1536]{2,1,0:T(8,128)(2,1)S(1)}, bf16[4,64,1536]{2,1,0:T(8,128)(2,1)S(1)}, u32[]{:S(2)}, u32[]{:S(2)}) collective-permute-start(bf16[4,64,1536]{2,1,0:T(8,128)(2,1)S(1)} %get-tuple-element.422), channel_id=1, source_target_pairs={{0,1},{1,0},{2,3},{3,2},{4,5},{5,4},{6,7},{7,6},{8,9},{9,8},{10,11... | collective-permute-start | bytes 2359304 | tf_op jit(solution)/shard_map/ppermute | solution.py:51
  297.7 38.0 %collective-permute-start.61 = (bf16[4,64,2048]{2,1,0:T(8,128)(2,1)}, bf16[4,64,2048]{2,1,0:T(8,128)(2,1)S(1)}, u32[]{:S(2)}, u32[]{:S(2)}) collective-permute-start(bf16[4,64,2048]{2,1,0:T(8,128)(2,1)} %get-tuple-element.437), channel_id=1, source_target_pairs={{0,16},{1,17},{2,18},{3,19},{4,20},{5,21},{6,22},{7,23},{8,24},{9,... | collective-permute-start | bytes 3145736 | tf_op jit(solution)/shard_map/ppermute | solution.py:62
  297.8 37.9 %collective-permute-start.62 = (bf16[4,64,2048]{2,1,0:T(8,128)(2,1)}, bf16[4,64,2048]{2,1,0:T(8,128)(2,1)S(1)}, u32[]{:S(2)}, u32[]{:S(2)}) collective-permute-start(bf16[4,64,2048]{2,1,0:T(8,128)(2,1)} %get-tuple-element.438), channel_id=1, source_target_pairs={{0,16},{1,17},{2,18},{3,19},{4,20},{5,21},{6,22},{7,23},{8,24},{9,... | collective-permute-start | bytes 3145736 | tf_op jit(solution)/shard_map/ppermute | solution.py:62
  299.7 35.6 %collective-permute-start.59 = (bf16[4,64,1536]{2,1,0:T(8,128)(2,1)S(1)}, bf16[4,64,1536]{2,1,0:T(8,128)(2,1)S(1)}, u32[]{:S(2)}, u32[]{:S(2)}) collective-permute-start(bf16[4,64,1536]{2,1,0:T(8,128)(2,1)S(1)} %get-tuple-element.432), channel_id=1, source_target_pairs={{0,1},{1,0},{2,3},{3,2},{4,5},{5,4},{6,7},{7,6},{8,9},{9,8},{10,11... | collective-permute-start | bytes 2359304 | tf_op jit(solution)/shard_map/ppermute | solution.py:51
  300.4 33.8 %collective-permute-start.58 = (bf16[1,64,1536]{2,1,0:T(8,128)(2,1)}, bf16[1,64,1536]{2,1,0:T(8,128)(2,1)S(1)}, u32[]{:S(2)}, u32[]{:S(2)}) collective-permute-start(bf16[1,64,1536]{2,1,0:T(8,128)(2,1)} %get-tuple-element.429), channel_id=1, source_target_pairs={{0,8},{1,9},{2,10},{3,11},{4,12},{5,13},{6,14},{7,15},{8,0},{9,1},... | collective-permute-start | bytes 589832 | tf_op jit(solution)/shard_map/ppermute | solution.py:51
  302.5 32.7 %collective-permute-start.60 = (bf16[4,64,1536]{2,1,0:T(8,128)(2,1)S(1)}, bf16[4,64,1536]{2,1,0:T(8,128)(2,1)S(1)}, u32[]{:S(2)}, u32[]{:S(2)}) collective-permute-start(bf16[4,64,1536]{2,1,0:T(8,128)(2,1)S(1)} %get-tuple-element.433), channel_id=1, source_target_pairs={{0,2},{1,3},{2,0},{3,1},{4,6},{5,7},{6,4},{7,5},{8,10},{9,11},{10,... | collective-permute-start | bytes 2359304 | tf_op jit(solution)/shard_map/ppermute | solution.py:51
  336.9 22.2 %collective-permute-start.64 = (bf16[4,64,2048]{2,1,0:T(8,128)(2,1)}, bf16[4,64,2048]{2,1,0:T(8,128)(2,1)S(1)}, u32[]{:S(2)}, u32[]{:S(2)}) collective-permute-start(bf16[4,64,2048]{2,1,0:T(8,128)(2,1)} %get-tuple-element.443), channel_id=1, source_target_pairs={{0,16},{1,17},{2,18},{3,19},{4,20},{5,21},{6,22},{7,23},{8,24},{9,... | collective-permute-start | bytes 3145736 | tf_op jit(solution)/shard_map/ppermute | solution.py:62
  337.0 22.1 %collective-permute-start.65 = (bf16[4,64,2048]{2,1,0:T(8,128)(2,1)}, bf16[4,64,2048]{2,1,0:T(8,128)(2,1)S(1)}, u32[]{:S(2)}, u32[]{:S(2)}) collective-permute-start(bf16[4,64,2048]{2,1,0:T(8,128)(2,1)} %get-tuple-element.441), channel_id=1, source_target_pairs={{0,16},{1,17},{2,18},{3,19},{4,20},{5,21},{6,22},{7,23},{8,24},{9,... | collective-permute-start | bytes 3145736 | tf_op jit(solution)/shard_map/ppermute | solution.py:62
  337.9 21.3 %collective-permute-start.66 = (bf16[4,64,2048]{2,1,0:T(8,128)(2,1)}, bf16[4,64,2048]{2,1,0:T(8,128)(2,1)S(1)}, u32[]{:S(2)}, u32[]{:S(2)}) collective-permute-start(bf16[4,64,2048]{2,1,0:T(8,128)(2,1)} %get-tuple-element.454), channel_id=1, source_target_pairs={{0,2},{1,3},{2,0},{3,1},{4,6},{5,7},{6,4},{7,5},{8,10},{9,11},{10,... | collective-permute-start | bytes 3145736 | tf_op jit(solution)/shard_map/ppermute | solution.py:51
  342.1 15.6 %collective-permute-start.63 = (bf16[2,64,1536]{2,1,0:T(8,128)(2,1)}, bf16[2,64,1536]{2,1,0:T(8,128)(2,1)S(1)}, u32[]{:S(2)}, u32[]{:S(2)}) collective-permute-start(bf16[2,64,1536]{2,1,0:T(8,128)(2,1)} %copy-done.56), channel_id=1, source_target_pairs={{0,4},{1,5},{2,6},{3,7},{4,0},{5,1},{6,2},{7,3},{8,12},{9,13},{10,... | collective-permute-start | bytes 1179656 | tf_op jit(solution)/shard_map/ppermute | solution.py:51
  342.4 36.5 %collective-permute-start.70 = (bf16[4,64,2048]{2,1,0:T(8,128)(2,1)}, bf16[4,64,2048]{2,1,0:T(8,128)(2,1)S(1)}, u32[]{:S(2)}, u32[]{:S(2)}) collective-permute-start(bf16[4,64,2048]{2,1,0:T(8,128)(2,1)} %copy-done.55), channel_id=1, source_target_pairs={{0,2},{1,3},{2,0},{3,1},{4,6},{5,7},{6,4},{7,5},{8,10},{9,11},{10,... | collective-permute-start | bytes 3145736 | tf_op jit(solution)/shard_map/ppermute | solution.py:51
  360.5 19.1 %collective-permute-start.71 = (bf16[4,64,2048]{2,1,0:T(8,128)(2,1)}, bf16[4,64,2048]{2,1,0:T(8,128)(2,1)S(1)}, u32[]{:S(2)}, u32[]{:S(2)}) collective-permute-start(bf16[4,64,2048]{2,1,0:T(8,128)(2,1)} %get-tuple-element.476), channel_id=1, source_target_pairs={{0,1},{1,0},{2,3},{3,2},{4,5},{5,4},{6,7},{7,6},{8,9},{9,8},{10,11... | collective-permute-start | bytes 3145736 | tf_op jit(solution)/shard_map/ppermute | solution.py:51
  377.1 24.5 %collective-permute-start.72 = (bf16[4,64,1536]{2,1,0:T(8,128)(2,1)}, bf16[4,64,1536]{2,1,0:T(8,128)(2,1)S(1)}, u32[]{:S(2)}, u32[]{:S(2)}) collective-permute-start(bf16[4,64,1536]{2,1,0:T(8,128)(2,1)} %get-tuple-element.472), channel_id=1, source_target_pairs={{0,16},{1,17},{2,18},{3,19},{4,20},{5,21},{6,22},{7,23},{8,24},{9,... | collective-permute-start | bytes 2359304 | tf_op jit(solution)/shard_map/ppermute | solution.py:62
  377.1 24.5 %collective-permute-start.73 = (bf16[4,64,1536]{2,1,0:T(8,128)(2,1)}, bf16[4,64,1536]{2,1,0:T(8,128)(2,1)S(1)}, u32[]{:S(2)}, u32[]{:S(2)}) collective-permute-start(bf16[4,64,1536]{2,1,0:T(8,128)(2,1)} %get-tuple-element.470), channel_id=1, source_target_pairs={{0,16},{1,17},{2,18},{3,19},{4,20},{5,21},{6,22},{7,23},{8,24},{9,... | collective-permute-start | bytes 2359304 | tf_op jit(solution)/shard_map/ppermute | solution.py:62
  377.6 24.0 %collective-permute-start.74 = (bf16[4,64,1536]{2,1,0:T(8,128)(2,1)}, bf16[4,64,1536]{2,1,0:T(8,128)(2,1)}, u32[]{:S(2)}, u32[]{:S(2)}) collective-permute-start(bf16[4,64,1536]{2,1,0:T(8,128)(2,1)} %get-tuple-element.484), channel_id=1, source_target_pairs={{0,1},{1,0},{2,3},{3,2},{4,5},{5,4},{6,7},{7,6},{8,9},{9,8},{10,11... | collective-permute-start | bytes 2359304 | tf_op jit(solution)/shard_map/ppermute | solution.py:51
  378.9 50.0 %collective-permute-start.79 = (bf16[4,64,1536]{2,1,0:T(8,128)(2,1)}, bf16[4,64,1536]{2,1,0:T(8,128)(2,1)S(1)}, u32[]{:S(2)}, u32[]{:S(2)}) collective-permute-start(bf16[4,64,1536]{2,1,0:T(8,128)(2,1)} %get-tuple-element.502), channel_id=1, source_target_pairs={{0,1},{1,0},{2,3},{3,2},{4,5},{5,4},{6,7},{7,6},{8,9},{9,8},{10,11... | collective-permute-start | bytes 2359304 | tf_op jit(solution)/shard_map/ppermute | solution.py:51
  381.7 24.4 %collective-permute-start.75 = (bf16[2,64,2048]{2,1,0:T(8,128)(2,1)}, bf16[2,64,2048]{2,1,0:T(8,128)(2,1)}, u32[]{:S(2)}, u32[]{:S(2)}) collective-permute-start(bf16[2,64,2048]{2,1,0:T(8,128)(2,1)} %get-tuple-element.487), channel_id=1, source_target_pairs={{0,4},{1,5},{2,6},{3,7},{4,0},{5,1},{6,2},{7,3},{8,12},{9,13},{10,... | collective-permute-start | bytes 1572872 | tf_op jit(solution)/shard_map/ppermute | solution.py:51
  404.7 26.8 %collective-permute-start.80 = (bf16[4,64,1536]{2,1,0:T(8,128)(2,1)}, bf16[4,64,1536]{2,1,0:T(8,128)(2,1)S(1)}, u32[]{:S(2)}, u32[]{:S(2)}) collective-permute-start(bf16[4,64,1536]{2,1,0:T(8,128)(2,1)} %get-tuple-element.503), channel_id=1, source_target_pairs={{0,2},{1,3},{2,0},{3,1},{4,6},{5,7},{6,4},{7,5},{8,10},{9,11},{10,... | collective-permute-start | bytes 2359304 | tf_op jit(solution)/shard_map/ppermute | solution.py:51
  409.2 15.9 %collective-permute-start.77 = (f32[1,96,128]{2,1,0:T(8,128)S(1)}, f32[1,96,128]{2,1,0:T(8,128)S(1)}, u32[]{:S(2)}, u32[]{:S(2)}) collective-permute-start(f32[1,96,128]{2,1,0:T(8,128)S(1)} %pad_maximum_fusion.2), channel_id=1, source_target_pairs={{0,2},{1,3},{2,0},{3,1},{4,6},{5,7},{6,4},{7,5},{8,10},{9,11},{10,... | collective-permute-start | bytes 147464 | tf_op jit(solution)/shard_map/ppermute | solution.py:51
  423.3 21.3 %collective-permute-start.81 = (bf16[1,64,2048]{2,1,0:T(8,128)(2,1)}, bf16[1,64,2048]{2,1,0:T(8,128)(2,1)}, u32[]{:S(2)}, u32[]{:S(2)}) collective-permute-start(bf16[1,64,2048]{2,1,0:T(8,128)(2,1)} %get-tuple-element.506), channel_id=1, source_target_pairs={{0,8},{1,9},{2,10},{3,11},{4,12},{5,13},{6,14},{7,15},{8,0},{9,1},... | collective-permute-start | bytes 786440 | tf_op jit(solution)/shard_map/ppermute | solution.py:51
  427.0 18.8 %collective-permute-start.82 = (f32[4,96,128]{2,1,0:T(8,128)}, f32[4,96,128]{2,1,0:T(8,128)}, u32[]{:S(2)}, u32[]{:S(2)}) collective-permute-start(f32[4,96,128]{2,1,0:T(8,128)} %get-tuple-element.546), channel_id=1, source_target_pairs={{0,4},{1,5},{2,6},{3,7},{4,0},{5,1},{6,2},{7,3},{8,12},{9,13},{10,... | collective-permute-start | bytes 589832 | tf_op jit(solution)/shard_map/ppermute | solution.py:51
  427.6 20.8 %collective-permute-start.83 = (f32[4,96,128]{2,1,0:T(8,128)}, f32[4,96,128]{2,1,0:T(8,128)}, u32[]{:S(2)}, u32[]{:S(2)}) collective-permute-start(f32[4,96,128]{2,1,0:T(8,128)} %get-tuple-element.546), channel_id=1, source_target_pairs={{0,8},{1,9},{2,10},{3,11},{4,12},{5,13},{6,14},{7,15},{8,0},{9,1},... | collective-permute-start | bytes 589832 | tf_op jit(solution)/shard_map/ppermute | solution.py:51
  429.0 19.5 %collective-permute-start.84 = (f32[4,96,128]{2,1,0:T(8,128)}, f32[4,96,128]{2,1,0:T(8,128)}, u32[]{:S(2)}, u32[]{:S(2)}) collective-permute-start(f32[4,96,128]{2,1,0:T(8,128)} %get-tuple-element.546), channel_id=1, source_target_pairs={{0,12},{1,13},{2,14},{3,15},{4,8},{5,9},{6,10},{7,11},{8,4},{9,5},... | collective-permute-start | bytes 589832 | tf_op jit(solution)/shard_map/ppermute | solution.py:51
  (136 other events, 1547.2 us)
